TPU v7x, 32 devices: a whole 2x2x4 slice. The times are simulated.
32 devices in a mesh: tensor: 8 (over y, x, core), dp: 4 (over z).
Axes of the slice: x: 2, y: 2, z: 4, core: 2. Of those that a mesh axis runs over, the one named last changes fastest.
Arguments:
- cotangent: bfloat16 [1024, 8192], P('dp', 'tensor'), may hold values from -12 to 12
- down_weight: bfloat16 [28672, 8192], P('tensor', 'dp'), may hold values from -0.0625 to 0.0625
- gate_pre: bfloat16 [1024, 28672], P('dp', 'tensor'), may hold values from -6 to 6
- up_pre: bfloat16 [1024, 28672], P('dp', 'tensor'), may hold values from -6 to 6
Outputs:
- factor: bfloat16 [8, 2, 5, 4, 3211264], P('tensor', None, None, 'dp')
All inputs are finite; a program needn't handle non-finite values.
Results may differ from a plain program's by a relative error of at most 0.0057.
Values may be sent and summed in bfloat16 or wider, within the bound.
No kernel may reach another device: no remote copies, remote signals or barrier semaphores. Data moves between devices by JAX's collectives and lax.ppermute only.
A program may use at most 256 MiB of HBM per device.

v0:
```python
import jax
import jax.numpy as jnp
from jax import lax
from jax.sharding import PartitionSpec as P


def per_device(cotangent, down_weight, gate_pre, up_pre):
    block_count = lax.axis_size("tensor")
    groups = lax.axis_size("dp")
    own_block = lax.axis_index("tensor")
    group_index = lax.axis_index("dp")
    local_tokens = gate_pre.shape[0]
    block_width = gate_pre.shape[1]
    slice_width = block_width // groups
    all_tokens = local_tokens * groups
    band_width = block_count // 2 + 1
    contract = (((1,), (1,)), ((), ()))
    features = lax.all_gather(cotangent, "tensor", axis=1, tiled=True)
    regrouped = lax.all_to_all(features, "dp", split_axis=1, concat_axis=0, tiled=True)
    hidden_cot = lax.psum_scatter(
        lax.dot_general(regrouped, down_weight, contract, preferred_element_type=jnp.float32),
        "dp",
        scatter_dimension=0,
        tiled=True,
    )
    gate_value = gate_pre.astype(jnp.float32)
    up_value = up_pre.astype(jnp.float32)
    sigmoid_gate = jax.nn.sigmoid(gate_value)
    grad_gate = (
        hidden_cot * up_value * sigmoid_gate * (1.0 + gate_value * (1.0 - sigmoid_gate))
    ).astype(jnp.bfloat16)
    grad_up = (hidden_cot * gate_value * sigmoid_gate).astype(jnp.bfloat16)
    stacked = jnp.stack([grad_gate, grad_up])
    own_rows = lax.all_gather(stacked, "dp", axis=1, tiled=True)
    own_slice = lax.dynamic_slice_in_dim(own_rows, group_index * slice_width, slice_width, 2)
    inverse_count = 1.0 / all_tokens

    def factor_tile(partner):
        product = jnp.einsum("ftr,ftc->frc", own_rows, partner, preferred_element_type=jnp.float32)
        return (product * inverse_count).astype(jnp.bfloat16)

    def place(result, offset, partner):
        return lax.dynamic_update_slice(
            result,
            factor_tile(partner)[:, None],
            (jnp.int32(0), offset, jnp.int32(0), jnp.int32(0)),
        )

    holder = jnp.zeros((2, band_width, block_width, slice_width), jnp.bfloat16)
    block_piece = lax.all_gather(own_slice[None], "tensor", axis=0, tiled=True)

    def place_block(position, current):
        offset = (own_block - position) % block_count
        partner = lax.dynamic_index_in_dim(block_piece, position, 0, keepdims=False)
        return lax.cond(
            offset < band_width,
            lambda kept: place(kept, offset, partner),
            lambda kept: kept,
            current,
        )

    factor = lax.fori_loop(0, block_piece.shape[0], place_block, holder)
    flat = factor.reshape(2, band_width, block_width * slice_width)
    return flat[None, :, :, None, :]


def solution(mesh):
    placed = (P("dp", "tensor"), P("tensor", "dp"), P("dp", "tensor"), P("dp", "tensor"))
    return jax.shard_map(
        per_device,
        mesh=mesh,
        in_specs=placed,
        out_specs=P("tensor", None, None, "dp", None),
        check_vma=False,
    )
```

profile of v0, /device:TPU:29, one launch (start us, length us, event | category | flops | bytes accessed | tf_op | source)
XLA Modules:
  0.0 1157.2 jit_solution(17738322638646693579)
XLA Ops:
  6.5 2.0 copy.13
  8.6 0.0 reduce-scatter.2.cloned.1.call-start
  8.7 38.5 %all-gather.5.cloned.1.call-done = bf16[256,8192]{0,1:T(8,128)(2,1)} async-done(((bf16[256,1024]{0,1:T(8,128)(2,1)}), bf16[256,8192]{0,1:T(8,128)(2,1)}) %all-gather.5.cloned.1.call-update) | async-done | bytes 4194320 | tf_op jit(solution)/shard_map/all_gather | solution.py:18
  47.2 96.9 %all_to_all.19 = bf16[256,4,2048]{0,2,1:T(8,128)(2,1)} all-to-all(bf16[256,4,2048]{0,2,1:T(8,128)(2,1)} %bitcast.24), channel_id=1, replica_groups=mesh['tensor'=8,'dp'=4] {'dp'}, dimensions={1} | all-to-all | bytes 8388608 | tf_op jit(solution)/shard_map/all_to_all | solution.py:19
  144.0 6.3 copy.14
  150.3 22.9 %fusion.13 = f32[1024,3584]{1,0:T(8,128)} fusion(bf16[1024,2048]{1,0:T(8,128)(2,1)} %bitcast.25, bf16[3584,2048]{1,0:T(8,128)(2,1)} %param.9), kind=kOutput, calls=%fused_computation.20 | convolution fusion | flops 15032385536 | bytes 33554432 | tf_op jit(solution)/shard_map/dot_general | solution.py:21
  173.2 0.0 reduce-scatter.2.cloned.1.call-update
  173.2 0.0 all-gather.7.cloned.1.call-start
  173.3 246.4 %reduce-scatter.2.cloned.1.call-done = f32[256,3584]{1,0:T(8,128)} async-done(((f32[1024,3584]{1,0:T(8,128)}), f32[256,3584]{1,0:T(8,128)}) %reduce-scatter.2.cloned.1.call-update) | async-done | bytes 3670032 | tf_op jit(solution)/shard_map/reduce_scatter | solution.py:20
  419.7 3.6 fusion.12
  423.3 2.2 pad_maximum_fusion
  425.4 0.0 all-gather.7.cloned.1.call-update
  425.4 0.2 all-gather.9.cloned.1.call-start
  425.7 250.8 %all-gather.7.cloned.1.call-done = bf16[2,1024,3584]{2,1,0:T(8,128)(2,1)} async-done(((bf16[2,256,3584]{2,1,0:T(8,128)(2,1)}), bf16[2,1024,3584]{2,1,0:T(8,128)(2,1)}) %all-gather.7.cloned.1.call-update) | async-done | bytes 14680080 | tf_op jit(solution)/shard_map/all_gather | solution.py:34
  676.5 4.2 constant_dynamic-slice_fusion
  680.6 0.0 all-gather.9.cloned.1.call-update
  680.6 143.5 %all-gather.9.cloned.1.call-done = bf16[16,1024,896]{2,1,0:T(8,128)(2,1)} async-done(((bf16[2,1024,896]{2,1,0:T(8,128)(2,1)}), bf16[16,1024,896]{2,1,0:T(8,128)(2,1)}) %all-gather.9.cloned.1.call-update) | async-done | bytes 29360144 | tf_op jit(solution)/shard_map/all_gather | solution.py:50
  824.2 40.8 %copy.15 = bf16[8,2,1024,896]{2,3,1,0:T(8,128)(2,1)} copy(bf16[8,2,1024,896]{3,2,1,0:T(8,128)(2,1)} %bitcast.22) | data formatting | bytes 58720256 | tf_op jit(solution)/shard_map/while | solution.py:62
  865.0 20.3 %broadcast_in_dim.10 = bf16[2,5,3584,896]{2,3,0,1:T(8,128)(2,1)} broadcast(bf16[]{:T(256)} %constant.82.clone.1), dimensions={} | broadcast | bytes 64225280 | tf_op jit(solution)/shard_map/broadcast_in_dim | solution.py:49
  885.3 110.7 %while.18 = (s32[]{:T(128)}, bf16[2,5,3584,896]{2,3,0,1:T(8,128)(2,1)}, s32[]{:T(128)}, bf16[8,2,1024,896]{2,3,1,0:T(8,128)(2,1)}, bf16[2,1024,3584]{2,1,0:T(8,1...) while((s32[]{:T(128)}, bf16[2,5,3584,896]{2,3,0,1:T(8,128)(2,1)}, s32[]{:T(128)}, ...), condition=%wide.region_4.5_spmd, body=%wide.region_1.4_spmd.sunk | while | flops 13166182400 | bytes 31195496 | solution.py:62
  885.3 22.1 %conditional.2 = (bf16[2,5,3584,896]{2,3,0,1:T(8,128)(2,1)}) conditional(s32[]{:T(128)} %convert_element_type.73, bf16[2,5,3584,896]{2,3,0,1:T(8,128)(2,1)} %get-tuple-element.266, (s32[]{:T(128)}, bf16[8,2,1024,896]{2,3,1,0:T(8,128)(2,1)}, bf16[2,1024,3584]{2,1,0:T(8,128)(2,1)}, s32[]{:T(128)}, bf16[2,5,3584,896]{2,3,0,1:T(8,128)(2,1)}) %tuple.60), branch_computations={%region_2.2_spmd, %region_3.3_spmd} | conditional | flops 13166182400 | bytes 31195220 | solution.py:55
  885.3 22.1 %bitcast_dynamic-update-slice_fusion = bf16[2,5,3584,896]{2,3,0,1:T(8,128)(2,1)} fusion(bf16[2,5,3584,896]{2,3,0,1:T(8,128)(2,1)} %get-tuple-element.179, s32[]{:T(128)S(6)} %select_n.35, bf16[2,1024,3584]{2,1,0:T(8,128)(2,1)} %get-tuple-element.182, bf16[8,2,1024,896]{2,3,1,0:T(8,128)(2,1)} %get-tuple-element.180, s32[]{:T(128)S(6)} %select_n.34), kind=kOutput, calls=%fused_computation.1 | convolution fusion | flops 13166182400 | bytes 31195144 | tf_op jit(solution)/shard_map/while/body/eval_jaxpr/cond/branch_1_fun/ftr,ftc->frc/dot_general | solution.py:39
  907.4 22.1 %conditional.2 = (bf16[2,5,3584,896]{2,3,0,1:T(8,128)(2,1)}) conditional(s32[]{:T(128)} %convert_element_type.73, bf16[2,5,3584,896]{2,3,0,1:T(8,128)(2,1)} %get-tuple-element.266, (s32[]{:T(128)}, bf16[8,2,1024,896]{2,3,1,0:T(8,128)(2,1)}, bf16[2,1024,3584]{2,1,0:T(8,128)(2,1)}, s32[]{:T(128)}, bf16[2,5,3584,896]{2,3,0,1:T(8,128)(2,1)}) %tuple.60), branch_computations={%region_2.2_spmd, %region_3.3_spmd} | conditional | flops 13166182400 | bytes 31195220 | solution.py:55
  907.4 22.1 %bitcast_dynamic-update-slice_fusion = bf16[2,5,3584,896]{2,3,0,1:T(8,128)(2,1)} fusion(bf16[2,5,3584,896]{2,3,0,1:T(8,128)(2,1)} %get-tuple-element.179, s32[]{:T(128)S(6)} %select_n.35, bf16[2,1024,3584]{2,1,0:T(8,128)(2,1)} %get-tuple-element.182, bf16[8,2,1024,896]{2,3,1,0:T(8,128)(2,1)} %get-tuple-element.180, s32[]{:T(128)S(6)} %select_n.34), kind=kOutput, calls=%fused_computation.1 | convolution fusion | flops 13166182400 | bytes 31195144 | tf_op jit(solution)/shard_map/while/body/eval_jaxpr/cond/branch_1_fun/ftr,ftc->frc/dot_general | solution.py:39
  929.5 22.1 %conditional.2 = (bf16[2,5,3584,896]{2,3,0,1:T(8,128)(2,1)}) conditional(s32[]{:T(128)} %convert_element_type.73, bf16[2,5,3584,896]{2,3,0,1:T(8,128)(2,1)} %get-tuple-element.266, (s32[]{:T(128)}, bf16[8,2,1024,896]{2,3,1,0:T(8,128)(2,1)}, bf16[2,1024,3584]{2,1,0:T(8,128)(2,1)}, s32[]{:T(128)}, bf16[2,5,3584,896]{2,3,0,1:T(8,128)(2,1)}) %tuple.60), branch_computations={%region_2.2_spmd, %region_3.3_spmd} | conditional | flops 13166182400 | bytes 31195220 | solution.py:55
  929.5 22.1 %bitcast_dynamic-update-slice_fusion = bf16[2,5,3584,896]{2,3,0,1:T(8,128)(2,1)} fusion(bf16[2,5,3584,896]{2,3,0,1:T(8,128)(2,1)} %get-tuple-element.179, s32[]{:T(128)S(6)} %select_n.35, bf16[2,1024,3584]{2,1,0:T(8,128)(2,1)} %get-tuple-element.182, bf16[8,2,1024,896]{2,3,1,0:T(8,128)(2,1)} %get-tuple-element.180, s32[]{:T(128)S(6)} %select_n.34), kind=kOutput, calls=%fused_computation.1 | convolution fusion | flops 13166182400 | bytes 31195144 | tf_op jit(solution)/shard_map/while/body/eval_jaxpr/cond/branch_1_fun/ftr,ftc->frc/dot_general | solution.py:39
  951.7 22.1 %conditional.2 = (bf16[2,5,3584,896]{2,3,0,1:T(8,128)(2,1)}) conditional(s32[]{:T(128)} %convert_element_type.73, bf16[2,5,3584,896]{2,3,0,1:T(8,128)(2,1)} %get-tuple-element.266, (s32[]{:T(128)}, bf16[8,2,1024,896]{2,3,1,0:T(8,128)(2,1)}, bf16[2,1024,3584]{2,1,0:T(8,128)(2,1)}, s32[]{:T(128)}, bf16[2,5,3584,896]{2,3,0,1:T(8,128)(2,1)}) %tuple.60), branch_computations={%region_2.2_spmd, %region_3.3_spmd} | conditional | flops 13166182400 | bytes 31195220 | solution.py:55
  951.7 22.1 %bitcast_dynamic-update-slice_fusion = bf16[2,5,3584,896]{2,3,0,1:T(8,128)(2,1)} fusion(bf16[2,5,3584,896]{2,3,0,1:T(8,128)(2,1)} %get-tuple-element.179, s32[]{:T(128)S(6)} %select_n.35, bf16[2,1024,3584]{2,1,0:T(8,128)(2,1)} %get-tuple-element.182, bf16[8,2,1024,896]{2,3,1,0:T(8,128)(2,1)} %get-tuple-element.180, s32[]{:T(128)S(6)} %select_n.34), kind=kOutput, calls=%fused_computation.1 | convolution fusion | flops 13166182400 | bytes 31195144 | tf_op jit(solution)/shard_map/while/body/eval_jaxpr/cond/branch_1_fun/ftr,ftc->frc/dot_general | solution.py:39
  973.8 22.1 %conditional.2 = (bf16[2,5,3584,896]{2,3,0,1:T(8,128)(2,1)}) conditional(s32[]{:T(128)} %convert_element_type.73, bf16[2,5,3584,896]{2,3,0,1:T(8,128)(2,1)} %get-tuple-element.266, (s32[]{:T(128)}, bf16[8,2,1024,896]{2,3,1,0:T(8,128)(2,1)}, bf16[2,1024,3584]{2,1,0:T(8,128)(2,1)}, s32[]{:T(128)}, bf16[2,5,3584,896]{2,3,0,1:T(8,128)(2,1)}) %tuple.60), branch_computations={%region_2.2_spmd, %region_3.3_spmd} | conditional | flops 13166182400 | bytes 31195220 | solution.py:55
  973.8 22.1 %bitcast_dynamic-update-slice_fusion = bf16[2,5,3584,896]{2,3,0,1:T(8,128)(2,1)} fusion(bf16[2,5,3584,896]{2,3,0,1:T(8,128)(2,1)} %get-tuple-element.179, s32[]{:T(128)S(6)} %select_n.35, bf16[2,1024,3584]{2,1,0:T(8,128)(2,1)} %get-tuple-element.182, bf16[8,2,1024,896]{2,3,1,0:T(8,128)(2,1)} %get-tuple-element.180, s32[]{:T(128)S(6)} %select_n.34), kind=kOutput, calls=%fused_computation.1 | convolution fusion | flops 13166182400 | bytes 31195144 | tf_op jit(solution)/shard_map/while/body/eval_jaxpr/cond/branch_1_fun/ftr,ftc->frc/dot_general | solution.py:39
  996.0 81.6 %copy.16 = bf16[2,5,3584,896]{3,2,0,1:T(8,128)(2,1)} copy(bf16[2,5,3584,896]{2,3,0,1:T(8,128)(2,1)} %get-tuple-element.191) | data formatting | bytes 128450560 | tf_op jit(solution)/shard_map/while | solution.py:62
  1077.5 73.1 %broadcast_in_dim_reshape.3 = bf16[1,2,5,1,3211264]{4,1,3,2,0:T(2,128)(2,1)} reshape(bf16[2,5,3584,896]{3,2,0,1:T(8,128)(2,1)} %copy.16) | data formatting | bytes 128450560 | tf_op jit(solution)/shard_map/broadcast_in_dim;reshape | solution.py:64
  (7 shorter events, 0.0 us)
Async XLA Ops:
  6.5 40.6 %all-gather.5.cloned.1.call-start = ((), (), s32[]{:S(2)}) async-start(), calls=%async_computation.2 | async-start | bytes 4718592 | tf_op jit(solution)/shard_map/all_gather | solution.py:18
  8.6 411.1 %reduce-scatter.2.cloned.1.call-start = ((), (), s32[]{:S(2)}) async-start(), calls=%async_computation.3 | async-start | bytes 18350080 | tf_op jit(solution)/shard_map/reduce_scatter | solution.py:20
  173.2 246.5 %copy-start = (bf16[256,3584]{1,0:T(8,128)(2,1)S(1)}, bf16[256,3584]{1,0:T(8,128)(2,1)}, u32[]{:S(2)}) copy-start(bf16[256,3584]{1,0:T(8,128)(2,1)} %param.10) | copy-start | bytes 5505028
  173.2 503.2 %all-gather.7.cloned.1.call-start = ((), (), s32[]{:S(2)}) async-start(), calls=%async_computation.4 | async-start | bytes 18350080 | tf_op jit(solution)/shard_map/all_gather | solution.py:34
  425.4 398.7 %all-gather.9.cloned.1.call-start = ((), (), s32[]{:S(2)}) async-start(), calls=%async_computation.5 | async-start | bytes 33030144 | tf_op jit(solution)/shard_map/all_gather | solution.py:50
Sparse Core Ops, SparseCore 0:
  9.2 37.8 all-gather.4
  173.4 246.2 reduce-scatter.1
  425.6 250.8 all-gather.6
  680.8 143.3 all-gather.8
where the time goes:
time: 1160 us
  waiting for transfers between devices  679 us (59%)
  local copies, waits for them, and re-layouts  228 us (20%)
  matrix products  134 us (12%)
  blocking collectives  96.9 us (8%)
  between operations  13.2 us (1%)
    all_gather x1, waiting for transfers between devices, per_device(): own_rows = lax.all_gather(stacked, 'dp', axis=1, tiled=True)  251 us
    reduce_scatter x1, waiting for transfers between devices, per_device(): lax.psum_scatter(lax.dot_general(regrouped, down_weight, contract, prefer...  246 us
    all_gather x1, waiting for transfers between devices, per_device(): block_piece = lax.all_gather(own_slice[None], 'tensor', axis=0, tiled=True)  144 us
    while x2, local copies, waits for them, and re-layouts, per_device(): factor = lax.fori_loop(0, block_piece.shape[0], place_block, holder)  122 us
    dot_general x5, matrix products, factor_tile(): jnp.einsum('ftr,ftc->frc', own_rows, partner, preferred_element_type=jnp....  111 us
    all_to_all x1, blocking collectives, per_device(): lax.all_to_all(features, 'dp', split_axis=1, concat_axis=0, tiled=True)  96.9 us
    another operation x1, local copies, waits for them, and re-layouts, per_device(): return flat[None, :, :, None, :]  73.1 us
    all_gather x1, waiting for transfers between devices, per_device(): features = lax.all_gather(cotangent, 'tensor', axis=1, tiled=True)  38.5 us
  transfers between devices with their start and end apart: 4, of which 4 were waited for; matrix products, arithmetic and copies ran while one was open for 0% of the time, Pallas kernels for 0%

commit v1 on v0

v1 whole, which is shorter than its diff:
```python
import functools
import jax
import jax.numpy as jnp
from jax import lax
from jax.experimental import pallas as pl
from jax.experimental.pallas import tpu as pltpu
from jax.sharding import PartitionSpec as P

CHUNKS = 2
LANES = 128
CONTRACT_LAST = (((1,), (1,)), ((), ()))


def factor_kernel(band, chunk_rows, chunk_total, scale, rows_ref, *refs):
    columns = refs[: band * chunk_total]
    out_ref, held, wide, sems = refs[-4:]
    slice_width = held.shape[2]
    lane_tiles = slice_width // LANES
    stride = 2 * lane_tiles
    step, k = pl.program_id(0), pl.program_id(1)

    def column_copy(source, slot, chunk):
        return pltpu.make_async_copy(
            source,
            held.at[slot, :, pl.ds(chunk * chunk_rows, chunk_rows)],
            sems.at[slot, chunk],
        )

    @pl.when((step == 0) & (k == 0))
    def _():
        for slot in range(band):
            for chunk in range(chunk_total):
                column_copy(columns[slot * chunk_total + chunk], slot, chunk).start()

    @pl.when(step == 0)
    def _():
        for chunk in range(chunk_total):
            column_copy(columns[chunk], k, chunk).wait()

    for f in range(2):
        rows = rows_ref[0, f]
        for first in range(0, lane_tiles, 2):
            count = min(2, lane_tiles - first)
            part = held[k, f, pl.ds(first * LANES, count * LANES), :]
            product = lax.dot_general(
                rows, part, CONTRACT_LAST, preferred_element_type=jnp.float32
            )
            product = product * scale
            for extra in range(count):
                wide[pl.ds((first + extra) * 2 + f, chunk_rows, stride=stride), :] = product[
                    :, extra * LANES : (extra + 1) * LANES
                ]
    out_ref[0] = wide[...].astype(out_ref.dtype)


def factor_rows(rows, columns, chunk, previous, slice_width, scale):
    slices, _, chunk_rows, tokens = rows.shape
    band = len(columns)
    chunk_total = len(columns[0])
    lane_tiles = slice_width // LANES
    height = chunk_rows * 2 * lane_tiles
    operands = [rows] + [piece for pieces in columns for piece in pieces]
    anywhere = pl.BlockSpec(memory_space=pl.ANY)
    in_specs = [pl.BlockSpec((1, 2, chunk_rows, tokens), lambda s, k: (s, 0, 0, 0))]
    in_specs += [anywhere] * (len(operands) - 1)
    aliases = {}
    if previous is not None:
        aliases = {len(operands): 0}
        operands.append(previous)
        in_specs.append(anywhere)
    return pl.pallas_call(
        functools.partial(factor_kernel, band, chunk_rows, chunk_total, scale),
        grid=(slices, band),
        in_specs=in_specs,
        out_specs=pl.BlockSpec((1, height, LANES), lambda s, k: (k, s * chunk_total + chunk, 0)),
        out_shape=jax.ShapeDtypeStruct((band, slices * chunk_total * height, LANES), rows.dtype),
        scratch_shapes=[
            pltpu.VMEM((band, 2, slice_width, tokens), rows.dtype),
            pltpu.VMEM((height, LANES), jnp.float32),
            pltpu.SemaphoreType.DMA((band, chunk_total)),
        ],
        input_output_aliases=aliases,
        compiler_params=pltpu.CompilerParams(
            dimension_semantics=("arbitrary", "arbitrary"), vmem_limit_bytes=52 * 2**20
        ),
        cost_estimate=pl.CostEstimate(
            flops=4 * slices * chunk_rows * tokens * band * slice_width,
            bytes_accessed=4 * slices * chunk_rows * (tokens + band * slice_width)
            + 4 * band * slice_width * tokens,
            transcendentals=0,
        ),
    )(*operands)


def per_device(cotangent, down_weight, gate_pre, up_pre):
    blocks = lax.axis_size("tensor")
    groups = lax.axis_size("dp")
    own_block = lax.axis_index("tensor")
    own_group = lax.axis_index("dp")
    per_group = blocks // groups
    local_tokens, block_width = gate_pre.shape
    slice_width = block_width // groups
    all_tokens = local_tokens * groups
    half_band = blocks // 2
    chunk_rows = slice_width // CHUNKS

    to_plane = [
        ((m * per_group + q) * groups + g, (g * per_group + q) * groups + m)
        for m in range(groups)
        for q in range(per_group)
        for g in range(groups)
    ]
    sent = lax.ppermute(cotangent.T, ("tensor", "dp"), to_plane)
    features = lax.all_gather(sent, "tensor", axis=0, tiled=True)
    features = features.reshape(groups, -1, local_tokens)
    features = features.transpose(1, 0, 2).reshape(-1, all_tokens)

    saved = jnp.stack([gate_pre, up_pre])

    def saved_slice(index):
        return lax.dynamic_slice_in_dim(saved, (index % groups) * slice_width, slice_width, 2)

    pieces = [saved_slice(own_group)]
    for shift in range(1, groups):
        ring = [(d, (d + shift) % groups) for d in range(groups)]
        pieces.append(lax.ppermute(saved_slice(own_group + shift), "dp", ring))
    pieces = jnp.stack(pieces)
    saved_all = jnp.concatenate(
        [
            lax.dynamic_index_in_dim(pieces, (own_group - h) % groups, 0, keepdims=False)
            for h in range(groups)
        ],
        axis=1,
    )
    saved_all = saved_all.transpose(0, 2, 1)

    weight = down_weight.reshape(groups, slice_width, -1)

    def reduced(chunk):
        part = weight[:, chunk * chunk_rows : (chunk + 1) * chunk_rows]
        partial = lax.dot_general(
            part.reshape(groups * chunk_rows, -1),
            features,
            (((1,), (0,)), ((), ())),
            preferred_element_type=jnp.float32,
        ).reshape(groups, chunk_rows, all_tokens)

        def slot(offset):
            return lax.dynamic_index_in_dim(
                partial, (own_group + offset) % groups, 0, keepdims=False
            )

        from_left = from_right = None
        for step in range(1, groups):
            right, left = slot(groups - step), slot(step)
            if step > 1:
                right = right + from_left.astype(jnp.float32)
                left = left + from_right.astype(jnp.float32)
            from_left = lax.ppermute(
                right.astype(jnp.bfloat16), "dp", [(d, d + 1) for d in range(step)]
            )
            from_right = lax.ppermute(
                left.astype(jnp.bfloat16),
                "dp",
                [(d, d - 1) for d in range(groups - step, groups)],
            )
        return slot(0) + from_left.astype(jnp.float32) + from_right.astype(jnp.float32)

    def gradients(chunk):
        hidden_cot = reduced(chunk)
        local = saved_all[:, chunk * chunk_rows : (chunk + 1) * chunk_rows].astype(jnp.float32)
        gate_value, up_value = local[0], local[1]
        sigmoid_gate = jax.nn.sigmoid(gate_value)
        grad_gate = hidden_cot * up_value * sigmoid_gate * (1.0 + gate_value * (1.0 - sigmoid_gate))
        grad_up = hidden_cot * gate_value * sigmoid_gate
        return jnp.stack([grad_gate.astype(jnp.bfloat16), grad_up.astype(jnp.bfloat16)])

    def partners(own):
        found = {0: own}
        for k in range(2, half_band + 1, 2):
            found[k] = lax.ppermute(
                own, "tensor", [(t, (t + k) % blocks) for t in range(blocks)]
            )
        swap = [(t, t ^ 1) for t in range(blocks)]
        odd = own_block % 2 == 1
        for k in range(1, half_band, 2):
            found[k] = lax.ppermute(jnp.where(odd, found[k + 1], found[k - 1]), "tensor", swap)
        return [found[k] for k in range(half_band + 1)]

    rows, columns = [], []
    for chunk in range(CHUNKS):
        own = gradients(chunk)
        rows.append(lax.all_gather(own, "dp", axis=0))
        columns.append(partners(own))
    columns = [[columns[c][k] for c in range(CHUNKS)] for k in range(half_band + 1)]
    inverse_count = 1.0 / all_tokens

    if slice_width % LANES == 0 and chunk_rows % 16 == 0:
        result = None
        for chunk in range(CHUNKS):
            result = factor_rows(rows[chunk], columns, chunk, result, slice_width, inverse_count)
        result = result.reshape(half_band + 1, -1, 2, LANES).transpose(2, 0, 1, 3)
    else:
        all_rows = jnp.concatenate(rows, axis=2)
        all_columns = jnp.stack([jnp.concatenate(pieces, axis=1) for pieces in columns])
        result = jnp.einsum(
            "sfrt,kfct->fksrc", all_rows, all_columns, preferred_element_type=jnp.float32
        )
        result = (result * inverse_count).astype(jnp.bfloat16)
    return result.reshape(1, 2, half_band + 1, 1, block_width * slice_width)


def solution(mesh):
    placed = (P("dp", "tensor"), P("tensor", "dp"), P("dp", "tensor"), P("dp", "tensor"))
    return jax.shard_map(
        per_device,
        mesh=mesh,
        in_specs=placed,
        out_specs=P("tensor", None, None, "dp", None),
        check_vma=False,
    )
```

time: 1160 us -> 751 us (0.65)
  waiting for transfers between devices: 679 us -> 417 us
  local copies, waits for them, and re-layouts: 228 us -> 41.3 us
  starting transfers between devices: 0.31 us -> 123 us
  matrix products: 134 us -> 22.5 us
  Pallas kernels: 0 us -> 97.4 us
  blocking collectives: 96.9 us -> 0 us
  other arithmetic: 5.71 us -> 32.1 us
    all_gather x3, waiting for transfers between devices: 433 us -> 37.8 us  [the longest x1 37.8 us: per_device(): features = lax.all_gather(sent, 'tensor', axis=0, tiled=True)]
    ppermute x0 -> x24, waiting for transfers between devices: none -> 379 us  [the longest x4 147 us: partners(): lax.ppermute(own, 'tensor', [(t, (t + k) % blocks) for t in range(blocks)])]
    reduce_scatter x1 -> x0, waiting for transfers between devices: 246 us -> none  [per_device(): lax.psum_scatter(lax.dot_general(regrouped, down_weight, contract, prefer...]
    ppermute x0 -> x24, starting transfers between devices: none -> 123 us  [the longest x6 80 us: reduced(): lax.ppermute(left.astype(jnp.bfloat16), 'dp', [(d, d - 1) for d in range(...]
    while x2 -> x0, local copies, waits for them, and re-layouts: 122 us -> none  [per_device(): factor = lax.fori_loop(0, block_piece.shape[0], place_block, holder)]
    dot_general x6 -> x2, matrix products: 134 us -> 22.5 us  [reduced(): lax.dot_general(part.reshape(groups * chunk_rows, -1), features, (((1,),...]
    pallas_call x0 -> x2, Pallas kernels: none -> 97.4 us  [factor_rows(): pl.pallas_call(functools.partial(factor_kernel, band, chunk_rows, chunk_t...]
    all_to_all x1 -> x0, blocking collectives: 96.9 us -> none  [per_device(): lax.all_to_all(features, 'dp', split_axis=1, concat_axis=0, tiled=True)]
  transfers between devices with their start and end apart: 4 -> 27, of which waited for: 4 -> 13; matrix products, arithmetic and copies ran while one was open for 0% -> 6% of each run, Pallas kernels for 0% -> 7%
where the time goes in v1:
time: 751 us; the launch traced here: 747 us
  waiting for transfers between devices  417 us (56%)
  starting transfers between devices  123 us (16%)
  Pallas kernels  97.4 us (13%)
  local copies, waits for them, and re-layouts  41.3 us (5%)
  other arithmetic  32.1 us (4%)
  matrix products  22.5 us (3%)
  between operations  13.4 us (2%)
    ppermute x4, waiting for transfers between devices, partners(): lax.ppermute(own, 'tensor', [(t, (t + k) % blocks) for t in range(blocks)])  147 us
    ppermute x6, waiting for transfers between devices, reduced(): lax.ppermute(left.astype(jnp.bfloat16), 'dp', [(d, d - 1) for d in range(...  108 us
    pallas_call x2, Pallas kernels, factor_rows(): pl.pallas_call(functools.partial(factor_kernel, band, chunk_rows, chunk_t...  97.4 us
    ppermute x6, starting transfers between devices, reduced(): lax.ppermute(left.astype(jnp.bfloat16), 'dp', [(d, d - 1) for d in range(...  80 us
    ppermute x3, waiting for transfers between devices, per_device(): pieces.append(lax.ppermute(saved_slice(own_group + shift), 'dp', ring))  72 us
    all_gather x1, waiting for transfers between devices, per_device(): features = lax.all_gather(sent, 'tensor', axis=0, tiled=True)  37.8 us
    ppermute x1, waiting for transfers between devices, per_device(): sent = lax.ppermute(cotangent.T, ('tensor', 'dp'), to_plane)  35.4 us
    dot_general x2, matrix products, reduced(): lax.dot_general(part.reshape(groups * chunk_rows, -1), features, (((1,),...  22.5 us
  transfers between devices with their start and end apart: 27, of which 13 were waited for; matrix products, arithmetic and copies ran while one was open for 6% of the time, Pallas kernels for 7%

profile of v1, /device:TPU:29, one launch (start us, length us, event | category | flops | bytes accessed | tf_op | source)
XLA Modules:
  0.0 746.7 jit_solution(4291860524262160027)
XLA Ops:
  9.5 35.4 %collective-permute-done = bf16[1024,256]{0,1:T(8,128)(2,1)S(1)} collective-permute-done((bf16[1024,256]{0,1:T(8,128)(2,1)}, bf16[1024,256]{0,1:T(8,128)(2,1)S(1)}, u32[]{:S(2)}, u32[]{:S(2)}) %collective-permute-start) | collective-permute-done | bytes 524320 | tf_op jit(solution)/shard_map/ppermute | solution.py:113
  45.9 37.8 %all-gather.6.cloned.1.call-done = bf16[8192,256]{0,1:T(8,128)(2,1)} async-done(((bf16[1024,256]{0,1:T(8,128)(2,1)}), bf16[8192,256]{0,1:T(8,128)(2,1)}) %all-gather.6.cloned.1.call-update) | async-done | bytes 4194320 | tf_op jit(solution)/shard_map/all_gather | solution.py:114
  83.6 7.8 %reshape.24 = bf16[4,2048,256]{1,0,2:T(4,128)(2,1)} reshape(bf16[8192,256]{0,1:T(8,128)(2,1)} %all-gather.6.cloned.1.call-done) | data formatting | bytes 8388608 | tf_op jit(solution)/shard_map/reshape | solution.py:115
  91.4 10.2 %copy.12 = bf16[4,2048,256]{2,0,1:T(4,128)(2,1)} copy(bf16[4,2048,256]{1,0,2:T(4,128)(2,1)} %reshape.24) | data formatting | bytes 8388608 | tf_op jit(solution)/shard_map/reshape | solution.py:115
  101.6 7.8 %reshape.30 = bf16[2048,1024,1]{1,0,2:T(8,128)(2,1)} reshape(bf16[2048,4,256]{2,1,0:T(4,128)(2,1)} %bitcast.129) | data formatting | bytes 8388608 | tf_op jit(solution)/shard_map/reshape | solution.py:116
  109.4 11.2 %fusion = f32[4,448,1024]{2,1,0:T(8,128)S(1)} fusion(bf16[2048,1024,1]{1,0,2:T(8,128)(2,1)} %reshape.30, bf16[4,896,2048]{2,1,0:T(8,128)(2,1)} %bitcast.139), kind=kOutput, calls=%fused_computation | convolution fusion | flops 7516192768 | bytes 18874368 | tf_op jit(solution)/shard_map/dot_general | solution.py:141
  120.6 3.0 copy-done.1
  126.5 3.2 collective-permute-start.13
  129.8 3.0 fusion.13
  134.4 3.2 fusion.24
  137.6 21.5 %collective-permute-start.7 = (bf16[2,256,896]{2,1,0:T(8,128)(2,1)}, bf16[2,256,896]{2,1,0:T(8,128)(2,1)S(1)}, u32[]{:S(2)}, u32[]{:S(2)}) collective-permute-start(bf16[2,256,896]{2,1,0:T(8,128)(2,1)} %get-tuple-element.24), channel_id=1, source_target_pairs={{0,1},{1,2},{2,3},{3,0},{4,5},{5,6},{6,7},{7,4},{8,9},{9,10},{10,1... | collective-permute-start | bytes 2752520 | tf_op jit(solution)/shard_map/ppermute | solution.py:126
  159.4 3.5 fusion.15
  162.9 17.4 %collective-permute-start.14 = (bf16[448,1024]{1,0:T(8,128)(2,1)}, bf16[448,1024]{1,0:T(8,128)(2,1)}, u32[]{:S(2)}, u32[]{:S(2)}) collective-permute-start(bf16[448,1024]{1,0:T(8,128)(2,1)} %get-tuple-element.10), channel_id=1, source_target_pairs={{2,1},{3,2},{6,5},{7,6},{10,9},{11,10},{14,13},{15,14},{18,17},{19... | collective-permute-start | bytes 2752520 | tf_op jit(solution)/shard_map/ppermute | solution.py:162
  180.2 71.9 %collective-permute-done.8 = bf16[2,256,896]{2,1,0:T(8,128)(2,1)S(1)} collective-permute-done((bf16[2,256,896]{2,1,0:T(8,128)(2,1)}, bf16[2,256,896]{2,1,0:T(8,128)(2,1)S(1)}, u32[]{:S(2)}, u32[]{:S(2)}) %collective-permute-start.8) | collective-permute-done | bytes 917536 | tf_op jit(solution)/shard_map/ppermute | solution.py:126
  255.1 3.0 fusion.12
  258.1 5.2 collective-permute-start.15
  276.2 4.5 collective-permute-done.15
  280.7 3.2 fusion.30
  286.6 11.2 %fusion.2 = f32[4,448,1024]{2,1,0:T(8,128)S(1)} fusion(bf16[2048,1024,1]{1,0,2:T(8,128)(2,1)} %reshape.30, bf16[4,896,2048]{2,1,0:T(8,128)(2,1)} %bitcast.140), kind=kOutput, calls=%fused_computation.2 | convolution fusion | flops 7516192768 | bytes 18874368 | tf_op jit(solution)/shard_map/dot_general | solution.py:141
  298.9 4.4 collective-permute-start.4
  304.3 37.7 %collective-permute-done.4 = bf16[448,1024]{1,0:T(8,128)(2,1)S(1)} collective-permute-done((bf16[448,1024]{1,0:T(8,128)(2,1)S(1)}, bf16[448,1024]{1,0:T(8,128)(2,1)S(1)}, u32[]{:S(2)}, u32[]{:S(2)}) %collective-permute-start.4) | collective-permute-done | bytes 917536 | tf_op jit(solution)/shard_map/ppermute | solution.py:162
  342.8 45.2 %collective-permute-start.5 = (bf16[448,1024]{1,0:T(8,128)(2,1)S(1)}, bf16[448,1024]{1,0:T(8,128)(2,1)S(1)}, u32[]{:S(2)}, u32[]{:S(2)}) collective-permute-start(bf16[448,1024]{1,0:T(8,128)(2,1)S(1)} %get-tuple-element.14), channel_id=1, source_target_pairs={{2,1},{3,2},{6,5},{7,6},{10,9},{11,10},{14,13},{15,14},{18,17},{19... | collective-permute-start | bytes 2752520 | tf_op jit(solution)/shard_map/ppermute | solution.py:162
  389.6 36.8 %collective-permute-done.5 = bf16[448,1024]{1,0:T(8,128)(2,1)S(1)} collective-permute-done((bf16[448,1024]{1,0:T(8,128)(2,1)S(1)}, bf16[448,1024]{1,0:T(8,128)(2,1)S(1)}, u32[]{:S(2)}, u32[]{:S(2)}) %collective-permute-start.5) | collective-permute-done | bytes 917536 | tf_op jit(solution)/shard_map/ppermute | solution.py:162
  426.7 4.6 collective-permute-start.6
  431.4 8.3 %collective-permute-done.3 = bf16[448,1024]{1,0:T(8,128)(2,1)S(1)} collective-permute-done((bf16[448,1024]{1,0:T(8,128)(2,1)S(1)}, bf16[448,1024]{1,0:T(8,128)(2,1)S(1)}, u32[]{:S(2)}, u32[]{:S(2)}) %collective-permute-start.3) | collective-permute-done | bytes 917536 | tf_op jit(solution)/shard_map/ppermute | solution.py:159
  439.7 28.6 %collective-permute-done.6 = bf16[448,1024]{1,0:T(8,128)(2,1)S(1)} collective-permute-done((bf16[448,1024]{1,0:T(8,128)(2,1)S(1)}, bf16[448,1024]{1,0:T(8,128)(2,1)S(1)}, u32[]{:S(2)}, u32[]{:S(2)}) %collective-permute-start.6) | collective-permute-done | bytes 917536 | tf_op jit(solution)/shard_map/ppermute | solution.py:162
  478.3 114.8 %collective-permute-done.20.refs_8_ = bf16[2,448,1024]{2,1,0:T(8,128)(2,1)} collective-permute-done((bf16[2,448,1024]{2,1,0:T(8,128)(2,1)S(1)}, bf16[2,448,1024]{2,1,0:T(8,128)(2,1)}, u32[]{:S(2)}, u32[]{:S(2)}) %collective-permute-start.20) | collective-permute-done | bytes 1835040 | tf_op jit(solution)/shard_map/ppermute | solution.py:181
  595.7 4.3 collective-permute-start.21
  600.1 32.4 %collective-permute-done.22.refs_9_ = bf16[2,448,1024]{2,1,0:T(8,128)(2,1)} collective-permute-done((bf16[2,448,1024]{2,1,0:T(8,128)(2,1)}, bf16[2,448,1024]{2,1,0:T(8,128)(2,1)}, u32[]{:S(2)}, u32[]{:S(2)}) %collective-permute-start.22) | collective-permute-done | bytes 1835040 | tf_op jit(solution)/shard_map/ppermute | solution.py:181
  636.7 3.5 collective-permute-done.23.refs_7_
  642.8 48.7 %shard_map.46.refs_10_ = bf16[5,50176,128]{2,1,0:T(8,128)(2,1)} custom-call(bf16[4,2,448,1024]{3,2,1,0:T(8,128)(2,1)} %bitcast.141, bf16[2,448,1024]{2,1,0:T(8,128)(2,1)S(1)} %copy-done, bf16[2,448,1024]{2,1,0:T(8,128)(2,1)} %pad_maximum_fusion.1.refs_1_, bf16[2,448,1024]{2,1,0:T(8,128)(2,1)} %collective-permute-done.17.refs_2_, ...), custom_call_target="tpu_custom_call" | custom-call | flops 32883343360 | bytes 57802752 | tf_op jit(solution)/shard_map/pallas_call | solution.py:71
  691.5 48.7 %shard_map.47 = bf16[5,50176,128]{2,1,0:T(8,128)(2,1)} custom-call(bf16[4,2,448,1024]{3,2,1,0:T(8,128)(2,1)} %bitcast.130, bf16[2,448,1024]{2,1,0:T(8,128)(2,1)S(1)} %copy-done, bf16[2,448,1024]{2,1,0:T(8,128)(2,1)} %pad_maximum_fusion.1.refs_1_, bf16[2,448,1024]{2,1,0:T(8,128)(2,1)} %collective-permute-done.17.refs_2_, ...), custom_call_target="tpu_custom_call", output_to_operand_aliasing={{}: (11, {})} | custom-call | flops 32883343360 | bytes 57802752 | tf_op jit(solution)/shard_map/pallas_call | solution.py:71
  (77 shorter events, 51.2 us)
Async XLA Ops:
  6.5 77.1 %all-gather.6.cloned.1.call-start = ((), (), s32[]{:S(2)}) async-start(), calls=%async_computation | async-start | bytes 4718592 | tf_op jit(solution)/shard_map/all_gather | solution.py:114
  6.5 38.4 %collective-permute-start = (bf16[1024,256]{0,1:T(8,128)(2,1)}, bf16[1024,256]{0,1:T(8,128)(2,1)S(1)}, u32[]{:S(2)}, u32[]{:S(2)}) collective-permute-start(bf16[1024,256]{0,1:T(8,128)(2,1)} %bitcast.142), channel_id=1, source_target_pairs={{0,0},{1,8},{2,16},{3,24},{4,4},{5,12},{6,20},{7,28},{8,1},{9,9},{... | collective-permute-start | bytes 1572872 | tf_op jit(solution)/shard_map/ppermute | solution.py:113
  45.8 597.0 %all-gather.10.cloned.1.call-start = ((), (), s32[]{:S(2)}) async-start(), calls=%async_computation.2 | async-start | bytes 9175040 | tf_op jit(solution)/shard_map/all_gather | solution.py:193
  124.9 4.8 collective-permute-start.10
  126.5 7.9 %copy-start.9 = (bf16[256,3584]{1,0:T(8,128)(2,1)S(1)}, bf16[256,3584]{1,0:T(8,128)(2,1)}, u32[]{:S(2)}) copy-start(bf16[256,3584]{1,0:T(8,128)(2,1)} %param.6) | copy-start | bytes 5505028
  126.5 32.9 %collective-permute-start.13 = (bf16[448,1024]{1,0:T(8,128)(2,1)}, bf16[448,1024]{1,0:T(8,128)(2,1)}, u32[]{:S(2)}, u32[]{:S(2)}) collective-permute-start(bf16[448,1024]{1,0:T(8,128)(2,1)} %get-tuple-element.12), channel_id=1, source_target_pairs={{3,2},{7,6},{11,10},{15,14},{19,18},{23,22},{27,26},{31,30}} | collective-permute-start | bytes 2752520 | tf_op jit(solution)/shard_map/ppermute | solution.py:162
  132.8 26.6 %collective-permute-start.11 = (bf16[448,1024]{1,0:T(8,128)(2,1)}, bf16[448,1024]{1,0:T(8,128)(2,1)}, u32[]{:S(2)}, u32[]{:S(2)}) collective-permute-start(bf16[448,1024]{1,0:T(8,128)(2,1)} %fusion.13), channel_id=1, source_target_pairs={{0,1},{1,2},{4,5},{5,6},{8,9},{9,10},{12,13},{13,14},{16,17},{17,1... | collective-permute-start | bytes 2752520 | tf_op jit(solution)/shard_map/ppermute | solution.py:159
  134.4 25.0 %copy-start.2 = (f32[4,448,1024]{2,1,0:T(8,128)S(1)}, f32[4,448,1024]{2,1,0:T(8,128)}, u32[]{:S(2)}) copy-start(f32[4,448,1024]{2,1,0:T(8,128)} %copy-done.1) | copy-start | bytes 22020100
  137.6 42.6 %collective-permute-start.7 = (bf16[2,256,896]{2,1,0:T(8,128)(2,1)}, bf16[2,256,896]{2,1,0:T(8,128)(2,1)S(1)}, u32[]{:S(2)}, u32[]{:S(2)}) collective-permute-start(bf16[2,256,896]{2,1,0:T(8,128)(2,1)} %get-tuple-element.24), channel_id=1, source_target_pairs={{0,1},{1,2},{2,3},{3,0},{4,5},{5,6},{6,7},{7,4},{8,9},{9,10},{10,1... | collective-permute-start | bytes 2752520 | tf_op jit(solution)/shard_map/ppermute | solution.py:126
  159.1 93.1 %collective-permute-start.8 = (bf16[2,256,896]{2,1,0:T(8,128)(2,1)}, bf16[2,256,896]{2,1,0:T(8,128)(2,1)S(1)}, u32[]{:S(2)}, u32[]{:S(2)}) collective-permute-start(bf16[2,256,896]{2,1,0:T(8,128)(2,1)} %get-tuple-element.25), channel_id=1, source_target_pairs={{0,2},{1,3},{2,0},{3,1},{4,6},{5,7},{6,4},{7,5},{8,10},{9,11},{10,... | collective-permute-start | bytes 2752520 | tf_op jit(solution)/shard_map/ppermute | solution.py:126
  159.1 93.1 %collective-permute-start.9 = (bf16[2,256,896]{2,1,0:T(8,128)(2,1)}, bf16[2,256,896]{2,1,0:T(8,128)(2,1)}, u32[]{:S(2)}, u32[]{:S(2)}) collective-permute-start(bf16[2,256,896]{2,1,0:T(8,128)(2,1)} %get-tuple-element.26), channel_id=1, source_target_pairs={{0,3},{1,0},{2,1},{3,2},{4,7},{5,4},{6,5},{7,6},{8,11},{9,8},{10,9... | collective-permute-start | bytes 2752520 | tf_op jit(solution)/shard_map/ppermute | solution.py:126
  162.9 92.2 %collective-permute-start.14 = (bf16[448,1024]{1,0:T(8,128)(2,1)}, bf16[448,1024]{1,0:T(8,128)(2,1)}, u32[]{:S(2)}, u32[]{:S(2)}) collective-permute-start(bf16[448,1024]{1,0:T(8,128)(2,1)} %get-tuple-element.10), channel_id=1, source_target_pairs={{2,1},{3,2},{6,5},{7,6},{10,9},{11,10},{14,13},{15,14},{18,17},{19... | collective-permute-start | bytes 2752520 | tf_op jit(solution)/shard_map/ppermute | solution.py:162
  253.8 22.3 %collective-permute-start.12 = (bf16[448,1024]{1,0:T(8,128)(2,1)}, bf16[448,1024]{1,0:T(8,128)(2,1)}, u32[]{:S(2)}, u32[]{:S(2)}) collective-permute-start(bf16[448,1024]{1,0:T(8,128)(2,1)} %get-tuple-element.9), channel_id=1, source_target_pairs={{0,1},{1,2},{2,3},{4,5},{5,6},{6,7},{8,9},{9,10},{10,11},{12,13},{... | collective-permute-start | bytes 2752520 | tf_op jit(solution)/shard_map/ppermute | solution.py:159
  258.1 22.6 %collective-permute-start.15 = (bf16[448,1024]{1,0:T(8,128)(2,1)}, bf16[448,1024]{1,0:T(8,128)(2,1)}, u32[]{:S(2)}, u32[]{:S(2)}) collective-permute-start(bf16[448,1024]{1,0:T(8,128)(2,1)} %fusion.12), channel_id=1, source_target_pairs={{1,0},{2,1},{3,2},{5,4},{6,5},{7,6},{9,8},{10,9},{11,10},{13,12},{... | collective-permute-start | bytes 2752520 | tf_op jit(solution)/shard_map/ppermute | solution.py:162
  286.3 405.1 %all-gather.8.cloned.1.call-start = ((), (), s32[]{:S(2)}) async-start(), calls=%async_computation.1 | async-start | bytes 9175040 | tf_op jit(solution)/shard_map/all_gather | solution.py:193
  298.1 5.1 collective-permute-start.1
  298.9 43.2 %collective-permute-start.4 = (bf16[448,1024]{1,0:T(8,128)(2,1)S(1)}, bf16[448,1024]{1,0:T(8,128)(2,1)S(1)}, u32[]{:S(2)}, u32[]{:S(2)}) collective-permute-start(bf16[448,1024]{1,0:T(8,128)(2,1)S(1)} %get-tuple-element.16), channel_id=1, source_target_pairs={{3,2},{7,6},{11,10},{15,14},{19,18},{23,22},{27,26},{31,30}} | collective-permute-start | bytes 2752520 | tf_op jit(solution)/shard_map/ppermute | solution.py:162
  303.6 38.4 %collective-permute-start.2 = (bf16[448,1024]{1,0:T(8,128)(2,1)S(1)}, bf16[448,1024]{1,0:T(8,128)(2,1)S(1)}, u32[]{:S(2)}, u32[]{:S(2)}) collective-permute-start(bf16[448,1024]{1,0:T(8,128)(2,1)S(1)} %fusion.18), channel_id=1, source_target_pairs={{0,1},{1,2},{4,5},{5,6},{8,9},{9,10},{12,13},{13,14},{16,17},{17,1... | collective-permute-start | bytes 2752520 | tf_op jit(solution)/shard_map/ppermute | solution.py:159
  342.8 83.6 %collective-permute-start.5 = (bf16[448,1024]{1,0:T(8,128)(2,1)S(1)}, bf16[448,1024]{1,0:T(8,128)(2,1)S(1)}, u32[]{:S(2)}, u32[]{:S(2)}) collective-permute-start(bf16[448,1024]{1,0:T(8,128)(2,1)S(1)} %get-tuple-element.14), channel_id=1, source_target_pairs={{2,1},{3,2},{6,5},{7,6},{10,9},{11,10},{14,13},{15,14},{18,17},{19... | collective-permute-start | bytes 2752520 | tf_op jit(solution)/shard_map/ppermute | solution.py:162
  388.0 80.2 %copy-start.3 = (f32[2,448,1024]{2,1,0:T(8,128)S(1)}, f32[2,448,1024]{2,1,0:T(8,128)}, u32[]{:S(2)}) copy-start(f32[2,448,1024]{2,1,0:T(8,128)} %get-tuple-element.18) | copy-start | bytes 11010052
  388.1 51.6 %collective-permute-start.3 = (bf16[448,1024]{1,0:T(8,128)(2,1)S(1)}, bf16[448,1024]{1,0:T(8,128)(2,1)S(1)}, u32[]{:S(2)}, u32[]{:S(2)}) collective-permute-start(bf16[448,1024]{1,0:T(8,128)(2,1)S(1)} %get-tuple-element.13), channel_id=1, source_target_pairs={{0,1},{1,2},{2,3},{4,5},{5,6},{6,7},{8,9},{9,10},{10,11},{12,13},{... | collective-permute-start | bytes 2752520 | tf_op jit(solution)/shard_map/ppermute | solution.py:159
  426.7 41.5 %collective-permute-start.6 = (bf16[448,1024]{1,0:T(8,128)(2,1)S(1)}, bf16[448,1024]{1,0:T(8,128)(2,1)S(1)}, u32[]{:S(2)}, u32[]{:S(2)}) collective-permute-start(bf16[448,1024]{1,0:T(8,128)(2,1)S(1)} %fusion.17), channel_id=1, source_target_pairs={{1,0},{2,1},{3,2},{5,4},{6,5},{7,6},{9,8},{10,9},{11,10},{13,12},{... | collective-permute-start | bytes 2752520 | tf_op jit(solution)/shard_map/ppermute | solution.py:162
  473.6 119.4 %collective-permute-start.20 = (bf16[2,448,1024]{2,1,0:T(8,128)(2,1)S(1)}, bf16[2,448,1024]{2,1,0:T(8,128)(2,1)}, u32[]{:S(2)}, u32[]{:S(2)}) collective-permute-start(bf16[2,448,1024]{2,1,0:T(8,128)(2,1)S(1)} %copy-done), channel_id=1, source_target_pairs={{0,16},{4,20},{8,24},{12,28},{16,0},{20,4},{24,8},{28,12},{1,17},{... | collective-permute-start | bytes 5505032 | tf_op jit(solution)/shard_map/ppermute | solution.py:181
  475.6 117.4 %collective-permute-start.16 = (bf16[2,448,1024]{2,1,0:T(8,128)(2,1)S(1)}, bf16[2,448,1024]{2,1,0:T(8,128)(2,1)}, u32[]{:S(2)}, u32[]{:S(2)}) collective-permute-start(bf16[2,448,1024]{2,1,0:T(8,128)(2,1)S(1)} %copy-done), channel_id=1, source_target_pairs={{0,8},{4,12},{8,16},{12,20},{16,24},{20,28},{24,0},{28,4},{1,9},{5... | collective-permute-start | bytes 5505032 | tf_op jit(solution)/shard_map/ppermute | solution.py:181
  476.2 156.3 %collective-permute-start.22 = (bf16[2,448,1024]{2,1,0:T(8,128)(2,1)}, bf16[2,448,1024]{2,1,0:T(8,128)(2,1)}, u32[]{:S(2)}, u32[]{:S(2)}) collective-permute-start(bf16[2,448,1024]{2,1,0:T(8,128)(2,1)} %pad_maximum_fusion.1.refs_1_), channel_id=1, source_target_pairs={{0,16},{4,20},{8,24},{12,28},{16,0},{20,4},{24,8},{28,12},{1,17},{... | collective-permute-start | bytes 5505032 | tf_op jit(solution)/shard_map/ppermute | solution.py:181
  476.2 156.3 %collective-permute-start.18 = (bf16[2,448,1024]{2,1,0:T(8,128)(2,1)}, bf16[2,448,1024]{2,1,0:T(8,128)(2,1)}, u32[]{:S(2)}, u32[]{:S(2)}) collective-permute-start(bf16[2,448,1024]{2,1,0:T(8,128)(2,1)} %pad_maximum_fusion.1.refs_1_), channel_id=1, source_target_pairs={{0,8},{4,12},{8,16},{12,20},{16,24},{20,28},{24,0},{28,4},{1,9},{5... | collective-permute-start | bytes 5505032 | tf_op jit(solution)/shard_map/ppermute | solution.py:181
  478.3 154.2 %copy-start.6 = (bf16[1,448,1024]{2,1,0:T(8,128)(2,1)S(1)}, bf16[1,448,1024]{2,1,0:T(8,128)(2,1)}, u32[]{:S(2)}) copy-start(bf16[1,448,1024]{2,1,0:T(8,128)(2,1)} %copy-done.5) | copy-start | bytes 2752516
  478.3 154.2 %copy-start.8 = (bf16[1,448,1024]{2,1,0:T(8,128)(2,1)S(1)}, bf16[1,448,1024]{2,1,0:T(8,128)(2,1)}, u32[]{:S(2)}) copy-start(bf16[1,448,1024]{2,1,0:T(8,128)(2,1)} %copy-done.7) | copy-start | bytes 2752516
  595.7 41.0 %collective-permute-start.21 = (bf16[2,448,1024]{2,1,0:T(8,128)(2,1)S(1)}, bf16[2,448,1024]{2,1,0:T(8,128)(2,1)}, u32[]{:S(2)}, u32[]{:S(2)}) collective-permute-start(bf16[2,448,1024]{2,1,0:T(8,128)(2,1)S(1)} %get-tuple-element.29), channel_id=1, source_target_pairs={{0,4},{4,0},{8,12},{12,8},{16,20},{20,16},{24,28},{28,24},{1,5},{5... | collective-permute-start | bytes 5505032 | tf_op jit(solution)/shard_map/ppermute | solution.py:187
  600.0 36.7 %collective-permute-start.17 = (bf16[2,448,1024]{2,1,0:T(8,128)(2,1)S(1)}, bf16[2,448,1024]{2,1,0:T(8,128)(2,1)}, u32[]{:S(2)}, u32[]{:S(2)}) collective-permute-start(bf16[2,448,1024]{2,1,0:T(8,128)(2,1)S(1)} %get-tuple-element.30), channel_id=1, source_target_pairs={{0,4},{4,0},{8,12},{12,8},{16,20},{20,16},{24,28},{28,24},{1,5},{5... | collective-permute-start | bytes 5505032 | tf_op jit(solution)/shard_map/ppermute | solution.py:187
  634.9 5.3 collective-permute-start.23
  636.6 6.2 collective-permute-start.19
  (6 other events, 8.7 us)
Sparse Core Ops, SparseCore 0:
  45.9 37.6 all-gather.5
  286.5 191.3 all-gather.9
  479.4 132.0 all-gather.7

commit v2 on v1

v2 whole, which is shorter than its diff:
```python
import functools
import jax
import jax.numpy as jnp
from jax import lax
from jax.experimental import pallas as pl
from jax.experimental.pallas import tpu as pltpu
from jax.sharding import PartitionSpec as P

CHUNKS = 2
LANES = 128
CONTRACT_LAST = (((1,), (1,)), ((), ()))


def factor_kernel(shape, candidates, scale, table_ref, *refs):
    band, chunk_total, chunk_rows = shape
    pieces = len(candidates)
    total = pieces * band
    row_refs = refs[: sum(candidates)]
    columns = refs[len(row_refs) : len(row_refs) + band * chunk_total]
    out_ref, held, rows_held, wide_even, wide_odd, column_sems, row_sems = refs[-7:]
    wides = (wide_even, wide_odd)
    slice_width = held.shape[2]
    lane_tiles = slice_width // LANES
    stride = 2 * lane_tiles
    step = pl.program_id(0)
    piece, k = step // band, step % band

    def column_copy(source, slot, chunk):
        return pltpu.make_async_copy(
            source,
            held.at[slot, :, pl.ds(chunk * chunk_rows, chunk_rows)],
            column_sems.at[slot, chunk],
        )

    def row_copy(source, slot):
        return pltpu.make_async_copy(source, rows_held.at[slot], row_sems.at[slot])

    def fetch(wanted):
        first = sum(candidates[:wanted])
        for choice in range(candidates[wanted]):

            @pl.when(table_ref[pieces + wanted] == choice)
            def _():
                row_copy(row_refs[first + choice], wanted % 2).start()

    @pl.when(step == 0)
    def _():
        fetch(0)
        for slot in range(band):
            for chunk in range(chunk_total):
                column_copy(columns[slot * chunk_total + chunk], slot, chunk).start()

    @pl.when((k == 0) & (step < total))
    def _():
        row_copy(row_refs[0], piece % 2).wait()

    for following in range(1, pieces):

        @pl.when(step == (following - 1) * band)
        def _():
            fetch(following)

    @pl.when(step < band)
    def _():
        for chunk in range(chunk_total):
            column_copy(columns[chunk], k, chunk).wait()

    def lay_out(wide):
        out_ref[0] = wide[...].astype(out_ref.dtype)

    def multiply(wide):
        for f in range(2):
            rows = rows_held[piece % 2, f]
            for first in range(0, lane_tiles, 2):
                count = min(2, lane_tiles - first)
                part = held[k, f, pl.ds(first * LANES, count * LANES), :]
                product = lax.dot_general(
                    rows, part, CONTRACT_LAST, preferred_element_type=jnp.float32
                )
                product = product * scale
                for extra in range(count):
                    start = (first + extra) * 2 + f
                    wide[pl.ds(start, chunk_rows, stride=stride), :] = product[
                        :, extra * LANES : (extra + 1) * LANES
                    ]

    for parity in range(2):

        @pl.when((step % 2 == parity) & (step < total))
        def _():
            multiply(wides[parity])
            lay_out(wides[1 - parity])

    @pl.when(step == total)
    def _():
        lay_out(wides[(total - 1) % 2])


def factor_rows(pieces, columns, previous, slices, slice_width, scale):
    _, chunk_rows, tokens = pieces[0][0][0].shape
    dtype = pieces[0][0][0].dtype
    band = len(columns)
    chunk_total = len(columns[0])
    lane_tiles = slice_width // LANES
    height = chunk_rows * 2 * lane_tiles
    count = len(pieces)
    table = jnp.stack(
        [jnp.int32(position) for _, _, position in pieces]
        + [jnp.int32(choice) for _, choice, _ in pieces]
    )
    operands = [array for arrays, _, _ in pieces for array in arrays]
    operands += [part for parts in columns for part in parts]
    aliases = {}
    if previous is not None:
        aliases = {1 + len(operands): 0}
        operands.append(previous)

    def placed(step, table_ref):
        done = jnp.maximum(step - 1, 0)
        return done % band, table_ref[done // band], 0

    return pl.pallas_call(
        functools.partial(
            factor_kernel,
            (band, chunk_total, chunk_rows),
            tuple(len(arrays) for arrays, _, _ in pieces),
            scale,
        ),
        grid_spec=pltpu.PrefetchScalarGridSpec(
            num_scalar_prefetch=1,
            grid=(count * band + 1,),
            in_specs=[pl.BlockSpec(memory_space=pl.ANY)] * len(operands),
            out_specs=pl.BlockSpec((1, height, LANES), placed),
            scratch_shapes=[
                pltpu.VMEM((band, 2, slice_width, tokens), dtype),
                pltpu.VMEM((2, 2, chunk_rows, tokens), dtype),
                pltpu.VMEM((height, LANES), jnp.float32),
                pltpu.VMEM((height, LANES), jnp.float32),
                pltpu.SemaphoreType.DMA((band, chunk_total)),
                pltpu.SemaphoreType.DMA((2,)),
            ],
        ),
        out_shape=jax.ShapeDtypeStruct((band, slices * chunk_total * height, LANES), dtype),
        input_output_aliases=aliases,
        compiler_params=pltpu.CompilerParams(
            dimension_semantics=("arbitrary",), vmem_limit_bytes=48 * 2**20
        ),
        cost_estimate=pl.CostEstimate(
            flops=4 * count * chunk_rows * tokens * band * slice_width,
            bytes_accessed=4 * count * chunk_rows * (tokens + band * slice_width)
            + 4 * band * slice_width * tokens,
            transcendentals=0,
        ),
    )(table, *operands)


def tie(*arrays):
    return lax.optimization_barrier(arrays)


def arrivals(groups, d):
    found = []
    for hops in range(1, groups):
        if d + hops < groups:
            found.append((hops, False))
        if d - hops >= 0:
            found.append((hops, True))
    return found


def per_device(cotangent, down_weight, gate_pre, up_pre):
    blocks = lax.axis_size("tensor")
    groups = lax.axis_size("dp")
    own_block = lax.axis_index("tensor")
    own_group = lax.axis_index("dp")
    per_group = blocks // groups
    local_tokens, block_width = gate_pre.shape
    local_features = cotangent.shape[1]
    slice_width = block_width // groups
    all_tokens = local_tokens * groups
    half_band = blocks // 2
    chunk_rows = slice_width // CHUNKS

    to_plane = [
        ((m * per_group + q) * groups + g, (q * groups + g) * groups + m)
        for m in range(groups)
        for q in range(per_group)
        for g in range(groups)
    ]
    sent = lax.ppermute(cotangent, ("tensor", "dp"), to_plane)
    sent, gate_pre, up_pre = tie(sent, gate_pre, up_pre)
    features = lax.all_gather(sent, "tensor", axis=0, tiled=True)

    saved = jnp.stack([gate_pre, up_pre])

    def saved_slice(index):
        return lax.dynamic_slice_in_dim(saved, (index % groups) * slice_width, slice_width, 2)

    pieces = [saved_slice(own_group)]
    for shift in range(1, groups):
        ring = [(d, (d + shift) % groups) for d in range(groups)]
        pieces.append(lax.ppermute(saved_slice(own_group + shift), "dp", ring))
    features, pieces[1], pieces[-1] = tie(features, pieces[1], pieces[-1])
    features = features.reshape(per_group, all_tokens, local_features)

    weight = down_weight.reshape(groups, slice_width, -1)

    def partial_products(chunk, features):
        part = weight[:, chunk * chunk_rows : (chunk + 1) * chunk_rows]
        part = part.reshape(groups * chunk_rows, per_group, local_features)
        return lax.dot_general(
            part,
            features,
            (((1, 2), (0, 2)), ((), ())),
            preferred_element_type=jnp.float32,
        ).reshape(groups, chunk_rows, all_tokens)

    def slot(partial, offset):
        return lax.dynamic_index_in_dim(partial, (own_group + offset) % groups, 0, keepdims=False)

    def reduce_step(partial, step, received):
        right, left = slot(partial, groups - step), slot(partial, step)
        if received is not None:
            right = right + received[0].astype(jnp.float32)
            left = left + received[1].astype(jnp.float32)
        return (
            lax.ppermute(right.astype(jnp.bfloat16), "dp", [(d, d + 1) for d in range(step)]),
            lax.ppermute(
                left.astype(jnp.bfloat16),
                "dp",
                [(d, d - 1) for d in range(groups - step, groups)],
            ),
        )

    def order_saved(pieces):
        pieces = jnp.stack(pieces)
        return jnp.concatenate(
            [
                lax.dynamic_index_in_dim(pieces, (own_group - h) % groups, 0, keepdims=False)
                for h in range(groups)
            ],
            axis=1,
        ).transpose(0, 2, 1)

    def gradients(partial, received, saved_all, chunk):
        hidden_cot = (
            slot(partial, 0) + received[0].astype(jnp.float32) + received[1].astype(jnp.float32)
        )
        local = saved_all[:, chunk * chunk_rows : (chunk + 1) * chunk_rows].astype(jnp.float32)
        gate_value, up_value = local[0], local[1]
        sigmoid_gate = jax.nn.sigmoid(gate_value)
        grad_gate = hidden_cot * up_value * sigmoid_gate * (1.0 + gate_value * (1.0 - sigmoid_gate))
        grad_up = hidden_cot * gate_value * sigmoid_gate
        return jnp.stack([grad_gate.astype(jnp.bfloat16), grad_up.astype(jnp.bfloat16)])

    def gather_step(step, left, right):
        return (
            lax.ppermute(left, "dp", [(d, d + 1) for d in range(step - 1, groups - 1)]),
            lax.ppermute(right, "dp", [(d, d - 1) for d in range(1, groups - step + 1)]),
        )

    shifts = list(range(half_band, 0, -2))
    turns = max(groups - 2, 1)

    def partner_step(step, found):
        if step <= turns:
            for k in shifts[step - 1 :: turns]:
                found[k] = lax.ppermute(
                    found[0], "tensor", [(t, (t + k) % blocks) for t in range(blocks)]
                )
        if step == groups - 1:
            swap = [(t, t ^ 1) for t in range(blocks)]
            odd = own_block % 2 == 1
            for k in range(1, half_band, 2):
                found[k] = lax.ppermute(jnp.where(odd, found[k + 1], found[k - 1]), "tensor", swap)

    partial = partial_products(0, features)
    received = reduce_step(partial, 1, None)
    received = tie(*received, *pieces)
    received, pieces = received[:2], received[2:]
    saved_all = order_saved(pieces)
    for step in range(2, groups):
        received = reduce_step(partial, step, received)
    rows, columns = [], []
    for chunk in range(CHUNKS):
        own = gradients(partial, received, saved_all, chunk)
        own, features = tie(own, features)
        later = chunk + 1 < CHUNKS
        if later:
            partial = partial_products(chunk + 1, features)
        found = {0: own}
        held = {}
        left = right = own
        received = None
        for step in range(1, groups):
            if later and step > 1:
                received = reduce_step(partial, step - 1, received)
            left, right = gather_step(step, left, right)
            partner_step(step, found)
            if later or step < groups - 1:
                keys = [k for k in found if k]
                moved = tie(left, right, *[found[k] for k in keys], *(received or ()))
                left, right = moved[:2]
                for place, k in enumerate(keys):
                    found[k] = moved[2 + place]
                if received is not None:
                    received = moved[-2:]
            held[step] = (right, left)
        if later:
            received = reduce_step(partial, groups - 1, received)
        rows.append((own, held))
        columns.append([found[k] for k in range(half_band + 1)])
    columns = [[columns[c][k] for c in range(CHUNKS)] for k in range(half_band + 1)]
    inverse_count = 1.0 / all_tokens

    if slice_width % LANES == 0 and chunk_rows % 16 == 0:
        order = [arrivals(groups, d) for d in range(groups)]

        def by_plane(values):
            return jnp.asarray(values, jnp.int32)[own_group]

        def row_piece(chunk, place):
            own, held = rows[chunk]
            if place == 0:
                return [own], 0, own_group * CHUNKS + chunk
            wanted = [order[d][place - 1] for d in range(groups)]
            kinds = sorted(set(wanted))
            origin = [d - hops if left else d + hops for d, (hops, left) in enumerate(wanted)]
            return (
                [held[hops][int(left)] for hops, left in kinds],
                by_plane([kinds.index(kind) for kind in wanted]),
                by_plane(origin) * CHUNKS + chunk,
            )

        pieces = [row_piece(chunk, place) for chunk in range(CHUNKS) for place in range(groups)]
        early = len(pieces) - groups // 2
        result = factor_rows(
            pieces[:early], columns, None, groups, slice_width, inverse_count
        )
        result = factor_rows(
            pieces[early:], columns, result, groups, slice_width, inverse_count
        )
        result = result.reshape(half_band + 1, -1, 2, LANES).transpose(2, 0, 1, 3)
    else:

        def in_order(own, held):
            turned = [own]
            for offset in range(1, groups):
                from_right = own_group + offset < groups
                turned.append(jnp.where(from_right, held[offset][0], held[groups - offset][1]))
            return jnp.roll(jnp.stack(turned), own_group, axis=0)

        all_rows = jnp.concatenate([in_order(*pair) for pair in rows], axis=2)
        all_columns = jnp.stack([jnp.concatenate(parts, axis=1) for parts in columns])
        result = jnp.einsum(
            "sfrt,kfct->fksrc", all_rows, all_columns, preferred_element_type=jnp.float32
        )
        result = (result * inverse_count).astype(jnp.bfloat16)
    return result.reshape(1, 2, half_band + 1, 1, block_width * slice_width)


def solution(mesh):
    placed = (P("dp", "tensor"), P("tensor", "dp"), P("dp", "tensor"), P("dp", "tensor"))
    return jax.shard_map(
        per_device,
        mesh=mesh,
        in_specs=placed,
        out_specs=P("tensor", None, None, "dp", None),
        check_vma=False,
    )
```

time: 751 us -> 675 us (0.90)
  waiting for transfers between devices: 417 us -> 274 us
  local copies, waits for them, and re-layouts: 41.3 us -> 77.9 us
  starting transfers between devices: 123 us -> 139 us
  Pallas kernels: 97.4 us -> 107 us
    ppermute x3, waiting for transfers between devices: 72 us -> 6.36 us  [per_device(): pieces.append(lax.ppermute(saved_slice(own_group + shift), 'dp', ring))]
    ppermute x21 -> x33, waiting for transfers between devices: 307 us -> 268 us  [the longest x4 121 us: partner_step(): lax.ppermute(found[0], 'tensor', [(t, (t + k) % blocks) for t in range(bl...]
    all_gather x1, waiting for transfers between devices: 37.8 us -> 0.01 us  [per_device(): features = lax.all_gather(sent, 'tensor', axis=0, tiled=True)]
    ppermute x21 -> x33, starting transfers between devices: 101 us -> 119 us  [the longest x6 54.2 us: reduce_step(): lax.ppermute(left.astype(jnp.bfloat16), 'dp', [(d, d - 1) for d in range(...]
    dot_general x0 -> x2, local copies, waits for them, and re-layouts: none -> 16.8 us  [partial_products(): lax.dot_general(part, features, (((1, 2), (0, 2)), ((), ())), preferred_e...]
    slice x0 -> x1, local copies, waits for them, and re-layouts: none -> 11.1 us  [partial_products(): part = weight[:, chunk * chunk_rows:(chunk + 1) * chunk_rows]]
    pallas_call x2, Pallas kernels: 97.4 us -> 107 us  [factor_rows(): pl.pallas_call(functools.partial(factor_kernel, (band, chunk_total, chunk...]
    reshape x3 -> x2, local copies, waits for them, and re-layouts: 25.8 us -> 25.9 us  [partial_products(): part = part.reshape(groups * chunk_rows, per_group, local_features)]
  transfers between devices with their start and end apart: 27 -> 37, of which waited for: 13 -> 12; matrix products, arithmetic and copies ran while one was open for 6% -> 17% of each run, Pallas kernels for 7% -> 11%
where the time goes in v2:
time: 675 us; the launch traced here: 674 us
  waiting for transfers between devices  274 us (41%)
  starting transfers between devices  139 us (21%)
  Pallas kernels  107 us (16%)
  local copies, waits for them, and re-layouts  77.9 us (12%)
  other arithmetic  32.2 us (5%)
  matrix products  27.5 us (4%)
  between operations  15.7 us (2%)
    ppermute x4, waiting for transfers between devices, partner_step(): lax.ppermute(found[0], 'tensor', [(t, (t + k) % blocks) for t in range(bl...  121 us
    pallas_call x2, Pallas kernels, factor_rows(): pl.pallas_call(functools.partial(factor_kernel, (band, chunk_total, chunk...  107 us
    ppermute x6, waiting for transfers between devices, gather_step(): lax.ppermute(left, 'dp', [(d, d + 1) for d in range(step - 1, groups - 1)])  58.6 us
    ppermute x6, starting transfers between devices, reduce_step(): lax.ppermute(left.astype(jnp.bfloat16), 'dp', [(d, d - 1) for d in range(...  54.2 us
    ppermute x6, waiting for transfers between devices, reduce_step(): lax.ppermute(left.astype(jnp.bfloat16), 'dp', [(d, d - 1) for d in range(...  51.8 us
    dot_general x2, matrix products, partial_products(): lax.dot_general(part, features, (((1, 2), (0, 2)), ((), ())), preferred_e...  27.5 us
    reshape x2, local copies, waits for them, and re-layouts, partial_products(): part = part.reshape(groups * chunk_rows, per_group, local_features)  25.9 us
    ppermute x1, waiting for transfers between devices, per_device(): sent = lax.ppermute(cotangent, ('tensor', 'dp'), to_plane)  25.4 us
  transfers between devices with their start and end apart: 37, of which 12 were waited for; matrix products, arithmetic and copies ran while one was open for 17% of the time, Pallas kernels for 11%

profile of v2, /device:TPU:29, one launch (start us, length us, event | category | flops | bytes accessed | tf_op | source)
XLA Modules:
  0.0 673.7 jit_solution(15226996616708289744)
XLA Ops:
  9.5 25.4 %collective-permute-done = bf16[256,1024]{1,0:T(8,128)(2,1)S(1)} collective-permute-done((bf16[256,1024]{1,0:T(8,128)(2,1)}, bf16[256,1024]{1,0:T(8,128)(2,1)S(1)}, u32[]{:S(2)}, u32[]{:S(2)}) %collective-permute-start) | collective-permute-done | bytes 524320 | tf_op jit(solution)/shard_map/ppermute | solution.py:190
  39.5 20.2 %collective-permute-start.1 = (bf16[2,256,896]{2,1,0:T(8,128)(2,1)}, bf16[2,256,896]{2,1,0:T(8,128)(2,1)S(1)}, u32[]{:S(2)}, u32[]{:S(2)}) collective-permute-start(bf16[2,256,896]{2,1,0:T(8,128)(2,1)} %get-tuple-element.106), channel_id=1, source_target_pairs={{0,1},{1,2},{2,3},{3,0},{4,5},{5,6},{6,7},{7,4},{8,9},{9,10},{10,1... | collective-permute-start | bytes 2752520 | tf_op jit(solution)/shard_map/ppermute | solution.py:202
  59.7 11.1 %fusion.36 = (bf16[4,448,2048]{2,1,0:T(8,128)(2,1)}, bf16[4,448,2048]{2,1,0:T(8,128)(2,1)}) fusion(bf16[4,896,2048]{2,1,0:T(8,128)(2,1)} %bitcast.146), kind=kLoop, calls=%fused_computation.77 | loop fusion | bytes 29360128 | tf_op jit(solution)/shard_map/slice | solution.py:209
  70.8 13.1 %reshape.50 = bf16[1792,2,1024]{2,1,0:T(2,128)(2,1)} reshape(bf16[4,448,2048]{2,1,0:T(8,128)(2,1)} %get-tuple-element.84) | data formatting | bytes 14680064 | tf_op jit(solution)/shard_map/reshape | solution.py:210
  84.1 6.4 collective-permute-done.2
  90.4 13.7 %fusion.4 = f32[1792,1024]{0,1:T(8,128)} fusion(bf16[2,1024,1024]{2,1,0:T(8,128)(2,1)} %bitcast.156, bf16[1792,2,1024]{2,1,0:T(2,128)(2,1)} %reshape.50), kind=kOutput, calls=%fused_computation.12 | convolution fusion | flops 7516192768 | bytes 18874368 | tf_op jit(solution)/shard_map/dot_general | solution.py:211
  104.2 8.4 %copy.32 = f32[1792,1024]{1,0:T(8,128)} copy(f32[1792,1024]{0,1:T(8,128)} %fusion.4) | data formatting | bytes 14680064 | tf_op jit(solution)/shard_map/dot_general | solution.py:211
  116.1 4.3 collective-permute-start.4
  122.1 16.6 %collective-permute-done.4 = bf16[448,1024]{1,0:T(8,128)(2,1)} collective-permute-done((bf16[448,1024]{1,0:T(8,128)(2,1)}, bf16[448,1024]{1,0:T(8,128)(2,1)}, u32[]{:S(2)}, u32[]{:S(2)}) %collective-permute-start.4) | collective-permute-done | bytes 917536 | tf_op jit(solution)/shard_map/ppermute | solution.py:228
  141.5 4.2 fusion.26
  145.7 27.8 %collective-permute-start.8 = (bf16[448,1024]{1,0:T(8,128)(2,1)}, bf16[448,1024]{1,0:T(8,128)(2,1)}, u32[]{:S(2)}, u32[]{:S(2)}) collective-permute-start(bf16[448,1024]{1,0:T(8,128)(2,1)} %get-tuple-element.96), channel_id=1, source_target_pairs={{2,1},{3,2},{6,5},{7,6},{10,9},{11,10},{14,13},{15,14},{18,17},{19... | collective-permute-start | bytes 2752520 | tf_op jit(solution)/shard_map/ppermute | solution.py:228
  176.4 15.1 %collective-permute-done.8 = bf16[448,1024]{1,0:T(8,128)(2,1)} collective-permute-done((bf16[448,1024]{1,0:T(8,128)(2,1)}, bf16[448,1024]{1,0:T(8,128)(2,1)}, u32[]{:S(2)}, u32[]{:S(2)}) %collective-permute-start.8) | collective-permute-done | bytes 917536 | tf_op jit(solution)/shard_map/ppermute | solution.py:228
  194.6 5.0 collective-permute-start.9
  210.1 6.7 collective-permute-done.9
  220.2 11.6 %collective-permute-start.12 = (bf16[2,448,1024]{2,1,0:T(8,128)(2,1)S(1)}, bf16[2,448,1024]{2,1,0:T(8,128)(2,1)}, u32[]{:S(2)}, u32[]{:S(2)}) collective-permute-start(bf16[2,448,1024]{2,1,0:T(8,128)(2,1)S(1)} %pad_maximum_fusion.1.refs_0_.refs_13_.refs_7_), channel_id=1, source_target_pairs={{0,16},{4,20},{8,24},{12,28},{16,0},{20,4},{24,8},{28,12},{1,17},{... | collective-permute-start | bytes 5505032 | tf_op jit(solution)/shard_map/ppermute | solution.py:268
  231.8 5.4 collective-permute-start.11
  238.7 12.8 %reshape.52 = bf16[1792,2,1024]{2,1,0:T(2,128)(2,1)} reshape(bf16[4,448,2048]{2,1,0:T(8,128)(2,1)} %get-tuple-element.83) | data formatting | bytes 14680064 | tf_op jit(solution)/shard_map/reshape | solution.py:210
  255.3 51.4 %collective-permute-done.12.refs_21_.refs_15_ = bf16[2,448,1024]{2,1,0:T(8,128)(2,1)} collective-permute-done((bf16[2,448,1024]{2,1,0:T(8,128)(2,1)S(1)}, bf16[2,448,1024]{2,1,0:T(8,128)(2,1)}, u32[]{:S(2)}, u32[]{:S(2)}) %collective-permute-start.12) | collective-permute-done | bytes 1835040 | tf_op jit(solution)/shard_map/ppermute | solution.py:268
  309.9 13.7 %fusion.7 = f32[1792,1024]{0,1:T(8,128)} fusion(bf16[2,1024,1024]{2,1,0:T(8,128)(2,1)} %bitcast.157, bf16[1792,2,1024]{2,1,0:T(2,128)(2,1)} %reshape.52), kind=kOutput, calls=%fused_computation.13 | convolution fusion | flops 7516192768 | bytes 18874368 | tf_op jit(solution)/shard_map/dot_general | solution.py:211
  323.7 8.4 %copy.38 = f32[1792,1024]{1,0:T(8,128)} copy(f32[1792,1024]{0,1:T(8,128)} %fusion.7) | data formatting | bytes 14680064 | tf_op jit(solution)/shard_map/dot_general | solution.py:211
  335.6 8.7 %collective-permute-start.17 = (bf16[448,1024]{1,0:T(8,128)(2,1)}, bf16[448,1024]{1,0:T(8,128)(2,1)S(1)}, u32[]{:S(2)}, u32[]{:S(2)}) collective-permute-start(bf16[448,1024]{1,0:T(8,128)(2,1)} %get-tuple-element.93), channel_id=1, source_target_pairs={{3,2},{7,6},{11,10},{15,14},{19,18},{23,22},{27,26},{31,30}} | collective-permute-start | bytes 2752520 | tf_op jit(solution)/shard_map/ppermute | solution.py:228
  345.9 12.2 %collective-permute-done.17 = bf16[448,1024]{1,0:T(8,128)(2,1)S(1)} collective-permute-done((bf16[448,1024]{1,0:T(8,128)(2,1)}, bf16[448,1024]{1,0:T(8,128)(2,1)S(1)}, u32[]{:S(2)}, u32[]{:S(2)}) %collective-permute-start.17) | collective-permute-done | bytes 917536 | tf_op jit(solution)/shard_map/ppermute | solution.py:228
  360.6 4.3 collective-permute-start.23
  369.3 6.8 %collective-permute-start.21 = (bf16[2,448,1024]{2,1,0:T(8,128)(2,1)S(1)}, bf16[2,448,1024]{2,1,0:T(8,128)(2,1)S(1)}, u32[]{:S(2)}, u32[]{:S(2)}) collective-permute-start(bf16[2,448,1024]{2,1,0:T(8,128)(2,1)S(1)} %get-tuple-element.111), channel_id=1, source_target_pairs={{0,4},{4,0},{8,12},{12,8},{16,20},{20,16},{24,28},{28,24},{1,5},{5... | collective-permute-start | bytes 5505032 | tf_op jit(solution)/shard_map/ppermute | solution.py:275
  378.1 23.0 %collective-permute-done.18.refs_9_ = bf16[2,448,1024]{2,1,0:T(8,128)(2,1)S(1)} collective-permute-done((bf16[2,448,1024]{2,1,0:T(8,128)(2,1)}, bf16[2,448,1024]{2,1,0:T(8,128)(2,1)S(1)}, u32[]{:S(2)}, u32[]{:S(2)}) %collective-permute-start.18) | collective-permute-done | bytes 1835040 | tf_op jit(solution)/shard_map/ppermute | solution.py:258
  404.8 4.0 collective-permute-start.25
  408.9 11.1 %collective-permute-done.24 = bf16[448,1024]{1,0:T(8,128)(2,1)S(1)} collective-permute-done((bf16[448,1024]{1,0:T(8,128)(2,1)S(1)}, bf16[448,1024]{1,0:T(8,128)(2,1)S(1)}, u32[]{:S(2)}, u32[]{:S(2)}) %collective-permute-start.24) | collective-permute-done | bytes 917536 | tf_op jit(solution)/shard_map/ppermute | solution.py:227
  426.8 69.6 %collective-permute-done.28.refs_22_.refs_16_ = bf16[2,448,1024]{2,1,0:T(8,128)(2,1)S(1)} collective-permute-done((bf16[2,448,1024]{2,1,0:T(8,128)(2,1)S(1)}, bf16[2,448,1024]{2,1,0:T(8,128)(2,1)S(1)}, u32[]{:S(2)}, u32[]{:S(2)}) %collective-permute-start.28) | collective-permute-done | bytes 1835040 | tf_op jit(solution)/shard_map/ppermute | solution.py:268
  500.1 35.6 %collective-permute-done.29.refs_2_.refs_4_ = bf16[2,448,1024]{2,1,0:T(8,128)(2,1)} collective-permute-done((bf16[2,448,1024]{2,1,0:T(8,128)(2,1)S(1)}, bf16[2,448,1024]{2,1,0:T(8,128)(2,1)}, u32[]{:S(2)}, u32[]{:S(2)}) %collective-permute-start.29) | collective-permute-done | bytes 1835040 | tf_op jit(solution)/shard_map/ppermute | solution.py:258
  537.9 8.2 %collective-permute-start.35 = (bf16[2,448,1024]{2,1,0:T(8,128)(2,1)}, bf16[2,448,1024]{2,1,0:T(8,128)(2,1)}, u32[]{:S(2)}, u32[]{:S(2)}) collective-permute-start(bf16[2,448,1024]{2,1,0:T(8,128)(2,1)} %get-tuple-element.109), channel_id=1, source_target_pairs={{0,4},{4,0},{8,12},{12,8},{16,20},{20,16},{24,28},{28,24},{1,5},{5... | collective-permute-start | bytes 5505032 | tf_op jit(solution)/shard_map/ppermute | solution.py:275
  557.5 74.4 %shard_map.154.refs_17_ = bf16[5,50176,128]{2,1,0:T(8,128)(2,1)} custom-call(s32[12]{0:T(128)S(1)} %stack.77.table_ref, bf16[2,448,1024]{2,1,0:T(8,128)(2,1)S(1)} %pad_maximum_fusion.1.refs_0_.refs_13_.refs_7_, bf16[2,448,1024]{2,1,0:T(8,128)(2,1)} %collective-permute-done.11.refs_1_, bf16[2,448,1024]{2,1,0:T(8,128)(2,1)} %collective-permute-done.10.refs_2_.refs_3_, ...), custom_call_target="tpu_custom_call" | custom-call | flops 49325015040 | bytes 77529088 | tf_op jit(solution)/shard_map/pallas_call | solution.py:122
  634.4 32.4 %shard_map.155 = bf16[5,50176,128]{2,1,0:T(8,128)(2,1)} custom-call(s32[4]{0:T(128)S(1)} %pad_add_fusion.table_ref, bf16[2,448,1024]{2,1,0:T(8,128)(2,1)S(1)} %copy-done.2, bf16[2,448,1024]{2,1,0:T(8,128)(2,1)} %collective-permute-done.30.refs_1_.refs_3_, ...), custom_call_target="tpu_custom_call", output_to_operand_aliasing={{}: (18, {})} | custom-call | flops 16441671680 | bytes 38076416 | tf_op jit(solution)/shard_map/pallas_call | solution.py:122
  (127 shorter events, 86.3 us)
Async XLA Ops:
  6.5 83.9 %all-gather.2.cloned.1.call-start = ((), (), s32[]{:S(2)}) async-start(), calls=%async_computation | async-start | bytes 4718592 | tf_op jit(solution)/shard_map/all_gather | solution.py:192
  6.5 28.4 %collective-permute-start = (bf16[256,1024]{1,0:T(8,128)(2,1)}, bf16[256,1024]{1,0:T(8,128)(2,1)S(1)}, u32[]{:S(2)}, u32[]{:S(2)}) collective-permute-start(bf16[256,1024]{1,0:T(8,128)(2,1)} %param.16), channel_id=1, source_target_pairs={{0,0},{1,4},{2,8},{3,12},{4,16},{5,20},{6,24},{7,28},{8,1},{9,5},{... | collective-permute-start | bytes 1572872 | tf_op jit(solution)/shard_map/ppermute | solution.py:190
  39.5 44.6 %collective-permute-start.1 = (bf16[2,256,896]{2,1,0:T(8,128)(2,1)}, bf16[2,256,896]{2,1,0:T(8,128)(2,1)S(1)}, u32[]{:S(2)}, u32[]{:S(2)}) collective-permute-start(bf16[2,256,896]{2,1,0:T(8,128)(2,1)} %get-tuple-element.106), channel_id=1, source_target_pairs={{0,1},{1,2},{2,3},{3,0},{4,5},{5,6},{6,7},{7,4},{8,9},{9,10},{10,1... | collective-permute-start | bytes 2752520 | tf_op jit(solution)/shard_map/ppermute | solution.py:202
  59.7 30.8 %collective-permute-start.2 = (bf16[2,256,896]{2,1,0:T(8,128)(2,1)}, bf16[2,256,896]{2,1,0:T(8,128)(2,1)S(1)}, u32[]{:S(2)}, u32[]{:S(2)}) collective-permute-start(bf16[2,256,896]{2,1,0:T(8,128)(2,1)} %get-tuple-element.107), channel_id=1, source_target_pairs={{0,3},{1,0},{2,1},{3,2},{4,7},{5,4},{6,5},{7,6},{8,11},{9,8},{10,9... | collective-permute-start | bytes 2752520 | tf_op jit(solution)/shard_map/ppermute | solution.py:202
  83.8 38.3 %collective-permute-start.5 = (bf16[2,256,896]{2,1,0:T(8,128)(2,1)}, bf16[2,256,896]{2,1,0:T(8,128)(2,1)}, u32[]{:S(2)}, u32[]{:S(2)}) collective-permute-start(bf16[2,256,896]{2,1,0:T(8,128)(2,1)} %get-tuple-element.105), channel_id=1, source_target_pairs={{0,2},{1,3},{2,0},{3,1},{4,6},{5,7},{6,4},{7,5},{8,10},{9,11},{10,... | collective-permute-start | bytes 2752520 | tf_op jit(solution)/shard_map/ppermute | solution.py:202
  116.1 22.5 %collective-permute-start.4 = (bf16[448,1024]{1,0:T(8,128)(2,1)}, bf16[448,1024]{1,0:T(8,128)(2,1)}, u32[]{:S(2)}, u32[]{:S(2)}) collective-permute-start(bf16[448,1024]{1,0:T(8,128)(2,1)} %get-tuple-element.97), channel_id=1, source_target_pairs={{3,2},{7,6},{11,10},{15,14},{19,18},{23,22},{27,26},{31,30}} | collective-permute-start | bytes 2752520 | tf_op jit(solution)/shard_map/ppermute | solution.py:228
  120.4 18.3 %collective-permute-start.3 = (bf16[448,1024]{1,0:T(8,128)(2,1)}, bf16[448,1024]{1,0:T(8,128)(2,1)}, u32[]{:S(2)}, u32[]{:S(2)}) collective-permute-start(bf16[448,1024]{1,0:T(8,128)(2,1)} %get-tuple-element.98), channel_id=1, source_target_pairs={{0,1},{4,5},{8,9},{12,13},{16,17},{20,21},{24,25},{28,29}} | collective-permute-start | bytes 2752520 | tf_op jit(solution)/shard_map/ppermute | solution.py:227
  145.7 45.9 %collective-permute-start.8 = (bf16[448,1024]{1,0:T(8,128)(2,1)}, bf16[448,1024]{1,0:T(8,128)(2,1)}, u32[]{:S(2)}, u32[]{:S(2)}) collective-permute-start(bf16[448,1024]{1,0:T(8,128)(2,1)} %get-tuple-element.96), channel_id=1, source_target_pairs={{2,1},{3,2},{6,5},{7,6},{10,9},{11,10},{14,13},{15,14},{18,17},{19... | collective-permute-start | bytes 2752520 | tf_op jit(solution)/shard_map/ppermute | solution.py:228
  175.1 35.0 %collective-permute-start.7 = (bf16[448,1024]{1,0:T(8,128)(2,1)}, bf16[448,1024]{1,0:T(8,128)(2,1)}, u32[]{:S(2)}, u32[]{:S(2)}) collective-permute-start(bf16[448,1024]{1,0:T(8,128)(2,1)} %get-tuple-element.95), channel_id=1, source_target_pairs={{0,1},{1,2},{2,3},{4,5},{5,6},{6,7},{8,9},{9,10},{10,11},{12,13},{... | collective-permute-start | bytes 2752520 | tf_op jit(solution)/shard_map/ppermute | solution.py:227
  194.6 22.2 %collective-permute-start.9 = (bf16[448,1024]{1,0:T(8,128)(2,1)}, bf16[448,1024]{1,0:T(8,128)(2,1)}, u32[]{:S(2)}, u32[]{:S(2)}) collective-permute-start(bf16[448,1024]{1,0:T(8,128)(2,1)} %fusion.23), channel_id=1, source_target_pairs={{1,0},{2,1},{3,2},{5,4},{6,5},{7,6},{9,8},{10,9},{11,10},{13,12},{... | collective-permute-start | bytes 2752520 | tf_op jit(solution)/shard_map/ppermute | solution.py:228
  220.2 86.4 %collective-permute-start.12 = (bf16[2,448,1024]{2,1,0:T(8,128)(2,1)S(1)}, bf16[2,448,1024]{2,1,0:T(8,128)(2,1)}, u32[]{:S(2)}, u32[]{:S(2)}) collective-permute-start(bf16[2,448,1024]{2,1,0:T(8,128)(2,1)S(1)} %pad_maximum_fusion.1.refs_0_.refs_13_.refs_7_), channel_id=1, source_target_pairs={{0,16},{4,20},{8,24},{12,28},{16,0},{20,4},{24,8},{28,12},{1,17},{... | collective-permute-start | bytes 5505032 | tf_op jit(solution)/shard_map/ppermute | solution.py:268
  231.8 74.8 %collective-permute-start.11 = (bf16[2,448,1024]{2,1,0:T(8,128)(2,1)S(1)}, bf16[2,448,1024]{2,1,0:T(8,128)(2,1)}, u32[]{:S(2)}, u32[]{:S(2)}) collective-permute-start(bf16[2,448,1024]{2,1,0:T(8,128)(2,1)S(1)} %pad_maximum_fusion.1.refs_0_.refs_13_.refs_7_), channel_id=1, source_target_pairs={{1,0},{2,1},{3,2},{5,4},{6,5},{7,6},{9,8},{10,9},{11,10},{13,12},{... | collective-permute-start | bytes 5505032 | tf_op jit(solution)/shard_map/ppermute | solution.py:259
  237.2 69.4 %collective-permute-start.10 = (bf16[2,448,1024]{2,1,0:T(8,128)(2,1)S(1)}, bf16[2,448,1024]{2,1,0:T(8,128)(2,1)}, u32[]{:S(2)}, u32[]{:S(2)}) collective-permute-start(bf16[2,448,1024]{2,1,0:T(8,128)(2,1)S(1)} %pad_maximum_fusion.1.refs_0_.refs_13_.refs_7_), channel_id=1, source_target_pairs={{0,1},{1,2},{2,3},{4,5},{5,6},{6,7},{8,9},{9,10},{10,11},{12,13},{... | collective-permute-start | bytes 5505032 | tf_op jit(solution)/shard_map/ppermute | solution.py:258
  251.5 106.6 %collective-permute-start.15 = (bf16[2,448,1024]{2,1,0:T(8,128)(2,1)S(1)}, bf16[2,448,1024]{2,1,0:T(8,128)(2,1)}, u32[]{:S(2)}, u32[]{:S(2)}) collective-permute-start(bf16[2,448,1024]{2,1,0:T(8,128)(2,1)S(1)} %pad_maximum_fusion.1.refs_0_.refs_13_.refs_7_), channel_id=1, source_target_pairs={{0,8},{4,12},{8,16},{12,20},{16,24},{20,28},{24,0},{28,4},{1,9},{5... | collective-permute-start | bytes 5505032 | tf_op jit(solution)/shard_map/ppermute | solution.py:268
  306.7 51.4 %collective-permute-start.13 = (bf16[2,448,1024]{2,1,0:T(8,128)(2,1)}, bf16[2,448,1024]{2,1,0:T(8,128)(2,1)}, u32[]{:S(2)}, u32[]{:S(2)}) collective-permute-start(bf16[2,448,1024]{2,1,0:T(8,128)(2,1)} %collective-permute-done.10.refs_2_.refs_3_), channel_id=1, source_target_pairs={{1,2},{2,3},{5,6},{6,7},{9,10},{10,11},{13,14},{14,15},{17,18},{18... | collective-permute-start | bytes 5505032 | tf_op jit(solution)/shard_map/ppermute | solution.py:258
  308.0 50.1 %collective-permute-start.14 = (bf16[2,448,1024]{2,1,0:T(8,128)(2,1)}, bf16[2,448,1024]{2,1,0:T(8,128)(2,1)}, u32[]{:S(2)}, u32[]{:S(2)}) collective-permute-start(bf16[2,448,1024]{2,1,0:T(8,128)(2,1)} %collective-permute-done.11.refs_1_), channel_id=1, source_target_pairs={{1,0},{2,1},{5,4},{6,5},{9,8},{10,9},{13,12},{14,13},{17,16},{18,1... | collective-permute-start | bytes 5505032 | tf_op jit(solution)/shard_map/ppermute | solution.py:259
  335.6 22.5 %collective-permute-start.17 = (bf16[448,1024]{1,0:T(8,128)(2,1)}, bf16[448,1024]{1,0:T(8,128)(2,1)S(1)}, u32[]{:S(2)}, u32[]{:S(2)}) collective-permute-start(bf16[448,1024]{1,0:T(8,128)(2,1)} %get-tuple-element.93), channel_id=1, source_target_pairs={{3,2},{7,6},{11,10},{15,14},{19,18},{23,22},{27,26},{31,30}} | collective-permute-start | bytes 2752520 | tf_op jit(solution)/shard_map/ppermute | solution.py:228
  360.6 16.9 %collective-permute-start.23 = (bf16[448,1024]{1,0:T(8,128)(2,1)S(1)}, bf16[448,1024]{1,0:T(8,128)(2,1)S(1)}, u32[]{:S(2)}, u32[]{:S(2)}) collective-permute-start(bf16[448,1024]{1,0:T(8,128)(2,1)S(1)} %get-tuple-element.91), channel_id=1, source_target_pairs={{2,1},{3,2},{6,5},{7,6},{10,9},{11,10},{14,13},{15,14},{18,17},{19... | collective-permute-start | bytes 2752520 | tf_op jit(solution)/shard_map/ppermute | solution.py:228
  364.9 36.3 %collective-permute-start.18 = (bf16[2,448,1024]{2,1,0:T(8,128)(2,1)}, bf16[2,448,1024]{2,1,0:T(8,128)(2,1)S(1)}, u32[]{:S(2)}, u32[]{:S(2)}) collective-permute-start(bf16[2,448,1024]{2,1,0:T(8,128)(2,1)} %collective-permute-done.13.refs_5_.refs_7_), channel_id=1, source_target_pairs={{2,3},{6,7},{10,11},{14,15},{18,19},{22,23},{26,27},{30,31}} | collective-permute-start | bytes 5505032 | tf_op jit(solution)/shard_map/ppermute | solution.py:258
  366.2 35.0 %collective-permute-start.19 = (bf16[2,448,1024]{2,1,0:T(8,128)(2,1)}, bf16[2,448,1024]{2,1,0:T(8,128)(2,1)S(1)}, u32[]{:S(2)}, u32[]{:S(2)}) collective-permute-start(bf16[2,448,1024]{2,1,0:T(8,128)(2,1)} %collective-permute-done.14.refs_4_.refs_6_), channel_id=1, source_target_pairs={{1,0},{5,4},{9,8},{13,12},{17,16},{21,20},{25,24},{29,28}} | collective-permute-start | bytes 5505032 | tf_op jit(solution)/shard_map/ppermute | solution.py:259
  369.3 31.9 %collective-permute-start.21 = (bf16[2,448,1024]{2,1,0:T(8,128)(2,1)S(1)}, bf16[2,448,1024]{2,1,0:T(8,128)(2,1)S(1)}, u32[]{:S(2)}, u32[]{:S(2)}) collective-permute-start(bf16[2,448,1024]{2,1,0:T(8,128)(2,1)S(1)} %get-tuple-element.111), channel_id=1, source_target_pairs={{0,4},{4,0},{8,12},{12,8},{16,20},{20,16},{24,28},{28,24},{1,5},{5... | collective-permute-start | bytes 5505032 | tf_op jit(solution)/shard_map/ppermute | solution.py:275
  376.2 26.3 %collective-permute-start.20 = (bf16[2,448,1024]{2,1,0:T(8,128)(2,1)S(1)}, bf16[2,448,1024]{2,1,0:T(8,128)(2,1)}, u32[]{:S(2)}, u32[]{:S(2)}) collective-permute-start(bf16[2,448,1024]{2,1,0:T(8,128)(2,1)S(1)} %get-tuple-element.112), channel_id=1, source_target_pairs={{0,4},{4,0},{8,12},{12,8},{16,20},{20,16},{24,28},{28,24},{1,5},{5... | collective-permute-start | bytes 5505032 | tf_op jit(solution)/shard_map/ppermute | solution.py:275
  403.3 16.7 %collective-permute-start.24 = (bf16[448,1024]{1,0:T(8,128)(2,1)S(1)}, bf16[448,1024]{1,0:T(8,128)(2,1)S(1)}, u32[]{:S(2)}, u32[]{:S(2)}) collective-permute-start(bf16[448,1024]{1,0:T(8,128)(2,1)S(1)} %get-tuple-element.89), channel_id=1, source_target_pairs={{0,1},{1,2},{2,3},{4,5},{5,6},{6,7},{8,9},{9,10},{10,11},{12,13},{... | collective-permute-start | bytes 2752520 | tf_op jit(solution)/shard_map/ppermute | solution.py:227
  404.8 15.2 %collective-permute-start.25 = (bf16[448,1024]{1,0:T(8,128)(2,1)S(1)}, bf16[448,1024]{1,0:T(8,128)(2,1)S(1)}, u32[]{:S(2)}, u32[]{:S(2)}) collective-permute-start(bf16[448,1024]{1,0:T(8,128)(2,1)S(1)} %get-tuple-element.90), channel_id=1, source_target_pairs={{1,0},{2,1},{3,2},{5,4},{6,5},{7,6},{9,8},{10,9},{11,10},{13,12},{... | collective-permute-start | bytes 2752520 | tf_op jit(solution)/shard_map/ppermute | solution.py:228
  421.4 75.0 %collective-permute-start.28 = (bf16[2,448,1024]{2,1,0:T(8,128)(2,1)S(1)}, bf16[2,448,1024]{2,1,0:T(8,128)(2,1)S(1)}, u32[]{:S(2)}, u32[]{:S(2)}) collective-permute-start(bf16[2,448,1024]{2,1,0:T(8,128)(2,1)S(1)} %pad_maximum_fusion.2.refs_10_.refs_14_.refs_8_), channel_id=1, source_target_pairs={{0,16},{4,20},{8,24},{12,28},{16,0},{20,4},{24,8},{28,12},{1,17},{... | collective-permute-start | bytes 5505032 | tf_op jit(solution)/shard_map/ppermute | solution.py:268
  422.1 74.3 %collective-permute-start.27 = (bf16[2,448,1024]{2,1,0:T(8,128)(2,1)S(1)}, bf16[2,448,1024]{2,1,0:T(8,128)(2,1)S(1)}, u32[]{:S(2)}, u32[]{:S(2)}) collective-permute-start(bf16[2,448,1024]{2,1,0:T(8,128)(2,1)S(1)} %pad_maximum_fusion.2.refs_10_.refs_14_.refs_8_), channel_id=1, source_target_pairs={{1,0},{2,1},{3,2},{5,4},{6,5},{7,6},{9,8},{10,9},{11,10},{13,12},{... | collective-permute-start | bytes 5505032 | tf_op jit(solution)/shard_map/ppermute | solution.py:259
  425.5 70.9 %collective-permute-start.26 = (bf16[2,448,1024]{2,1,0:T(8,128)(2,1)S(1)}, bf16[2,448,1024]{2,1,0:T(8,128)(2,1)S(1)}, u32[]{:S(2)}, u32[]{:S(2)}) collective-permute-start(bf16[2,448,1024]{2,1,0:T(8,128)(2,1)S(1)} %pad_maximum_fusion.2.refs_10_.refs_14_.refs_8_), channel_id=1, source_target_pairs={{0,1},{1,2},{2,3},{4,5},{5,6},{6,7},{8,9},{9,10},{10,11},{12,13},{... | collective-permute-start | bytes 5505032 | tf_op jit(solution)/shard_map/ppermute | solution.py:258
  426.8 73.3 %collective-permute-start.31 = (bf16[2,448,1024]{2,1,0:T(8,128)(2,1)S(1)}, bf16[2,448,1024]{2,1,0:T(8,128)(2,1)S(1)}, u32[]{:S(2)}, u32[]{:S(2)}) collective-permute-start(bf16[2,448,1024]{2,1,0:T(8,128)(2,1)S(1)} %pad_maximum_fusion.2.refs_10_.refs_14_.refs_8_), channel_id=1, source_target_pairs={{0,8},{4,12},{8,16},{12,20},{16,24},{20,28},{24,0},{28,4},{1,9},{5... | collective-permute-start | bytes 5505032 | tf_op jit(solution)/shard_map/ppermute | solution.py:268
  498.8 36.9 %collective-permute-start.29 = (bf16[2,448,1024]{2,1,0:T(8,128)(2,1)S(1)}, bf16[2,448,1024]{2,1,0:T(8,128)(2,1)}, u32[]{:S(2)}, u32[]{:S(2)}) collective-permute-start(bf16[2,448,1024]{2,1,0:T(8,128)(2,1)S(1)} %collective-permute-done.26.refs_12_.refs_0_), channel_id=1, source_target_pairs={{1,2},{2,3},{5,6},{6,7},{9,10},{10,11},{13,14},{14,15},{17,18},{18... | collective-permute-start | bytes 5505032 | tf_op jit(solution)/shard_map/ppermute | solution.py:258
  537.9 19.6 %collective-permute-start.35 = (bf16[2,448,1024]{2,1,0:T(8,128)(2,1)}, bf16[2,448,1024]{2,1,0:T(8,128)(2,1)}, u32[]{:S(2)}, u32[]{:S(2)}) collective-permute-start(bf16[2,448,1024]{2,1,0:T(8,128)(2,1)} %get-tuple-element.109), channel_id=1, source_target_pairs={{0,4},{4,0},{8,12},{12,8},{16,20},{20,16},{24,28},{28,24},{1,5},{5... | collective-permute-start | bytes 5505032 | tf_op jit(solution)/shard_map/ppermute | solution.py:275
  555.1 76.9 %collective-permute-start.32 = (bf16[2,448,1024]{2,1,0:T(8,128)(2,1)}, bf16[2,448,1024]{2,1,0:T(8,128)(2,1)S(1)}, u32[]{:S(2)}, u32[]{:S(2)}) collective-permute-start(bf16[2,448,1024]{2,1,0:T(8,128)(2,1)} %collective-permute-done.30.refs_1_.refs_3_), channel_id=1, source_target_pairs={{1,0},{5,4},{9,8},{13,12},{17,16},{21,20},{25,24},{29,28}} | collective-permute-start | bytes 5505032 | tf_op jit(solution)/shard_map/ppermute | solution.py:259
  556.0 76.0 %collective-permute-start.33 = (bf16[2,448,1024]{2,1,0:T(8,128)(2,1)}, bf16[2,448,1024]{2,1,0:T(8,128)(2,1)S(1)}, u32[]{:S(2)}, u32[]{:S(2)}) collective-permute-start(bf16[2,448,1024]{2,1,0:T(8,128)(2,1)} %collective-permute-done.29.refs_2_.refs_4_), channel_id=1, source_target_pairs={{2,3},{6,7},{10,11},{14,15},{18,19},{22,23},{26,27},{30,31}} | collective-permute-start | bytes 5505032 | tf_op jit(solution)/shard_map/ppermute | solution.py:258
  (27 other events, 1594.2 us)
Sparse Core Ops, SparseCore 0:
  35.9 53.6 all-gather.1

commit v3 on v2

v3 whole, which is shorter than its diff:
```python
import functools
import jax
import jax.numpy as jnp
from jax import lax
from jax.experimental import pallas as pl
from jax.experimental.pallas import tpu as pltpu
from jax.sharding import PartitionSpec as P

CHUNKS = 2
LANES = 128
CONTRACT_LAST = (((1,), (1,)), ((), ()))


def hidden_kernel(count, table_ref, weight_ref, features_ref, out_ref):
    groups, per_group, local_tokens, local_features = features_ref.shape
    for g in range(groups):
        place = table_ref[count + g]
        total = None
        for q in range(per_group):
            part = lax.dot_general(
                weight_ref[:, q * local_features : (q + 1) * local_features],
                features_ref[place, q],
                CONTRACT_LAST,
                preferred_element_type=jnp.float32,
            )
            total = part if total is None else total + part
        out_ref[0, :, g * local_tokens : (g + 1) * local_tokens] = total


def hidden_parts(weight, features, chunk, chunk_rows, offsets, own_group):
    groups, per_group, local_tokens, local_features = features.shape
    width = weight.shape[1]
    tokens = groups * local_tokens
    count = len(offsets)
    table = jnp.stack(
        [(own_group + offset) % groups * CHUNKS + chunk for offset in offsets]
        + [(own_group + g) % groups for g in range(groups)]
    ).astype(jnp.int32)
    return pl.pallas_call(
        functools.partial(hidden_kernel, count),
        grid_spec=pltpu.PrefetchScalarGridSpec(
            num_scalar_prefetch=1,
            grid=(count,),
            in_specs=[
                pl.BlockSpec((chunk_rows, width), lambda i, table_ref: (table_ref[i], 0)),
                pl.BlockSpec(features.shape, lambda i, table_ref: (0, 0, 0, 0)),
            ],
            out_specs=pl.BlockSpec((1, chunk_rows, tokens), lambda i, table_ref: (i, 0, 0)),
        ),
        out_shape=jax.ShapeDtypeStruct((count, chunk_rows, tokens), jnp.float32),
        compiler_params=pltpu.CompilerParams(
            dimension_semantics=("arbitrary",), vmem_limit_bytes=32 * 2**20
        ),
        cost_estimate=pl.CostEstimate(
            flops=2 * count * chunk_rows * tokens * width,
            bytes_accessed=count * chunk_rows * (2 * width + 4 * tokens) + 2 * tokens * width,
            transcendentals=0,
        ),
    )(table, weight, features)


def factor_kernel(shape, candidates, plan, scale, table_ref, *refs):
    partners, chunk_total, chunk_rows = shape
    total = len(plan)
    row_refs = refs[: sum(candidates)]
    columns = refs[len(row_refs) : len(row_refs) + partners * chunk_total]
    out_ref, held, rows_held, wide_even, wide_odd, column_sems, row_sems = refs[-7:]
    wides = (wide_even, wide_odd)
    slice_width = held.shape[2]
    lane_tiles = slice_width // LANES
    stride = 2 * lane_tiles
    step = pl.program_id(0)
    current = jnp.minimum(step, total - 1)
    slot, buffer = table_ref[2 * total + current], table_ref[3 * total + current]
    loads = [i for i in range(total) if i == 0 or plan[i][0] != plan[i - 1][0]]
    firsts = {}
    for i, (_, k) in enumerate(plan):
        firsts.setdefault(k, i)

    def column_copy(k, chunk):
        return pltpu.make_async_copy(
            columns[k * chunk_total + chunk],
            held.at[k, :, pl.ds(chunk * chunk_rows, chunk_rows)],
            column_sems.at[k, chunk],
        )

    def row_copy(source, place):
        return pltpu.make_async_copy(source, rows_held.at[place], row_sems.at[place])

    def fetch(load):
        piece = plan[loads[load]][0]
        first = sum(candidates[:piece])
        for choice in range(candidates[piece]):

            @pl.when(table_ref[4 * total + piece] == choice)
            def _():
                row_copy(row_refs[first + choice], load % 2).start()

    @pl.when(step == 0)
    def _():
        fetch(0)
        for k in sorted(firsts, key=firsts.get):
            for chunk in range(chunk_total):
                column_copy(k, chunk).start()

    for load, i in enumerate(loads):

        @pl.when(step == i)
        def _():
            row_copy(row_refs[0], load % 2).wait()
            if load + 1 < len(loads):
                fetch(load + 1)

    for k, i in firsts.items():

        @pl.when(step == i)
        def _():
            for chunk in range(chunk_total):
                column_copy(k, chunk).wait()

    def lay_out(wide):
        out_ref[0] = wide[...].astype(out_ref.dtype)

    def multiply(wide):
        for f in range(2):
            rows = rows_held[buffer, f]
            for first in range(0, lane_tiles, 2):
                count = min(2, lane_tiles - first)
                part = held[slot, f, pl.ds(first * LANES, count * LANES), :]
                product = lax.dot_general(
                    rows, part, CONTRACT_LAST, preferred_element_type=jnp.float32
                )
                product = product * scale
                for extra in range(count):
                    start = (first + extra) * 2 + f
                    wide[pl.ds(start, chunk_rows, stride=stride), :] = product[
                        :, extra * LANES : (extra + 1) * LANES
                    ]

    for parity in range(2):

        @pl.when((step % 2 == parity) & (step < total))
        def _():
            multiply(wides[parity])
            lay_out(wides[1 - parity])

    @pl.when(step == total)
    def _():
        lay_out(wides[(total - 1) % 2])


def factor_rows(pieces, columns, plan, previous, band, slices, scale):
    used = sorted(pieces)
    plan = [(used.index(piece), k) for piece, k in plan]
    pieces = [pieces[piece] for piece in used]
    keys = sorted({k for _, k in plan})
    _, chunk_rows, tokens = pieces[0][0][0].shape
    dtype = pieces[0][0][0].dtype
    chunk_total = len(columns[keys[0]])
    slice_width = chunk_total * chunk_rows
    height = chunk_rows * 2 * (slice_width // LANES)
    buffers, last = [], None
    for piece, _ in plan:
        if not buffers:
            buffers.append(0)
        else:
            buffers.append(buffers[-1] if piece == last else 1 - buffers[-1])
        last = piece
    table = jnp.stack(
        [jnp.int32(pieces[piece][2]) for piece, _ in plan]
        + [jnp.int32(k) for _, k in plan]
        + [jnp.int32(keys.index(k)) for _, k in plan]
        + [jnp.int32(buffer) for buffer in buffers]
        + [jnp.int32(choice) for _, choice, _ in pieces]
    )
    operands = [array for arrays, _, _ in pieces for array in arrays]
    operands += [part for k in keys for part in columns[k]]
    aliases = {}
    if previous is not None:
        aliases = {1 + len(operands): 0}
        operands.append(previous)
    total = len(plan)

    def placed(step, table_ref):
        done = jnp.maximum(step - 1, 0)
        return table_ref[total + done], table_ref[done], 0

    return pl.pallas_call(
        functools.partial(
            factor_kernel,
            (len(keys), chunk_total, chunk_rows),
            tuple(len(arrays) for arrays, _, _ in pieces),
            tuple((piece, keys.index(k)) for piece, k in plan),
            scale,
        ),
        grid_spec=pltpu.PrefetchScalarGridSpec(
            num_scalar_prefetch=1,
            grid=(total + 1,),
            in_specs=[pl.BlockSpec(memory_space=pl.ANY)] * len(operands),
            out_specs=pl.BlockSpec((1, height, LANES), placed),
            scratch_shapes=[
                pltpu.VMEM((len(keys), 2, slice_width, tokens), dtype),
                pltpu.VMEM((2, 2, chunk_rows, tokens), dtype),
                pltpu.VMEM((height, LANES), jnp.float32),
                pltpu.VMEM((height, LANES), jnp.float32),
                pltpu.SemaphoreType.DMA((len(keys), chunk_total)),
                pltpu.SemaphoreType.DMA((2,)),
            ],
        ),
        out_shape=jax.ShapeDtypeStruct((band, slices * chunk_total * height, LANES), dtype),
        input_output_aliases=aliases,
        compiler_params=pltpu.CompilerParams(
            dimension_semantics=("arbitrary",), vmem_limit_bytes=48 * 2**20
        ),
        cost_estimate=pl.CostEstimate(
            flops=4 * total * chunk_rows * tokens * slice_width,
            bytes_accessed=4 * total * chunk_rows * (tokens + slice_width)
            + 4 * len(keys) * slice_width * tokens,
            transcendentals=0,
        ),
    )(table, *operands)


def tie(*arrays):
    return lax.optimization_barrier(arrays)


def arrivals(groups, d):
    found = []
    for hops in range(1, groups):
        if d + hops < groups:
            found.append((hops, False))
        if d - hops >= 0:
            found.append((hops, True))
    return found


def per_device(cotangent, down_weight, gate_pre, up_pre):
    blocks = lax.axis_size("tensor")
    groups = lax.axis_size("dp")
    own_block = lax.axis_index("tensor")
    own_group = lax.axis_index("dp")
    per_group = blocks // groups
    local_tokens, block_width = gate_pre.shape
    local_features = cotangent.shape[1]
    slice_width = block_width // groups
    all_tokens = local_tokens * groups
    half_band = blocks // 2
    chunk_rows = slice_width // CHUNKS
    use_kernels = (
        slice_width % LANES == 0
        and chunk_rows % 16 == 0
        and local_features % LANES == 0
        and local_tokens % LANES == 0
    )

    to_plane = [
        ((m * per_group + q) * groups + g, ((m + g) % groups * per_group + q) * groups + m)
        for m in range(groups)
        for q in range(per_group)
        for g in range(groups)
    ]
    sent = lax.ppermute(cotangent, ("tensor", "dp"), to_plane)
    sent, gate_pre, up_pre = tie(sent, gate_pre, up_pre)
    features = lax.all_gather(sent, "tensor", axis=0, tiled=True)

    saved = jnp.stack([gate_pre, up_pre])

    def saved_slice(index):
        return lax.dynamic_slice_in_dim(saved, (index % groups) * slice_width, slice_width, 2)

    saved_pieces = [saved_slice(own_group)]
    for shift in range(1, groups):
        ring = [(d, (d + shift) % groups) for d in range(groups)]
        saved_pieces.append(lax.ppermute(saved_slice(own_group + shift), "dp", ring))
    features, *saved_pieces = tie(features, *saved_pieces)
    features = features.reshape(groups, per_group, local_tokens, local_features)

    def partial_products(chunk, offsets, features):
        if use_kernels:
            made = hidden_parts(down_weight, features, chunk, chunk_rows, offsets, own_group)
            return {offset: made[place] for place, offset in enumerate(offsets)}
        ordered = jnp.roll(features, -own_group, axis=0)
        made = {}
        for offset in offsets:
            first = (own_group + offset) % groups * slice_width + chunk * chunk_rows
            part = lax.dynamic_slice_in_dim(down_weight, first, chunk_rows, 0)
            made[offset] = jnp.einsum(
                "uqw,gqtw->ugt",
                part.reshape(chunk_rows, per_group, local_features),
                ordered,
                preferred_element_type=jnp.float32,
            ).reshape(chunk_rows, all_tokens)
        return made

    def reduce_step(partial, step, received):
        right, left = partial[groups - step], partial[step]
        if received is not None:
            right = right + received[0].astype(jnp.float32)
            left = left + received[1].astype(jnp.float32)
        return (
            lax.ppermute(right.astype(jnp.bfloat16), "dp", [(d, d + 1) for d in range(step)]),
            lax.ppermute(
                left.astype(jnp.bfloat16),
                "dp",
                [(d, d - 1) for d in range(groups - step, groups)],
            ),
        )

    def order_saved(pieces):
        pieces = jnp.stack(pieces)
        return jnp.concatenate(
            [
                lax.dynamic_index_in_dim(pieces, (own_group - h) % groups, 0, keepdims=False)
                for h in range(groups)
            ],
            axis=1,
        ).transpose(0, 2, 1)

    def gradients(partial, received, saved_all, chunk):
        hidden_cot = partial[0] + received[0].astype(jnp.float32) + received[1].astype(jnp.float32)
        local = saved_all[:, chunk * chunk_rows : (chunk + 1) * chunk_rows].astype(jnp.float32)
        gate_value, up_value = local[0], local[1]
        sigmoid_gate = jax.nn.sigmoid(gate_value)
        grad_gate = hidden_cot * up_value * sigmoid_gate * (1.0 + gate_value * (1.0 - sigmoid_gate))
        grad_up = hidden_cot * gate_value * sigmoid_gate
        return jnp.stack([grad_gate.astype(jnp.bfloat16), grad_up.astype(jnp.bfloat16)])

    def gather_step(step, left, right):
        return (
            lax.ppermute(left, "dp", [(d, d + 1) for d in range(step - 1, groups - 1)]),
            lax.ppermute(right, "dp", [(d, d - 1) for d in range(1, groups - step + 1)]),
        )

    shifts = list(range(2, half_band + 1, 2))
    turns = max(groups - 2, 1)
    share = -(-len(shifts) // turns)

    def partner_step(step, found):
        made = {}
        if step > 1:
            swap = [(t, t ^ 1) for t in range(blocks)]
            odd = own_block % 2 == 1
            for k in range(1, half_band, 2):
                if k not in found and k - 1 in found and k + 1 in found:
                    made[k] = lax.ppermute(
                        jnp.where(odd, found[k + 1], found[k - 1]), "tensor", swap
                    )
        for k in shifts[(step - 1) * share : step * share]:
            made[k] = lax.ppermute(
                found[0], "tensor", [(t, (t + k) % blocks) for t in range(blocks)]
            )
        return made

    band = half_band + 1
    inverse_count = 1.0 / all_tokens
    order = [arrivals(groups, d) for d in range(groups)]

    ready = {0: 0}
    for place, k in enumerate(shifts):
        ready[k] = place // share + 1
    for k in range(1, half_band, 2):
        ready[k] = max(ready[k - 1], ready[k + 1]) + 0.5
    calls = {}
    for k in sorted(ready, key=ready.get):
        for chunk in range(CHUNKS):
            for place in range(groups):
                came = 0
                if chunk == CHUNKS - 1 and place:
                    came = max(order[d][place - 1][0] for d in range(groups))
                calls.setdefault(max(ready[k], came), []).append(((chunk, place), k))

    def by_plane(values):
        return jnp.asarray(values, jnp.int32)[own_group]

    def row_piece(chunk, place):
        own, held = rows[chunk]
        if place == 0:
            return [own], 0, own_group * CHUNKS + chunk
        wanted = [order[d][place - 1] for d in range(groups)]
        kinds = sorted(set(wanted))
        origin = [d - hops if left else d + hops for d, (hops, left) in enumerate(wanted)]
        return (
            [held[hops][int(left)] for hops, left in kinds],
            by_plane([kinds.index(kind) for kind in wanted]),
            by_plane(origin) * CHUNKS + chunk,
        )

    def multiply(since, until, result):
        for time in sorted(calls):
            if since <= time < until:
                plan = calls[time]
                pieces = {piece: row_piece(*piece) for piece, _ in plan}
                keys = {k for _, k in plan}
                parts = {k: [columns[c][k] for c in range(CHUNKS)] for k in keys}
                result = factor_rows(pieces, parts, plan, result, band, groups, inverse_count)
        return result

    first_offsets = sorted({1, groups - 1})
    other_offsets = [offset for offset in range(groups) if offset not in first_offsets]
    partial = partial_products(0, first_offsets, features)
    received = reduce_step(partial, 1, None)
    partial.update(partial_products(0, other_offsets, features))
    received = tie(*received, *saved_pieces)
    received, saved_pieces = received[:2], received[2:]
    saved_all = order_saved(saved_pieces)
    for step in range(2, groups):
        received = tie(*reduce_step(partial, step, received))
    rows, columns, result = [], [], None
    for chunk in range(CHUNKS):
        own = gradients(partial, received, saved_all, chunk)
        own, features = tie(own, features)
        later = chunk + 1 < CHUNKS
        partial, received = {}, ()
        if later:
            partial = partial_products(chunk + 1, list(range(groups)), features)
        held, column, found = {}, {0: own}, {0: own}
        rows.append((own, held))
        columns.append(column)
        left = right = own
        for step in range(1, groups):
            if later and step > 1:
                received = reduce_step(partial, step - 1, received or None)
            left, right = gather_step(step, left, right)
            held[step] = (right, left)
            made = partner_step(step, found)
            column.update(made)
            found.update(made)
            if use_kernels and not later:
                result = multiply(step - 1.5, step - 0.5, result)
            if step < groups - 1 or later:
                keys, offsets = list(found), list(partial) if step == 1 else []
                moved = tie(
                    left, right, *received, *[found[k] for k in keys], *[partial[o] for o in offsets]
                )
                left, right = moved[:2]
                moved = moved[2:]
                received, moved = moved[: len(received)], moved[len(received) :]
                found = dict(zip(keys, moved))
                partial.update(zip(offsets, moved[len(keys) :]))
                if result is not None:
                    result, left, right = tie(result, left, right)
        if later:
            received = reduce_step(partial, groups - 1, received)

    if use_kernels:
        result = multiply(groups - 1.5, groups, result)
        result = result.reshape(band, -1, 2, LANES).transpose(2, 0, 1, 3)
    else:

        def in_order(own, held):
            turned = [own]
            for offset in range(1, groups):
                from_right = own_group + offset < groups
                turned.append(jnp.where(from_right, held[offset][0], held[groups - offset][1]))
            return jnp.roll(jnp.stack(turned), own_group, axis=0)

        all_rows = jnp.concatenate([in_order(*pair) for pair in rows], axis=2)
        all_columns = jnp.stack([jnp.concatenate([columns[c][k] for c in range(CHUNKS)], axis=1) for k in range(band)])
        result = jnp.einsum(
            "sfrt,kfct->fksrc", all_rows, all_columns, preferred_element_type=jnp.float32
        )
        result = (result * inverse_count).astype(jnp.bfloat16)
    return result.reshape(1, 2, band, 1, block_width * slice_width)


def solution(mesh):
    placed = (P("dp", "tensor"), P("tensor", "dp"), P("dp", "tensor"), P("dp", "tensor"))
    return jax.shard_map(
        per_device,
        mesh=mesh,
        in_specs=placed,
        out_specs=P("tensor", None, None, "dp", None),
        check_vma=False,
    )
```

time: 675 us -> 626 us (0.927); the launches traced: 674 us -> 617 us
  starting transfers between devices: 139 us -> 94.8 us
  Pallas kernels: 107 us -> 144 us
  matrix products: 27.5 us -> 0 us
  local copies, waits for them, and re-layouts: 77.9 us -> 51.3 us
    ppermute x4, waiting for transfers between devices: 121 us -> 29 us  [partner_step(): lax.ppermute(found[0], 'tensor', [(t, (t + k) % blocks) for t in range(bl...]
    ppermute x3, waiting for transfers between devices: 6.36 us -> 77 us  [per_device(): lax.ppermute(saved_slice(own_group + shift), 'dp', ring)]
    pallas_call x2 -> x9, Pallas kernels: 107 us -> 144 us  [the longest x6 124 us: factor_rows(): pl.pallas_call(functools.partial(factor_kernel, (len(keys), chunk_total,...]
    dot_general x2 -> x0, matrix products: 27.5 us -> none  [partial_products(): lax.dot_general(part, features, (((1, 2), (0, 2)), ((), ())), preferred_e...]
    reshape x2 -> x0, local copies, waits for them, and re-layouts: 25.9 us -> none  [partial_products(): part = part.reshape(groups * chunk_rows, per_group, local_features)]
    ppermute x6, starting transfers between devices: 54.2 us -> 31.4 us  [reduce_step(): lax.ppermute(left.astype(jnp.bfloat16), 'dp', [(d, d - 1) for d in range(...]
    unnamed x44 -> x54, local copies, waits for them, and re-layouts: 4.65 us -> 22.8 us
    dot_general x2 -> x0, local copies, waits for them, and re-layouts: 16.8 us -> none  [partial_products(): lax.dot_general(part, features, (((1, 2), (0, 2)), ((), ())), preferred_e...]
  transfers between devices with their start and end apart: 37 -> 37, of which waited for: 12 -> 20; matrix products, arithmetic and copies ran while one was open for 17% -> 6% of each run, Pallas kernels for 11% -> 19%
where the time goes in v3:
time: 626 us; the launch traced here: 617 us
  waiting for transfers between devices  280 us (45%)
  Pallas kernels  144 us (23%)
  starting transfers between devices  94.8 us (15%)
  local copies, waits for them, and re-layouts  51.3 us (8%)
  other arithmetic  29.7 us (5%)
  between operations  16.7 us (3%)
    pallas_call x6, Pallas kernels, factor_rows(): pl.pallas_call(functools.partial(factor_kernel, (len(keys), chunk_total,...  124 us
    ppermute x3, waiting for transfers between devices, per_device(): lax.ppermute(saved_slice(own_group + shift), 'dp', ring)  77 us
    ppermute x6, waiting for transfers between devices, gather_step(): lax.ppermute(left, 'dp', [(d, d + 1) for d in range(step - 1, groups - 1)])  63 us
    ppermute x6, waiting for transfers between devices, reduce_step(): lax.ppermute(left.astype(jnp.bfloat16), 'dp', [(d, d - 1) for d in range(...  62.1 us
    ppermute x6, starting transfers between devices, reduce_step(): lax.ppermute(left.astype(jnp.bfloat16), 'dp', [(d, d - 1) for d in range(...  31.4 us
    ppermute x4, waiting for transfers between devices, partner_step(): lax.ppermute(found[0], 'tensor', [(t, (t + k) % blocks) for t in range(bl...  29 us
    unnamed x54, local copies, waits for them, and re-layouts  22.8 us
    ppermute x6, waiting for transfers between devices, reduce_step(): lax.ppermute(right.astype(jnp.bfloat16), 'dp', [(d, d + 1) for d in range...  22 us
  transfers between devices with their start and end apart: 37, of which 20 were waited for; matrix products, arithmetic and copies ran while one was open for 6% of the time, Pallas kernels for 19%

profile of v3, /device:TPU:29, one launch (start us, length us, event | category | flops | bytes accessed | tf_op | source)
XLA Modules:
  0.0 616.9 jit_solution(1806684493083560514)
XLA Ops:
  9.5 13.0 %collective-permute-done = bf16[256,1024]{1,0:T(8,128)(2,1)S(1)} collective-permute-done((bf16[256,1024]{1,0:T(8,128)(2,1)}, bf16[256,1024]{1,0:T(8,128)(2,1)S(1)}, u32[]{:S(2)}, u32[]{:S(2)}) %collective-permute-start) | collective-permute-done | bytes 524320 | tf_op jit(solution)/shard_map/ppermute | solution.py:263
  27.0 12.0 %collective-permute-start.1 = (bf16[2,256,896]{2,1,0:T(8,128)(2,1)}, bf16[2,256,896]{2,1,0:T(8,128)(2,1)S(1)}, u32[]{:S(2)}, u32[]{:S(2)}) collective-permute-start(bf16[2,256,896]{2,1,0:T(8,128)(2,1)} %get-tuple-element.129), channel_id=1, source_target_pairs={{0,1},{1,2},{2,3},{3,0},{4,5},{5,6},{6,7},{7,4},{8,9},{9,10},{10,1... | collective-permute-start | bytes 2752520 | tf_op jit(solution)/shard_map/ppermute | solution.py:275
  39.9 17.6 %collective-permute-done.1 = bf16[2,256,896]{2,1,0:T(8,128)(2,1)S(1)} collective-permute-done((bf16[2,256,896]{2,1,0:T(8,128)(2,1)}, bf16[2,256,896]{2,1,0:T(8,128)(2,1)S(1)}, u32[]{:S(2)}, u32[]{:S(2)}) %collective-permute-start.1) | collective-permute-done | bytes 917536 | tf_op jit(solution)/shard_map/ppermute | solution.py:275
  57.5 59.4 %collective-permute-done.2 = bf16[2,256,896]{2,1,0:T(8,128)(2,1)S(1)} collective-permute-done((bf16[2,256,896]{2,1,0:T(8,128)(2,1)}, bf16[2,256,896]{2,1,0:T(8,128)(2,1)S(1)}, u32[]{:S(2)}, u32[]{:S(2)}) %collective-permute-start.2) | collective-permute-done | bytes 917536 | tf_op jit(solution)/shard_map/ppermute | solution.py:275
  117.0 5.2 copy-done.1
  133.1 4.8 collective-permute-start.5
  137.9 5.2 copy-done.2
  145.3 4.8 shard_map.442
  150.1 5.9 collective-permute-done.5
  167.4 15.4 %collective-permute-done.7 = bf16[448,1024]{1,0:T(8,128)(2,1)} collective-permute-done((bf16[448,1024]{1,0:T(8,128)(2,1)}, bf16[448,1024]{1,0:T(8,128)(2,1)}, u32[]{:S(2)}, u32[]{:S(2)}) %collective-permute-start.7) | collective-permute-done | bytes 917536 | tf_op jit(solution)/shard_map/ppermute | solution.py:303
  187.5 5.7 collective-permute-start.9
  212.3 5.4 collective-permute-start.10
  218.9 5.8 collective-permute-start.12
  227.1 10.5 %shard_map.444 = f32[4,448,1024]{2,1,0:T(8,128)S(1)} custom-call(s32[8]{0:T(128)S(1)} %stack.186.table_ref, bf16[3584,2048]{1,0:T(8,128)(2,1)} %weight_ref.5, bf16[4,2,256,1024]{3,2,1,0:T(8,128)(2,1)S(1)} %bitcast.122), custom_call_target="tpu_custom_call" | custom-call | flops 7516192768 | bytes 18874368 | tf_op jit(solution)/shard_map/pallas_call | solution.py:39
  238.9 13.1 %collective-permute-done.10.refs_1_ = bf16[2,448,1024]{2,1,0:T(8,128)(2,1)} collective-permute-done((bf16[2,448,1024]{2,1,0:T(8,128)(2,1)S(1)}, bf16[2,448,1024]{2,1,0:T(8,128)(2,1)}, u32[]{:S(2)}, u32[]{:S(2)}) %collective-permute-start.10) | collective-permute-done | bytes 1835040 | tf_op jit(solution)/shard_map/ppermute | solution.py:332
  252.0 5.2 collective-permute-done.11.refs_2_.refs_3_
  257.2 24.7 %collective-permute-done.12.refs_15_.refs_20_.refs_8_ = bf16[2,448,1024]{2,1,0:T(8,128)(2,1)} collective-permute-done((bf16[2,448,1024]{2,1,0:T(8,128)(2,1)S(1)}, bf16[2,448,1024]{2,1,0:T(8,128)(2,1)}, u32[]{:S(2)}, u32[]{:S(2)}) %collective-permute-start.12) | collective-permute-done | bytes 1835040 | tf_op jit(solution)/shard_map/ppermute | solution.py:350
  290.5 7.4 %collective-permute-start.16 = (bf16[448,1024]{1,0:T(8,128)(2,1)S(1)}, bf16[448,1024]{1,0:T(8,128)(2,1)S(1)}, u32[]{:S(2)}, u32[]{:S(2)}) collective-permute-start(bf16[448,1024]{1,0:T(8,128)(2,1)S(1)} %convert_element_type.106), channel_id=1, source_target_pairs={{3,2},{7,6},{11,10},{15,14},{19,18},{23,22},{27,26},{31,30}} | collective-permute-start | bytes 2752520 | tf_op jit(solution)/shard_map/ppermute | solution.py:303
  297.9 19.4 %collective-permute-done.16 = bf16[448,1024]{1,0:T(8,128)(2,1)S(1)} collective-permute-done((bf16[448,1024]{1,0:T(8,128)(2,1)S(1)}, bf16[448,1024]{1,0:T(8,128)(2,1)S(1)}, u32[]{:S(2)}, u32[]{:S(2)}) %collective-permute-start.16) | collective-permute-done | bytes 917536 | tf_op jit(solution)/shard_map/ppermute | solution.py:303
  317.3 18.8 %collective-permute-done.14.refs_5_.refs_7_ = bf16[2,448,1024]{2,1,0:T(8,128)(2,1)S(1)} collective-permute-done((bf16[2,448,1024]{2,1,0:T(8,128)(2,1)}, bf16[2,448,1024]{2,1,0:T(8,128)(2,1)S(1)}, u32[]{:S(2)}, u32[]{:S(2)}) %collective-permute-start.14) | collective-permute-done | bytes 1835040 | tf_op jit(solution)/shard_map/ppermute | solution.py:331
  348.1 19.3 %collective-permute-done.22 = bf16[448,1024]{1,0:T(8,128)(2,1)S(1)} collective-permute-done((bf16[448,1024]{1,0:T(8,128)(2,1)S(1)}, bf16[448,1024]{1,0:T(8,128)(2,1)S(1)}, u32[]{:S(2)}, u32[]{:S(2)}) %collective-permute-start.22) | collective-permute-done | bytes 917536 | tf_op jit(solution)/shard_map/ppermute | solution.py:303
  367.5 16.8 %collective-permute-done.20.refs_9_ = bf16[2,448,1024]{2,1,0:T(8,128)(2,1)S(1)} collective-permute-done((bf16[2,448,1024]{2,1,0:T(8,128)(2,1)S(1)}, bf16[2,448,1024]{2,1,0:T(8,128)(2,1)S(1)}, u32[]{:S(2)}, u32[]{:S(2)}) %collective-permute-start.20) | collective-permute-done | bytes 1835040 | tf_op jit(solution)/shard_map/ppermute | solution.py:331
  391.6 17.3 %collective-permute-done.24 = bf16[448,1024]{1,0:T(8,128)(2,1)S(1)} collective-permute-done((bf16[448,1024]{1,0:T(8,128)(2,1)S(1)}, bf16[448,1024]{1,0:T(8,128)(2,1)S(1)}, u32[]{:S(2)}, u32[]{:S(2)}) %collective-permute-start.24) | collective-permute-done | bytes 917536 | tf_op jit(solution)/shard_map/ppermute | solution.py:302
  414.0 6.0 collective-permute-start.27
  428.0 15.6 %shard_map.445.refs_17_ = bf16[5,50176,128]{2,1,0:T(8,128)(2,1)} custom-call(s32[25]{0:T(128)S(1)} %stack.77.table_ref, bf16[2,448,1024]{2,1,0:T(8,128)(2,1)S(1)} %pad_maximum_fusion.1.refs_0_.refs_11_.refs_13_.refs_16_.refs_4_, bf16[2,448,1024]{2,1,0:T(8,128)(2,1)} %collective-permute-done.10.refs_1_, ...), custom_call_target="tpu_custom_call" | custom-call | flops 8220835840 | bytes 20873216 | tf_op jit(solution)/shard_map/pallas_call | solution.py:188
  443.6 11.8 %collective-permute-done.26.refs_12_.refs_13_ = bf16[2,448,1024]{2,1,0:T(8,128)(2,1)} collective-permute-done((bf16[2,448,1024]{2,1,0:T(8,128)(2,1)}, bf16[2,448,1024]{2,1,0:T(8,128)(2,1)}, u32[]{:S(2)}, u32[]{:S(2)}) %collective-permute-start.26) | collective-permute-done | bytes 1835040 | tf_op jit(solution)/shard_map/ppermute | solution.py:331
  483.0 20.7 %shard_map.446.refs_15_ = bf16[5,50176,128]{2,1,0:T(8,128)(2,1)} custom-call(s32[34]{0:T(128)S(1)} %stack.190.table_ref, bf16[2,448,1024]{2,1,0:T(8,128)(2,1)S(1)} %pad_maximum_fusion.1.refs_0_.refs_11_.refs_13_.refs_16_.refs_4_, bf16[2,448,1024]{2,1,0:T(8,128)(2,1)} %collective-permute-done.10.refs_1_, ...), custom_call_target="tpu_custom_call", output_to_operand_aliasing={{}: (18, {})} | custom-call | flops 11509170176 | bytes 31424512 | tf_op jit(solution)/shard_map/pallas_call | solution.py:188
  503.7 10.4 %collective-permute-done.30.refs_15_.refs_1_ = bf16[2,448,1024]{2,1,0:T(8,128)(2,1)} collective-permute-done((bf16[2,448,1024]{2,1,0:T(8,128)(2,1)}, bf16[2,448,1024]{2,1,0:T(8,128)(2,1)}, u32[]{:S(2)}, u32[]{:S(2)}) %collective-permute-start.30) | collective-permute-done | bytes 1835040 | tf_op jit(solution)/shard_map/ppermute | solution.py:331
  519.0 18.4 %shard_map.447.refs_24_ = bf16[5,50176,128]{2,1,0:T(8,128)(2,1)} custom-call(s32[30]{0:T(128)S(1)} %stack.193.table_ref, bf16[2,448,1024]{2,1,0:T(8,128)(2,1)S(1)} %pad_maximum_fusion.1.refs_0_.refs_11_.refs_13_.refs_16_.refs_4_, bf16[2,448,1024]{2,1,0:T(8,128)(2,1)} %collective-permute-done.10.refs_1_, ...), custom_call_target="tpu_custom_call", output_to_operand_aliasing={{}: (16, {})} | custom-call | flops 9865003008 | bytes 24313856 | tf_op jit(solution)/shard_map/pallas_call | solution.py:188
  537.4 27.8 %shard_map.448.refs_18_ = bf16[5,50176,128]{2,1,0:T(8,128)(2,1)} custom-call(s32[47]{0:T(128)S(1)} %stack.192.table_ref, bf16[2,448,1024]{2,1,0:T(8,128)(2,1)S(1)} %pad_maximum_fusion.1.refs_0_.refs_11_.refs_13_.refs_16_.refs_4_, bf16[2,448,1024]{2,1,0:T(8,128)(2,1)} %collective-permute-done.10.refs_1_, ...), custom_call_target="tpu_custom_call", output_to_operand_aliasing={{}: (25, {})} | custom-call | flops 16441671680 | bytes 49086464 | tf_op jit(solution)/shard_map/pallas_call | solution.py:188
  566.5 20.8 %shard_map.449.refs_14_ = bf16[5,50176,128]{2,1,0:T(8,128)(2,1)} custom-call(s32[35]{0:T(128)S(1)} %stack.191.table_ref, bf16[2,448,1024]{2,1,0:T(8,128)(2,1)S(1)} %pad_maximum_fusion.1.refs_0_.refs_11_.refs_13_.refs_16_.refs_4_, bf16[2,448,1024]{2,1,0:T(8,128)(2,1)} %collective-permute-done.10.refs_1_, ...), custom_call_target="tpu_custom_call", output_to_operand_aliasing={{}: (19, {})} | custom-call | flops 11509170176 | bytes 27754496 | tf_op jit(solution)/shard_map/pallas_call | solution.py:188
  588.6 20.9 %shard_map.450 = bf16[5,50176,128]{2,1,0:T(8,128)(2,1)} custom-call(s32[21]{0:T(128)S(1)} %stack.74.table_ref, bf16[2,448,1024]{2,1,0:T(8,128)(2,1)} %collective-permute-done.29.refs_14_.refs_0_, bf16[2,448,1024]{2,1,0:T(8,128)(2,1)} %collective-permute-done.30.refs_15_.refs_1_, ...), custom_call_target="tpu_custom_call", output_to_operand_aliasing={{}: (15, {})} | custom-call | flops 8220835840 | bytes 35553280 | tf_op jit(solution)/shard_map/pallas_call | solution.py:188
  (158 shorter events, 135.3 us)
Async XLA Ops:
  6.5 110.4 %all-gather.2.cloned.1.call-start = ((), (), s32[]{:S(2)}) async-start(), calls=%async_computation | async-start | bytes 4718592 | tf_op jit(solution)/shard_map/all_gather | solution.py:265
  27.0 30.5 %collective-permute-start.1 = (bf16[2,256,896]{2,1,0:T(8,128)(2,1)}, bf16[2,256,896]{2,1,0:T(8,128)(2,1)S(1)}, u32[]{:S(2)}, u32[]{:S(2)}) collective-permute-start(bf16[2,256,896]{2,1,0:T(8,128)(2,1)} %get-tuple-element.129), channel_id=1, source_target_pairs={{0,1},{1,2},{2,3},{3,0},{4,5},{5,6},{6,7},{7,4},{8,9},{9,10},{10,1... | collective-permute-start | bytes 2752520 | tf_op jit(solution)/shard_map/ppermute | solution.py:275
  39.0 77.9 %collective-permute-start.2 = (bf16[2,256,896]{2,1,0:T(8,128)(2,1)}, bf16[2,256,896]{2,1,0:T(8,128)(2,1)S(1)}, u32[]{:S(2)}, u32[]{:S(2)}) collective-permute-start(bf16[2,256,896]{2,1,0:T(8,128)(2,1)} %get-tuple-element.130), channel_id=1, source_target_pairs={{0,2},{1,3},{2,0},{3,1},{4,6},{5,7},{6,4},{7,5},{8,10},{9,11},{10,... | collective-permute-start | bytes 2752520 | tf_op jit(solution)/shard_map/ppermute | solution.py:275
  39.0 77.9 %collective-permute-start.3 = (bf16[2,256,896]{2,1,0:T(8,128)(2,1)}, bf16[2,256,896]{2,1,0:T(8,128)(2,1)}, u32[]{:S(2)}, u32[]{:S(2)}) collective-permute-start(bf16[2,256,896]{2,1,0:T(8,128)(2,1)} %get-tuple-element.127), channel_id=1, source_target_pairs={{0,3},{1,0},{2,1},{3,2},{4,7},{5,4},{6,5},{7,6},{8,11},{9,8},{10,9... | collective-permute-start | bytes 2752520 | tf_op jit(solution)/shard_map/ppermute | solution.py:275
  133.1 22.9 %collective-permute-start.5 = (bf16[448,1024]{1,0:T(8,128)(2,1)}, bf16[448,1024]{1,0:T(8,128)(2,1)}, u32[]{:S(2)}, u32[]{:S(2)}) collective-permute-start(bf16[448,1024]{1,0:T(8,128)(2,1)} %get-tuple-element.125), channel_id=1, source_target_pairs={{3,2},{7,6},{11,10},{15,14},{19,18},{23,22},{27,26},{31,30}} | collective-permute-start | bytes 2752520 | tf_op jit(solution)/shard_map/ppermute | solution.py:303
  160.9 21.9 %collective-permute-start.7 = (bf16[448,1024]{1,0:T(8,128)(2,1)}, bf16[448,1024]{1,0:T(8,128)(2,1)}, u32[]{:S(2)}, u32[]{:S(2)}) collective-permute-start(bf16[448,1024]{1,0:T(8,128)(2,1)} %get-tuple-element.119), channel_id=1, source_target_pairs={{2,1},{3,2},{6,5},{7,6},{10,9},{11,10},{14,13},{15,14},{18,17},{19... | collective-permute-start | bytes 2752520 | tf_op jit(solution)/shard_map/ppermute | solution.py:303
  186.2 22.3 %collective-permute-start.8 = (bf16[448,1024]{1,0:T(8,128)(2,1)}, bf16[448,1024]{1,0:T(8,128)(2,1)}, u32[]{:S(2)}, u32[]{:S(2)}) collective-permute-start(bf16[448,1024]{1,0:T(8,128)(2,1)} %get-tuple-element.118), channel_id=1, source_target_pairs={{0,1},{1,2},{2,3},{4,5},{5,6},{6,7},{8,9},{9,10},{10,11},{12,13},{... | collective-permute-start | bytes 2752520 | tf_op jit(solution)/shard_map/ppermute | solution.py:302
  187.5 22.0 %collective-permute-start.9 = (bf16[448,1024]{1,0:T(8,128)(2,1)}, bf16[448,1024]{1,0:T(8,128)(2,1)}, u32[]{:S(2)}, u32[]{:S(2)}) collective-permute-start(bf16[448,1024]{1,0:T(8,128)(2,1)} %get-tuple-element.117), channel_id=1, source_target_pairs={{1,0},{2,1},{3,2},{5,4},{6,5},{7,6},{9,8},{10,9},{11,10},{13,12},{... | collective-permute-start | bytes 2752520 | tf_op jit(solution)/shard_map/ppermute | solution.py:303
  212.3 39.7 %collective-permute-start.10 = (bf16[2,448,1024]{2,1,0:T(8,128)(2,1)S(1)}, bf16[2,448,1024]{2,1,0:T(8,128)(2,1)}, u32[]{:S(2)}, u32[]{:S(2)}) collective-permute-start(bf16[2,448,1024]{2,1,0:T(8,128)(2,1)S(1)} %pad_maximum_fusion.1.refs_0_.refs_11_.refs_13_.refs_16_.refs_4_), channel_id=1, source_target_pairs={{1,0},{2,1},{3,2},{5,4},{6,5},{7,6},{9,8},{10,9},{11,10},{13,12},{... | collective-permute-start | bytes 5505032 | tf_op jit(solution)/shard_map/ppermute | solution.py:332
  217.7 39.6 %collective-permute-start.11 = (bf16[2,448,1024]{2,1,0:T(8,128)(2,1)S(1)}, bf16[2,448,1024]{2,1,0:T(8,128)(2,1)}, u32[]{:S(2)}, u32[]{:S(2)}) collective-permute-start(bf16[2,448,1024]{2,1,0:T(8,128)(2,1)S(1)} %pad_maximum_fusion.1.refs_0_.refs_11_.refs_13_.refs_16_.refs_4_), channel_id=1, source_target_pairs={{0,1},{1,2},{2,3},{4,5},{5,6},{6,7},{8,9},{9,10},{10,11},{12,13},{... | collective-permute-start | bytes 5505032 | tf_op jit(solution)/shard_map/ppermute | solution.py:331
  218.9 62.9 %collective-permute-start.12 = (bf16[2,448,1024]{2,1,0:T(8,128)(2,1)S(1)}, bf16[2,448,1024]{2,1,0:T(8,128)(2,1)}, u32[]{:S(2)}, u32[]{:S(2)}) collective-permute-start(bf16[2,448,1024]{2,1,0:T(8,128)(2,1)S(1)} %pad_maximum_fusion.1.refs_0_.refs_11_.refs_13_.refs_16_.refs_4_), channel_id=1, source_target_pairs={{0,8},{4,12},{8,16},{12,20},{16,24},{20,28},{24,0},{28,4},{1,9},{5... | collective-permute-start | bytes 5505032 | tf_op jit(solution)/shard_map/ppermute | solution.py:350
  283.6 33.7 %collective-permute-start.17 = (bf16[2,448,1024]{2,1,0:T(8,128)(2,1)S(1)}, bf16[2,448,1024]{2,1,0:T(8,128)(2,1)S(1)}, u32[]{:S(2)}, u32[]{:S(2)}) collective-permute-start(bf16[2,448,1024]{2,1,0:T(8,128)(2,1)S(1)} %broadcast_select_fusion.3), channel_id=1, source_target_pairs={{0,4},{4,0},{8,12},{12,8},{16,20},{20,16},{24,28},{28,24},{1,5},{5... | collective-permute-start | bytes 5505032 | tf_op jit(solution)/shard_map/ppermute | solution.py:346
  288.1 29.1 %collective-permute-start.13 = (bf16[2,448,1024]{2,1,0:T(8,128)(2,1)}, bf16[2,448,1024]{2,1,0:T(8,128)(2,1)S(1)}, u32[]{:S(2)}, u32[]{:S(2)}) collective-permute-start(bf16[2,448,1024]{2,1,0:T(8,128)(2,1)} %collective-permute-done.10.refs_1_), channel_id=1, source_target_pairs={{1,0},{2,1},{5,4},{6,5},{9,8},{10,9},{13,12},{14,13},{17,16},{18,1... | collective-permute-start | bytes 5505032 | tf_op jit(solution)/shard_map/ppermute | solution.py:332
  288.9 47.1 %collective-permute-start.14 = (bf16[2,448,1024]{2,1,0:T(8,128)(2,1)}, bf16[2,448,1024]{2,1,0:T(8,128)(2,1)S(1)}, u32[]{:S(2)}, u32[]{:S(2)}) collective-permute-start(bf16[2,448,1024]{2,1,0:T(8,128)(2,1)} %collective-permute-done.11.refs_2_.refs_3_), channel_id=1, source_target_pairs={{1,2},{2,3},{5,6},{6,7},{9,10},{10,11},{13,14},{14,15},{17,18},{18... | collective-permute-start | bytes 5505032 | tf_op jit(solution)/shard_map/ppermute | solution.py:331
  290.2 45.8 %collective-permute-start.18 = (bf16[2,448,1024]{2,1,0:T(8,128)(2,1)S(1)}, bf16[2,448,1024]{2,1,0:T(8,128)(2,1)S(1)}, u32[]{:S(2)}, u32[]{:S(2)}) collective-permute-start(bf16[2,448,1024]{2,1,0:T(8,128)(2,1)S(1)} %pad_maximum_fusion.1.refs_0_.refs_11_.refs_13_.refs_16_.refs_4_), channel_id=1, source_target_pairs={{0,16},{4,20},{8,24},{12,28},{16,0},{20,4},{24,8},{28,12},{1,17},{... | collective-permute-start | bytes 5505032 | tf_op jit(solution)/shard_map/ppermute | solution.py:350
  290.5 26.8 %collective-permute-start.16 = (bf16[448,1024]{1,0:T(8,128)(2,1)S(1)}, bf16[448,1024]{1,0:T(8,128)(2,1)S(1)}, u32[]{:S(2)}, u32[]{:S(2)}) collective-permute-start(bf16[448,1024]{1,0:T(8,128)(2,1)S(1)} %convert_element_type.106), channel_id=1, source_target_pairs={{3,2},{7,6},{11,10},{15,14},{19,18},{23,22},{27,26},{31,30}} | collective-permute-start | bytes 2752520 | tf_op jit(solution)/shard_map/ppermute | solution.py:303
  337.3 30.1 %collective-permute-start.23 = (bf16[2,448,1024]{2,1,0:T(8,128)(2,1)S(1)}, bf16[2,448,1024]{2,1,0:T(8,128)(2,1)S(1)}, u32[]{:S(2)}, u32[]{:S(2)}) collective-permute-start(bf16[2,448,1024]{2,1,0:T(8,128)(2,1)S(1)} %broadcast_select_fusion.2), channel_id=1, source_target_pairs={{0,4},{4,0},{8,12},{12,8},{16,20},{20,16},{24,28},{28,24},{1,5},{5... | collective-permute-start | bytes 5505032 | tf_op jit(solution)/shard_map/ppermute | solution.py:346
  340.0 27.5 %collective-permute-start.19 = (bf16[2,448,1024]{2,1,0:T(8,128)(2,1)S(1)}, bf16[2,448,1024]{2,1,0:T(8,128)(2,1)S(1)}, u32[]{:S(2)}, u32[]{:S(2)}) collective-permute-start(bf16[2,448,1024]{2,1,0:T(8,128)(2,1)S(1)} %collective-permute-done.13.refs_4_.refs_6_), channel_id=1, source_target_pairs={{1,0},{5,4},{9,8},{13,12},{17,16},{21,20},{25,24},{29,28}} | collective-permute-start | bytes 5505032 | tf_op jit(solution)/shard_map/ppermute | solution.py:332
  340.8 43.5 %collective-permute-start.20 = (bf16[2,448,1024]{2,1,0:T(8,128)(2,1)S(1)}, bf16[2,448,1024]{2,1,0:T(8,128)(2,1)S(1)}, u32[]{:S(2)}, u32[]{:S(2)}) collective-permute-start(bf16[2,448,1024]{2,1,0:T(8,128)(2,1)S(1)} %collective-permute-done.14.refs_5_.refs_7_), channel_id=1, source_target_pairs={{2,3},{6,7},{10,11},{14,15},{18,19},{22,23},{26,27},{30,31}} | collective-permute-start | bytes 5505032 | tf_op jit(solution)/shard_map/ppermute | solution.py:331
  343.4 24.1 %collective-permute-start.22 = (bf16[448,1024]{1,0:T(8,128)(2,1)S(1)}, bf16[448,1024]{1,0:T(8,128)(2,1)S(1)}, u32[]{:S(2)}, u32[]{:S(2)}) collective-permute-start(bf16[448,1024]{1,0:T(8,128)(2,1)S(1)} %get-tuple-element.131), channel_id=1, source_target_pairs={{2,1},{3,2},{6,5},{7,6},{10,9},{11,10},{14,13},{15,14},{18,17},{19... | collective-permute-start | bytes 2752520 | tf_op jit(solution)/shard_map/ppermute | solution.py:303
  385.6 23.2 %collective-permute-start.24 = (bf16[448,1024]{1,0:T(8,128)(2,1)S(1)}, bf16[448,1024]{1,0:T(8,128)(2,1)S(1)}, u32[]{:S(2)}, u32[]{:S(2)}) collective-permute-start(bf16[448,1024]{1,0:T(8,128)(2,1)S(1)} %add_convert_fusion.1), channel_id=1, source_target_pairs={{0,1},{1,2},{2,3},{4,5},{5,6},{6,7},{8,9},{9,10},{10,11},{12,13},{... | collective-permute-start | bytes 2752520 | tf_op jit(solution)/shard_map/ppermute | solution.py:302
  387.5 22.5 %collective-permute-start.25 = (bf16[448,1024]{1,0:T(8,128)(2,1)S(1)}, bf16[448,1024]{1,0:T(8,128)(2,1)S(1)}, u32[]{:S(2)}, u32[]{:S(2)}) collective-permute-start(bf16[448,1024]{1,0:T(8,128)(2,1)S(1)} %add_convert_fusion), channel_id=1, source_target_pairs={{1,0},{2,1},{3,2},{5,4},{6,5},{7,6},{9,8},{10,9},{11,10},{13,12},{... | collective-permute-start | bytes 2752520 | tf_op jit(solution)/shard_map/ppermute | solution.py:303
  412.7 42.7 %collective-permute-start.26 = (bf16[2,448,1024]{2,1,0:T(8,128)(2,1)}, bf16[2,448,1024]{2,1,0:T(8,128)(2,1)}, u32[]{:S(2)}, u32[]{:S(2)}) collective-permute-start(bf16[2,448,1024]{2,1,0:T(8,128)(2,1)} %pad_maximum_fusion.2.refs_10_.refs_12_.refs_14_.refs_17_.refs_5_), channel_id=1, source_target_pairs={{0,1},{1,2},{2,3},{4,5},{5,6},{6,7},{8,9},{9,10},{10,11},{12,13},{... | collective-permute-start | bytes 5505032 | tf_op jit(solution)/shard_map/ppermute | solution.py:331
  414.0 42.3 %collective-permute-start.27 = (bf16[2,448,1024]{2,1,0:T(8,128)(2,1)}, bf16[2,448,1024]{2,1,0:T(8,128)(2,1)}, u32[]{:S(2)}, u32[]{:S(2)}) collective-permute-start(bf16[2,448,1024]{2,1,0:T(8,128)(2,1)} %pad_maximum_fusion.2.refs_10_.refs_12_.refs_14_.refs_17_.refs_5_), channel_id=1, source_target_pairs={{1,0},{2,1},{3,2},{5,4},{6,5},{7,6},{9,8},{10,9},{11,10},{13,12},{... | collective-permute-start | bytes 5505032 | tf_op jit(solution)/shard_map/ppermute | solution.py:332
  420.0 40.6 %collective-permute-start.28 = (bf16[2,448,1024]{2,1,0:T(8,128)(2,1)}, bf16[2,448,1024]{2,1,0:T(8,128)(2,1)}, u32[]{:S(2)}, u32[]{:S(2)}) collective-permute-start(bf16[2,448,1024]{2,1,0:T(8,128)(2,1)} %pad_maximum_fusion.2.refs_10_.refs_12_.refs_14_.refs_17_.refs_5_), channel_id=1, source_target_pairs={{0,8},{4,12},{8,16},{12,20},{16,24},{20,28},{24,0},{28,4},{1,9},{5... | collective-permute-start | bytes 5505032 | tf_op jit(solution)/shard_map/ppermute | solution.py:350
  463.6 40.1 %collective-permute-start.31 = (bf16[2,448,1024]{2,1,0:T(8,128)(2,1)}, bf16[2,448,1024]{2,1,0:T(8,128)(2,1)}, u32[]{:S(2)}, u32[]{:S(2)}) collective-permute-start(bf16[2,448,1024]{2,1,0:T(8,128)(2,1)} %broadcast_select_fusion.1), channel_id=1, source_target_pairs={{0,4},{4,0},{8,12},{12,8},{16,20},{20,16},{24,28},{28,24},{1,5},{5... | collective-permute-start | bytes 5505032 | tf_op jit(solution)/shard_map/ppermute | solution.py:346
  466.8 36.9 %collective-permute-start.29 = (bf16[2,448,1024]{2,1,0:T(8,128)(2,1)}, bf16[2,448,1024]{2,1,0:T(8,128)(2,1)}, u32[]{:S(2)}, u32[]{:S(2)}) collective-permute-start(bf16[2,448,1024]{2,1,0:T(8,128)(2,1)} %collective-permute-done.27.refs_11_), channel_id=1, source_target_pairs={{1,0},{2,1},{5,4},{6,5},{9,8},{10,9},{13,12},{14,13},{17,16},{18,1... | collective-permute-start | bytes 5505032 | tf_op jit(solution)/shard_map/ppermute | solution.py:332
  468.7 45.4 %collective-permute-start.30 = (bf16[2,448,1024]{2,1,0:T(8,128)(2,1)}, bf16[2,448,1024]{2,1,0:T(8,128)(2,1)}, u32[]{:S(2)}, u32[]{:S(2)}) collective-permute-start(bf16[2,448,1024]{2,1,0:T(8,128)(2,1)} %collective-permute-done.26.refs_12_.refs_13_), channel_id=1, source_target_pairs={{1,2},{2,3},{5,6},{6,7},{9,10},{10,11},{13,14},{14,15},{17,18},{18... | collective-permute-start | bytes 5505032 | tf_op jit(solution)/shard_map/ppermute | solution.py:331
  470.0 44.1 %collective-permute-start.32 = (bf16[2,448,1024]{2,1,0:T(8,128)(2,1)}, bf16[2,448,1024]{2,1,0:T(8,128)(2,1)}, u32[]{:S(2)}, u32[]{:S(2)}) collective-permute-start(bf16[2,448,1024]{2,1,0:T(8,128)(2,1)} %pad_maximum_fusion.2.refs_10_.refs_12_.refs_14_.refs_17_.refs_5_), channel_id=1, source_target_pairs={{0,16},{4,20},{8,24},{12,28},{16,0},{20,4},{24,8},{28,12},{1,17},{... | collective-permute-start | bytes 5505032 | tf_op jit(solution)/shard_map/ppermute | solution.py:350
  515.8 49.4 %collective-permute-start.35 = (bf16[2,448,1024]{2,1,0:T(8,128)(2,1)S(1)}, bf16[2,448,1024]{2,1,0:T(8,128)(2,1)S(1)}, u32[]{:S(2)}, u32[]{:S(2)}) collective-permute-start(bf16[2,448,1024]{2,1,0:T(8,128)(2,1)S(1)} %broadcast_select_fusion), channel_id=1, source_target_pairs={{0,4},{4,0},{8,12},{12,8},{16,20},{20,16},{24,28},{28,24},{1,5},{5... | collective-permute-start | bytes 5505032 | tf_op jit(solution)/shard_map/ppermute | solution.py:346
  516.7 70.6 %collective-permute-start.33 = (bf16[2,448,1024]{2,1,0:T(8,128)(2,1)}, bf16[2,448,1024]{2,1,0:T(8,128)(2,1)S(1)}, u32[]{:S(2)}, u32[]{:S(2)}) collective-permute-start(bf16[2,448,1024]{2,1,0:T(8,128)(2,1)} %collective-permute-done.29.refs_14_.refs_0_), channel_id=1, source_target_pairs={{1,0},{5,4},{9,8},{13,12},{17,16},{21,20},{25,24},{29,28}} | collective-permute-start | bytes 5505032 | tf_op jit(solution)/shard_map/ppermute | solution.py:332
  517.4 69.9 %collective-permute-start.34 = (bf16[2,448,1024]{2,1,0:T(8,128)(2,1)}, bf16[2,448,1024]{2,1,0:T(8,128)(2,1)S(1)}, u32[]{:S(2)}, u32[]{:S(2)}) collective-permute-start(bf16[2,448,1024]{2,1,0:T(8,128)(2,1)} %collective-permute-done.30.refs_15_.refs_1_), channel_id=1, source_target_pairs={{2,3},{6,7},{10,11},{14,15},{18,19},{22,23},{26,27},{30,31}} | collective-permute-start | bytes 5505032 | tf_op jit(solution)/shard_map/ppermute | solution.py:331
  (32 other events, 666.3 us)
Sparse Core Ops, SparseCore 0:
  23.4 77.8 all-gather.1

commit v4 on v3

--- a/solution.py
+++ b/solution.py
@@ -1,6 +1,7 @@
 import functools
 import jax
 import jax.numpy as jnp
+import numpy as np
 from jax import lax
 from jax.experimental import pallas as pl
 from jax.experimental.pallas import tpu as pltpu
@@ -11,10 +12,10 @@
 CONTRACT_LAST = (((1,), (1,)), ((), ()))
 
 
-def hidden_kernel(count, table_ref, weight_ref, features_ref, out_ref):
+def hidden_kernel(base, table_ref, weight_ref, features_ref, out_ref):
     groups, per_group, local_tokens, local_features = features_ref.shape
     for g in range(groups):
-        place = table_ref[count + g]
+        place = table_ref[base + g]
         total = None
         for q in range(per_group):
             part = lax.dot_general(
@@ -27,29 +28,24 @@
         out_ref[0, :, g * local_tokens : (g + 1) * local_tokens] = total
 
 
-def hidden_parts(weight, features, chunk, chunk_rows, offsets, own_group):
+def hidden_parts(weight, features, chunk_rows, table, base, count):
     groups, per_group, local_tokens, local_features = features.shape
     width = weight.shape[1]
     tokens = groups * local_tokens
-    count = len(offsets)
-    table = jnp.stack(
-        [(own_group + offset) % groups * CHUNKS + chunk for offset in offsets]
-        + [(own_group + g) % groups for g in range(groups)]
-    ).astype(jnp.int32)
     return pl.pallas_call(
-        functools.partial(hidden_kernel, count),
+        functools.partial(hidden_kernel, base + count),
         grid_spec=pltpu.PrefetchScalarGridSpec(
             num_scalar_prefetch=1,
             grid=(count,),
             in_specs=[
-                pl.BlockSpec((chunk_rows, width), lambda i, table_ref: (table_ref[i], 0)),
+                pl.BlockSpec((chunk_rows, width), lambda i, table_ref: (table_ref[base + i], 0)),
                 pl.BlockSpec(features.shape, lambda i, table_ref: (0, 0, 0, 0)),
             ],
             out_specs=pl.BlockSpec((1, chunk_rows, tokens), lambda i, table_ref: (i, 0, 0)),
         ),
         out_shape=jax.ShapeDtypeStruct((count, chunk_rows, tokens), jnp.float32),
         compiler_params=pltpu.CompilerParams(
-            dimension_semantics=("arbitrary",), vmem_limit_bytes=32 * 2**20
+            dimension_semantics=("arbitrary",), vmem_limit_bytes=56 * 2**20
         ),
         cost_estimate=pl.CostEstimate(
             flops=2 * count * chunk_rows * tokens * width,
@@ -59,7 +55,7 @@
     )(table, weight, features)
 
 
-def factor_kernel(shape, candidates, plan, scale, table_ref, *refs):
+def factor_kernel(shape, candidates, plan, base, scale, table_ref, *refs):
     partners, chunk_total, chunk_rows = shape
     total = len(plan)
     row_refs = refs[: sum(candidates)]
@@ -71,7 +67,7 @@
     stride = 2 * lane_tiles
     step = pl.program_id(0)
     current = jnp.minimum(step, total - 1)
-    slot, buffer = table_ref[2 * total + current], table_ref[3 * total + current]
+    slot, buffer = table_ref[base + 2 * total + current], table_ref[base + 3 * total + current]
     loads = [i for i in range(total) if i == 0 or plan[i][0] != plan[i - 1][0]]
     firsts = {}
     for i, (_, k) in enumerate(plan):
@@ -92,7 +88,7 @@
         first = sum(candidates[:piece])
         for choice in range(candidates[piece]):
 
-            @pl.when(table_ref[4 * total + piece] == choice)
+            @pl.when(table_ref[base + 4 * total + piece] == choice)
             def _():
                 row_copy(row_refs[first + choice], load % 2).start()
 
@@ -149,31 +145,29 @@
         lay_out(wides[(total - 1) % 2])
 
 
-def factor_rows(pieces, columns, plan, previous, band, slices, scale):
-    used = sorted(pieces)
+def factor_table(plan, used, keys, positions, choices):
+    buffers = [0]
+    for last, now in zip(plan, plan[1:]):
+        buffers.append(buffers[-1] if last[0] == now[0] else 1 - buffers[-1])
+    return (
+        [positions[piece] for piece, _ in plan]
+        + [k for _, k in plan]
+        + [keys.index(k) for _, k in plan]
+        + buffers
+        + [choices[piece] for piece in used]
+    )
+
+
+def factor_rows(pieces, columns, plan, table, base, previous, band, slices, scale):
+    used, keys = sorted(pieces), sorted(columns)
     plan = [(used.index(piece), k) for piece, k in plan]
     pieces = [pieces[piece] for piece in used]
-    keys = sorted({k for _, k in plan})
-    _, chunk_rows, tokens = pieces[0][0][0].shape
-    dtype = pieces[0][0][0].dtype
+    _, chunk_rows, tokens = pieces[0][0].shape
+    dtype = pieces[0][0].dtype
     chunk_total = len(columns[keys[0]])
     slice_width = chunk_total * chunk_rows
     height = chunk_rows * 2 * (slice_width // LANES)
-    buffers, last = [], None
-    for piece, _ in plan:
-        if not buffers:
-            buffers.append(0)
-        else:
-            buffers.append(buffers[-1] if piece == last else 1 - buffers[-1])
-        last = piece
-    table = jnp.stack(
-        [jnp.int32(pieces[piece][2]) for piece, _ in plan]
-        + [jnp.int32(k) for _, k in plan]
-        + [jnp.int32(keys.index(k)) for _, k in plan]
-        + [jnp.int32(buffer) for buffer in buffers]
-        + [jnp.int32(choice) for _, choice, _ in pieces]
-    )
-    operands = [array for arrays, _, _ in pieces for array in arrays]
+    operands = [array for arrays in pieces for array in arrays]
     operands += [part for k in keys for part in columns[k]]
     aliases = {}
     if previous is not None:
@@ -183,14 +177,15 @@
 
     def placed(step, table_ref):
         done = jnp.maximum(step - 1, 0)
-        return table_ref[total + done], table_ref[done], 0
+        return table_ref[base + total + done], table_ref[base + done], 0
 
     return pl.pallas_call(
         functools.partial(
             factor_kernel,
             (len(keys), chunk_total, chunk_rows),
-            tuple(len(arrays) for arrays, _, _ in pieces),
+            tuple(len(arrays) for arrays in pieces),
             tuple((piece, keys.index(k)) for piece, k in plan),
+            base,
             scale,
         ),
         grid_spec=pltpu.PrefetchScalarGridSpec(
@@ -261,40 +256,56 @@
         for g in range(groups)
     ]
     sent = lax.ppermute(cotangent, ("tensor", "dp"), to_plane)
-    sent, gate_pre, up_pre = tie(sent, gate_pre, up_pre)
+    saved = jnp.stack([gate_pre.T, up_pre.T])
+    sent, saved = tie(sent, saved)
     features = lax.all_gather(sent, "tensor", axis=0, tiled=True)
 
-    saved = jnp.stack([gate_pre, up_pre])
-
-    def saved_slice(index):
-        return lax.dynamic_slice_in_dim(saved, (index % groups) * slice_width, slice_width, 2)
-
-    saved_pieces = [saved_slice(own_group)]
-    for shift in range(1, groups):
-        ring = [(d, (d + shift) % groups) for d in range(groups)]
-        saved_pieces.append(lax.ppermute(saved_slice(own_group + shift), "dp", ring))
-    features, *saved_pieces = tie(features, *saved_pieces)
+    def saved_pieces(chunk, saved):
+        def part(index):
+            first = (index % groups) * slice_width + chunk * chunk_rows
+            return lax.dynamic_slice_in_dim(saved, first, chunk_rows, 1)
+
+        pieces = [part(own_group)]
+        for shift in range(1, groups):
+            ring = [(d, (d + shift) % groups) for d in range(groups)]
+            pieces.append(lax.ppermute(part(own_group + shift), "dp", ring))
+        return pieces
+
+    def order_saved(pieces):
+        pieces = jnp.stack(pieces)
+        return jnp.concatenate(
+            [
+                lax.dynamic_index_in_dim(pieces, (own_group - h) % groups, 0, keepdims=False)
+                for h in range(groups)
+            ],
+            axis=2,
+        )
+
+    first_saved = saved_pieces(0, saved)
+    features, saved, *first_saved = tie(features, saved, *first_saved)
     features = features.reshape(groups, per_group, local_tokens, local_features)
 
     def partial_products(chunk, offsets, features):
         if use_kernels:
-            made = hidden_parts(down_weight, features, chunk, chunk_rows, offsets, own_group)
-            return {offset: made[place] for place, offset in enumerate(offsets)}
+            base = bases["hidden", chunk, offsets]
+            return hidden_parts(down_weight, features, chunk_rows, table, base, len(offsets))
         ordered = jnp.roll(features, -own_group, axis=0)
-        made = {}
+        made = []
         for offset in offsets:
             first = (own_group + offset) % groups * slice_width + chunk * chunk_rows
             part = lax.dynamic_slice_in_dim(down_weight, first, chunk_rows, 0)
-            made[offset] = jnp.einsum(
-                "uqw,gqtw->ugt",
-                part.reshape(chunk_rows, per_group, local_features),
-                ordered,
-                preferred_element_type=jnp.float32,
-            ).reshape(chunk_rows, all_tokens)
-        return made
+            made.append(
+                jnp.einsum(
+                    "uqw,gqtw->ugt",
+                    part.reshape(chunk_rows, per_group, local_features),
+                    ordered,
+                    preferred_element_type=jnp.float32,
+                ).reshape(chunk_rows, all_tokens)
+            )
+        return jnp.stack(made)
 
     def reduce_step(partial, step, received):
-        right, left = partial[groups - step], partial[step]
+        right, left = partial(groups - step), partial(step)
         if received is not None:
             right = right + received[0].astype(jnp.float32)
             left = left + received[1].astype(jnp.float32)
@@ -307,19 +318,9 @@
             ),
         )
 
-    def order_saved(pieces):
-        pieces = jnp.stack(pieces)
-        return jnp.concatenate(
-            [
-                lax.dynamic_index_in_dim(pieces, (own_group - h) % groups, 0, keepdims=False)
-                for h in range(groups)
-            ],
-            axis=1,
-        ).transpose(0, 2, 1)
-
-    def gradients(partial, received, saved_all, chunk):
-        hidden_cot = partial[0] + received[0].astype(jnp.float32) + received[1].astype(jnp.float32)
-        local = saved_all[:, chunk * chunk_rows : (chunk + 1) * chunk_rows].astype(jnp.float32)
+    def gradients(partial, received, saved):
+        hidden_cot = partial(0) + received[0].astype(jnp.float32) + received[1].astype(jnp.float32)
+        local = saved.astype(jnp.float32)
         gate_value, up_value = local[0], local[1]
         sigmoid_gate = jax.nn.sigmoid(gate_value)
         grad_gate = hidden_cot * up_value * sigmoid_gate * (1.0 + gate_value * (1.0 - sigmoid_gate))
@@ -360,7 +361,7 @@
     for place, k in enumerate(shifts):
         ready[k] = place // share + 1
     for k in range(1, half_band, 2):
-        ready[k] = max(ready[k - 1], ready[k + 1]) + 0.5
+        ready[k] = max(ready[k - 1], ready[k + 1]) + 1
     calls = {}
     for k in sorted(ready, key=ready.get):
         for chunk in range(CHUNKS):
@@ -370,50 +371,86 @@
                     came = max(order[d][place - 1][0] for d in range(groups))
                 calls.setdefault(max(ready[k], came), []).append(((chunk, place), k))
 
-    def by_plane(values):
-        return jnp.asarray(values, jnp.int32)[own_group]
-
-    def row_piece(chunk, place):
+    def row_arrays(chunk, place):
         own, held = rows[chunk]
         if place == 0:
-            return [own], 0, own_group * CHUNKS + chunk
-        wanted = [order[d][place - 1] for d in range(groups)]
-        kinds = sorted(set(wanted))
-        origin = [d - hops if left else d + hops for d, (hops, left) in enumerate(wanted)]
-        return (
-            [held[hops][int(left)] for hops, left in kinds],
-            by_plane([kinds.index(kind) for kind in wanted]),
-            by_plane(origin) * CHUNKS + chunk,
-        )
-
-    def multiply(since, until, result):
-        for time in sorted(calls):
-            if since <= time < until:
-                plan = calls[time]
-                pieces = {piece: row_piece(*piece) for piece, _ in plan}
-                keys = {k for _, k in plan}
-                parts = {k: [columns[c][k] for c in range(CHUNKS)] for k in keys}
-                result = factor_rows(pieces, parts, plan, result, band, groups, inverse_count)
-        return result
-
-    first_offsets = sorted({1, groups - 1})
-    other_offsets = [offset for offset in range(groups) if offset not in first_offsets]
-    partial = partial_products(0, first_offsets, features)
-    received = reduce_step(partial, 1, None)
-    partial.update(partial_products(0, other_offsets, features))
-    received = tie(*received, *saved_pieces)
-    received, saved_pieces = received[:2], received[2:]
-    saved_all = order_saved(saved_pieces)
-    for step in range(2, groups):
+            return [own]
+        kinds = sorted({order[d][place - 1] for d in range(groups)})
+        return [held[hops][int(left)] for hops, left in kinds]
+
+    def row_entry(d, chunk, place):
+        if place == 0:
+            return d * CHUNKS + chunk, 0
+        kinds = sorted({order[e][place - 1] for e in range(groups)})
+        hops, left = order[d][place - 1]
+        return (d - hops if left else d + hops) * CHUNKS + chunk, kinds.index((hops, left))
+
+    first_offsets = tuple(sorted({1, groups - 1}))
+    other_offsets = tuple(o for o in range(groups) if o not in first_offsets)
+    all_offsets = tuple(range(groups))
+    hidden_calls = [(0, first_offsets), (0, other_offsets)]
+    hidden_calls += [(chunk, all_offsets) for chunk in range(1, CHUNKS)]
+    bases, lines = {}, [[] for _ in range(groups)]
+    for chunk, offsets in hidden_calls:
+        bases["hidden", chunk, offsets] = len(lines[0])
+        for d in range(groups):
+            lines[d] += [(d + offset) % groups * CHUNKS + chunk for offset in offsets]
+            lines[d] += [(d + g) % groups for g in range(groups)]
+    for time, plan in calls.items():
+        bases["factor", time] = len(lines[0])
+        used = sorted({piece for piece, _ in plan})
+        keys = sorted({k for _, k in plan})
+        for d in range(groups):
+            entries = [row_entry(d, *piece) for piece in used]
+            lines[d] += factor_table(
+                [(used.index(piece), k) for piece, k in plan],
+                list(range(len(used))),
+                keys,
+                [position for position, _ in entries],
+                [choice for _, choice in entries],
+            )
+    table = lax.dynamic_index_in_dim(
+        jnp.asarray(np.array(lines, np.int32)), own_group, 0, keepdims=False
+    )
+
+    def multiply(time, result):
+        if time not in calls:
+            return result
+        plan = calls[time]
+        pieces = {piece: row_arrays(*piece) for piece, _ in plan}
+        parts = {k: [columns[c][k] for c in range(CHUNKS)] for _, k in plan}
+        base = bases["factor", time]
+        return factor_rows(
+            pieces, parts, plan, table, base, result, band, groups, inverse_count
+        )
+
+    def lookup(*made):
+        return lambda offset: next(
+            array[offsets.index(offset)] for offsets, array in made if offset in offsets
+        )
+
+    first_parts = partial_products(0, first_offsets, features)
+    other_parts = partial_products(0, other_offsets, features)
+    partial = lookup((first_offsets, first_parts), (other_offsets, other_parts))
+    later_saved = [saved_pieces(chunk, saved) for chunk in range(1, CHUNKS)]
+    received = None
+    for step in range(1, groups):
         received = tie(*reduce_step(partial, step, received))
+        if step == groups - 2:
+            moved = tie(*received, *[piece for pieces in later_saved for piece in pieces])
+            received, moved = moved[:2], moved[2:]
+            later_saved = [
+                list(moved[c * groups : (c + 1) * groups]) for c in range(CHUNKS - 1)
+            ]
+    all_saved = [order_saved(pieces) for pieces in [first_saved, *later_saved]]
     rows, columns, result = [], [], None
     for chunk in range(CHUNKS):
-        own = gradients(partial, received, saved_all, chunk)
+        own = gradients(partial, received, all_saved[chunk])
         own, features = tie(own, features)
         later = chunk + 1 < CHUNKS
-        partial, received = {}, ()
+        received = ()
         if later:
-            partial = partial_products(chunk + 1, list(range(groups)), features)
+            parts = partial_products(chunk + 1, all_offsets, features)
         held, column, found = {}, {0: own}, {0: own}
         rows.append((own, held))
         columns.append(column)
@@ -427,24 +464,25 @@
             column.update(made)
             found.update(made)
             if use_kernels and not later:
-                result = multiply(step - 1.5, step - 0.5, result)
+                result = multiply(step - 1, result)
             if step < groups - 1 or later:
-                keys, offsets = list(found), list(partial) if step == 1 else []
-                moved = tie(
-                    left, right, *received, *[found[k] for k in keys], *[partial[o] for o in offsets]
-                )
+                keys = list(found)
+                new_parts = [parts] if later and step == 1 else []
+                moved = tie(left, right, *received, *[found[k] for k in keys], *new_parts)
                 left, right = moved[:2]
                 moved = moved[2:]
                 received, moved = moved[: len(received)], moved[len(received) :]
                 found = dict(zip(keys, moved))
-                partial.update(zip(offsets, moved[len(keys) :]))
+                if new_parts:
+                    partial = lookup((all_offsets, moved[-1]))
                 if result is not None:
                     result, left, right = tie(result, left, right)
+        column.update(partner_step(groups, found))
         if later:
             received = reduce_step(partial, groups - 1, received)
 
     if use_kernels:
-        result = multiply(groups - 1.5, groups, result)
+        result = multiply(groups - 1, result)
         result = result.reshape(band, -1, 2, LANES).transpose(2, 0, 1, 3)
     else:
 

time: 626 us -> 618 us (0.987)
  local copies, waits for them, and re-layouts: 51.3 us -> 28.4 us
  starting transfers between devices: 94.8 us -> 108 us
    all_gather x1, waiting for transfers between devices: 0.01 us -> 20.8 us  [per_device(): features = lax.all_gather(sent, 'tensor', axis=0, tiled=True)]
    ppermute x6, waiting for transfers between devices: 62.1 us -> 43.3 us  [reduce_step(): lax.ppermute(left.astype(jnp.bfloat16), 'dp', [(d, d - 1) for d in range(...]
    ppermute x4, waiting for transfers between devices: 29 us -> 47.6 us  [partner_step(): lax.ppermute(found[0], 'tensor', [(t, (t + k) % blocks) for t in range(bl...]
    unnamed x54, local copies, waits for them, and re-layouts: 22.8 us -> 6.17 us
    another operation x20 -> x0, local copies, waits for them, and re-layouts: 15.1 us -> none  [the longest x6 14.8 us: factor_rows(): jnp.stack([jnp.int32(pieces[piece][2]) for piece, _ in plan] + [jnp.int32...]
    ppermute x6, waiting for transfers between devices: 14 us -> 1.24 us  [gather_step(): lax.ppermute(right, 'dp', [(d, d - 1) for d in range(1, groups - step + 1)])]
    pallas_call x6 -> x4, Pallas kernels: 124 us -> 112 us  [factor_rows(): pl.pallas_call(functools.partial(factor_kernel, (len(keys), chunk_total,...]
    pallas_call x3, Pallas kernels: 20 us -> 31 us  [hidden_parts(): pl.pallas_call(functools.partial(hidden_kernel, base + count), grid_spec=...]
  transfers between devices with their start and end apart: 37 -> 40, of which waited for: 20 -> 24; matrix products, arithmetic and copies ran while one was open for 6% -> 5% of each run, Pallas kernels for 19% -> 17%
where the time goes in v4:
time: 618 us; the launch traced here: 607 us
  waiting for transfers between devices  281 us (45%)
  Pallas kernels  143 us (23%)
  starting transfers between devices  108 us (17%)
  other arithmetic  31.7 us (5%)
  local copies, waits for them, and re-layouts  28.4 us (5%)
  between operations  14.6 us (2%)
    pallas_call x4, Pallas kernels, factor_rows(): pl.pallas_call(functools.partial(factor_kernel, (len(keys), chunk_total,...  112 us
    ppermute x6, waiting for transfers between devices, gather_step(): lax.ppermute(left, 'dp', [(d, d + 1) for d in range(step - 1, groups - 1)])  72.9 us
    ppermute x6, waiting for transfers between devices, saved_pieces(): pieces.append(lax.ppermute(part(own_group + shift), 'dp', ring))  70.3 us
    ppermute x4, waiting for transfers between devices, partner_step(): lax.ppermute(found[0], 'tensor', [(t, (t + k) % blocks) for t in range(bl...  47.6 us
    ppermute x6, waiting for transfers between devices, reduce_step(): lax.ppermute(left.astype(jnp.bfloat16), 'dp', [(d, d - 1) for d in range(...  43.3 us
    ppermute x6, starting transfers between devices, reduce_step(): lax.ppermute(left.astype(jnp.bfloat16), 'dp', [(d, d - 1) for d in range(...  34.4 us
    pallas_call x3, Pallas kernels, hidden_parts(): pl.pallas_call(functools.partial(hidden_kernel, base + count), grid_spec=...  31 us
    all_gather x1, waiting for transfers between devices, per_device(): features = lax.all_gather(sent, 'tensor', axis=0, tiled=True)  20.8 us
  transfers between devices with their start and end apart: 40, of which 24 were waited for; matrix products, arithmetic and copies ran while one was open for 5% of the time, Pallas kernels for 17%

profile of v4, /device:TPU:29, one launch (start us, length us, event | category | flops | bytes accessed | tf_op | source)
XLA Modules:
  0.0 606.7 jit_solution(8604865482415890004)
XLA Ops:
  13.7 8.8 %collective-permute-done = bf16[256,1024]{1,0:T(8,128)(2,1)S(1)} collective-permute-done((bf16[256,1024]{1,0:T(8,128)(2,1)}, bf16[256,1024]{1,0:T(8,128)(2,1)S(1)}, u32[]{:S(2)}, u32[]{:S(2)}) %collective-permute-start) | collective-permute-done | bytes 524320 | tf_op jit(solution)/shard_map/ppermute | solution.py:258
  27.0 12.2 %collective-permute-start.2 = (bf16[2,448,256]{1,2,0:T(8,128)(2,1)S(1)}, bf16[2,448,256]{1,2,0:T(8,128)(2,1)S(1)}, u32[]{:S(2)}, u32[]{:S(2)}) collective-permute-start(bf16[2,448,256]{1,2,0:T(8,128)(2,1)S(1)} %get-tuple-element.126), channel_id=1, source_target_pairs={{0,2},{1,3},{2,0},{3,1},{4,6},{5,7},{6,4},{7,5},{8,10},{9,11},{10,... | collective-permute-start | bytes 1376264 | tf_op jit(solution)/shard_map/ppermute | solution.py:271
  41.9 8.0 %collective-permute-done.3 = bf16[2,448,256]{1,2,0:T(8,128)(2,1)S(1)} collective-permute-done((bf16[2,448,256]{1,2,0:T(8,128)(2,1)}, bf16[2,448,256]{1,2,0:T(8,128)(2,1)S(1)}, u32[]{:S(2)}, u32[]{:S(2)}) %collective-permute-start.3) | collective-permute-done | bytes 458784 | tf_op jit(solution)/shard_map/ppermute | solution.py:271
  49.9 24.1 %collective-permute-done.2 = bf16[2,448,256]{1,2,0:T(8,128)(2,1)S(1)} collective-permute-done((bf16[2,448,256]{1,2,0:T(8,128)(2,1)S(1)}, bf16[2,448,256]{1,2,0:T(8,128)(2,1)S(1)}, u32[]{:S(2)}, u32[]{:S(2)}) %collective-permute-start.2) | collective-permute-done | bytes 458784 | tf_op jit(solution)/shard_map/ppermute | solution.py:271
  74.0 20.8 %all-gather.2.cloned.1.call-done = bf16[2048,1024]{1,0:T(8,128)(2,1)} async-done(((bf16[256,1024]{1,0:T(8,128)(2,1)}), bf16[2048,1024]{1,0:T(8,128)(2,1)}) %all-gather.2.cloned.1.call-update) | async-done | bytes 4194320 | tf_op jit(solution)/shard_map/all_gather | solution.py:261
  94.8 8.9 %shard_map.56 = f32[2,448,1024]{2,1,0:T(8,128)} custom-call(s32[206]{0:T(256)} %bitcast.134, bf16[3584,2048]{1,0:T(8,128)(2,1)} %weight_ref.5, bf16[4,2,256,1024]{3,2,1,0:T(8,128)(2,1)} %bitcast.141), custom_call_target="tpu_custom_call" | custom-call | flops 3758096384 | bytes 11534336 | tf_op jit(solution)/shard_map/pallas_call | solution.py:35
  109.1 8.9 %shard_map.55 = f32[2,448,1024]{2,1,0:T(8,128)} custom-call(s32[206]{0:T(256)} %bitcast.135, bf16[3584,2048]{1,0:T(8,128)(2,1)} %weight_ref.5, bf16[4,2,256,1024]{3,2,1,0:T(8,128)(2,1)} %bitcast.142), custom_call_target="tpu_custom_call" | custom-call | flops 3758096384 | bytes 11534336 | tf_op jit(solution)/shard_map/pallas_call | solution.py:35
  118.0 9.8 %collective-permute-done.5 = bf16[448,1024]{1,0:T(8,128)(2,1)S(1)} collective-permute-done((bf16[448,1024]{1,0:T(8,128)(2,1)S(1)}, bf16[448,1024]{1,0:T(8,128)(2,1)S(1)}, u32[]{:S(2)}, u32[]{:S(2)}) %collective-permute-start.5) | collective-permute-done | bytes 917536 | tf_op jit(solution)/shard_map/ppermute | solution.py:314
  144.6 9.5 %collective-permute-done.7 = bf16[448,1024]{1,0:T(8,128)(2,1)S(1)} collective-permute-done((bf16[448,1024]{1,0:T(8,128)(2,1)}, bf16[448,1024]{1,0:T(8,128)(2,1)S(1)}, u32[]{:S(2)}, u32[]{:S(2)}) %collective-permute-start.7) | collective-permute-done | bytes 917536 | tf_op jit(solution)/shard_map/ppermute | solution.py:314
  154.0 15.2 %collective-permute-done.10 = bf16[2,448,256]{1,2,0:T(8,128)(2,1)} collective-permute-done((bf16[2,448,256]{1,2,0:T(8,128)(2,1)S(1)}, bf16[2,448,256]{1,2,0:T(8,128)(2,1)}, u32[]{:S(2)}, u32[]{:S(2)}) %collective-permute-start.10) | collective-permute-done | bytes 458784 | tf_op jit(solution)/shard_map/ppermute | solution.py:271
  169.2 23.0 %collective-permute-done.9 = bf16[2,448,256]{1,2,0:T(8,128)(2,1)} collective-permute-done((bf16[2,448,256]{1,2,0:T(8,128)(2,1)S(1)}, bf16[2,448,256]{1,2,0:T(8,128)(2,1)}, u32[]{:S(2)}, u32[]{:S(2)}) %collective-permute-start.9) | collective-permute-done | bytes 458784 | tf_op jit(solution)/shard_map/ppermute | solution.py:271
  194.2 14.4 %collective-permute-start.12 = (bf16[448,1024]{1,0:T(8,128)(2,1)}, bf16[448,1024]{1,0:T(8,128)(2,1)}, u32[]{:S(2)}, u32[]{:S(2)}) collective-permute-start(bf16[448,1024]{1,0:T(8,128)(2,1)} %get-tuple-element.115), channel_id=1, source_target_pairs={{1,0},{2,1},{3,2},{5,4},{6,5},{7,6},{9,8},{10,9},{11,10},{13,12},{... | collective-permute-start | bytes 2752520 | tf_op jit(solution)/shard_map/ppermute | solution.py:314
  225.3 4.8 collective-permute-done.11
  232.8 5.6 collective-permute-start.15
  239.7 5.2 collective-permute-start.13
  244.9 13.2 %shard_map.57 = f32[4,448,1024]{2,1,0:T(8,128)} custom-call(s32[206]{0:T(256)} %bitcast.136, bf16[3584,2048]{1,0:T(8,128)(2,1)} %weight_ref.5, bf16[4,2,256,1024]{3,2,1,0:T(8,128)(2,1)} %bitcast.143), custom_call_target="tpu_custom_call" | custom-call | flops 7516192768 | bytes 18874368 | tf_op jit(solution)/shard_map/pallas_call | solution.py:35
  258.1 19.1 %collective-permute-done.15.refs_15_.refs_20_.refs_24_ = bf16[2,448,1024]{2,1,0:T(8,128)(2,1)} collective-permute-done((bf16[2,448,1024]{2,1,0:T(8,128)(2,1)S(1)}, bf16[2,448,1024]{2,1,0:T(8,128)(2,1)}, u32[]{:S(2)}, u32[]{:S(2)}) %collective-permute-start.15) | collective-permute-done | bytes 1835040 | tf_op jit(solution)/shard_map/ppermute | solution.py:351
  286.1 5.4 collective-permute-start.20
  298.1 37.8 %collective-permute-done.17.refs_5_.refs_7_ = bf16[2,448,1024]{2,1,0:T(8,128)(2,1)S(1)} collective-permute-done((bf16[2,448,1024]{2,1,0:T(8,128)(2,1)}, bf16[2,448,1024]{2,1,0:T(8,128)(2,1)S(1)}, u32[]{:S(2)}, u32[]{:S(2)}) %collective-permute-start.17) | collective-permute-done | bytes 1835040 | tf_op jit(solution)/shard_map/ppermute | solution.py:332
  348.2 18.6 %collective-permute-done.25 = bf16[448,1024]{1,0:T(8,128)(2,1)S(1)} collective-permute-done((bf16[448,1024]{1,0:T(8,128)(2,1)S(1)}, bf16[448,1024]{1,0:T(8,128)(2,1)S(1)}, u32[]{:S(2)}, u32[]{:S(2)}) %collective-permute-start.25) | collective-permute-done | bytes 917536 | tf_op jit(solution)/shard_map/ppermute | solution.py:314
  368.0 16.9 %collective-permute-done.23.refs_9_ = bf16[2,448,1024]{2,1,0:T(8,128)(2,1)S(1)} collective-permute-done((bf16[2,448,1024]{2,1,0:T(8,128)(2,1)S(1)}, bf16[2,448,1024]{2,1,0:T(8,128)(2,1)S(1)}, u32[]{:S(2)}, u32[]{:S(2)}) %collective-permute-start.23) | collective-permute-done | bytes 1835040 | tf_op jit(solution)/shard_map/ppermute | solution.py:332
  388.2 4.9 collective-permute-start.28
  399.0 11.2 %collective-permute-done.27 = bf16[448,1024]{1,0:T(8,128)(2,1)} collective-permute-done((bf16[448,1024]{1,0:T(8,128)(2,1)}, bf16[448,1024]{1,0:T(8,128)(2,1)}, u32[]{:S(2)}, u32[]{:S(2)}) %collective-permute-start.27) | collective-permute-done | bytes 917536 | tf_op jit(solution)/shard_map/ppermute | solution.py:313
  416.0 4.8 collective-permute-start.29
  420.9 15.6 %shard_map.58.refs_17_ = bf16[5,50176,128]{2,1,0:T(8,128)(2,1)} custom-call(s32[206]{0:T(256)S(1)} %bitcast.137, bf16[2,448,1024]{2,1,0:T(8,128)(2,1)S(1)} %pad_maximum_fusion.3.refs_0_.refs_11_.refs_13_.refs_16_.refs_20_, bf16[2,448,1024]{2,1,0:T(8,128)(2,1)} %collective-permute-done.13.refs_1_, ...), custom_call_target="tpu_custom_call" | custom-call | flops 8220835840 | bytes 20873216 | tf_op jit(solution)/shard_map/pallas_call | solution.py:182
  436.5 18.9 %collective-permute-done.31.refs_16_.refs_21_.refs_25_ = bf16[2,448,1024]{2,1,0:T(8,128)(2,1)S(1)} collective-permute-done((bf16[2,448,1024]{2,1,0:T(8,128)(2,1)S(1)}, bf16[2,448,1024]{2,1,0:T(8,128)(2,1)S(1)}, u32[]{:S(2)}, u32[]{:S(2)}) %collective-permute-start.31) | collective-permute-done | bytes 1835040 | tf_op jit(solution)/shard_map/ppermute | solution.py:351
  462.0 5.0 collective-permute-start.34
  469.3 20.7 %shard_map.59.refs_24_ = bf16[5,50176,128]{2,1,0:T(8,128)(2,1)} custom-call(s32[206]{0:T(256)S(1)} %bitcast.138, bf16[2,448,1024]{2,1,0:T(8,128)(2,1)S(1)} %pad_maximum_fusion.3.refs_0_.refs_11_.refs_13_.refs_16_.refs_20_, bf16[2,448,1024]{2,1,0:T(8,128)(2,1)} %collective-permute-done.13.refs_1_, ...), custom_call_target="tpu_custom_call", output_to_operand_aliasing={{}: (18, {})} | custom-call | flops 11509170176 | bytes 31424512 | tf_op jit(solution)/shard_map/pallas_call | solution.py:182
  490.0 8.0 %collective-permute-done.35.refs_23_.refs_29_ = bf16[2,448,1024]{2,1,0:T(8,128)(2,1)} collective-permute-done((bf16[2,448,1024]{2,1,0:T(8,128)(2,1)}, bf16[2,448,1024]{2,1,0:T(8,128)(2,1)}, u32[]{:S(2)}, u32[]{:S(2)}) %collective-permute-start.35) | collective-permute-done | bytes 1835040 | tf_op jit(solution)/shard_map/ppermute | solution.py:351
  498.0 16.9 %collective-permute-done.33.refs_15_.refs_17_ = bf16[2,448,1024]{2,1,0:T(8,128)(2,1)S(1)} collective-permute-done((bf16[2,448,1024]{2,1,0:T(8,128)(2,1)S(1)}, bf16[2,448,1024]{2,1,0:T(8,128)(2,1)S(1)}, u32[]{:S(2)}, u32[]{:S(2)}) %collective-permute-start.33) | collective-permute-done | bytes 1835040 | tf_op jit(solution)/shard_map/ppermute | solution.py:332
  520.9 42.7 %shard_map.60.refs_30_ = bf16[5,50176,128]{2,1,0:T(8,128)(2,1)} custom-call(s32[206]{0:T(256)S(1)} %bitcast.139, bf16[2,448,1024]{2,1,0:T(8,128)(2,1)S(1)} %pad_maximum_fusion.3.refs_0_.refs_11_.refs_13_.refs_16_.refs_20_, bf16[2,448,1024]{2,1,0:T(8,128)(2,1)} %collective-permute-done.13.refs_1_, ...), custom_call_target="tpu_custom_call", output_to_operand_aliasing={{}: (25, {})} | custom-call | flops 26306674688 | bytes 69730304 | tf_op jit(solution)/shard_map/pallas_call | solution.py:182
  566.7 32.7 %shard_map.61 = bf16[5,50176,128]{2,1,0:T(8,128)(2,1)} custom-call(s32[206]{0:T(256)S(1)} %bitcast.140, bf16[2,448,1024]{2,1,0:T(8,128)(2,1)S(1)} %pad_maximum_fusion.3.refs_0_.refs_11_.refs_13_.refs_16_.refs_20_, bf16[2,448,1024]{2,1,0:T(8,128)(2,1)} %collective-permute-done.13.refs_1_, ...), custom_call_target="tpu_custom_call", output_to_operand_aliasing={{}: (31, {})} | custom-call | flops 19730006016 | bytes 59637760 | tf_op jit(solution)/shard_map/pallas_call | solution.py:182
  (142 shorter events, 120.4 us)
Async XLA Ops:
  6.5 88.3 %all-gather.2.cloned.1.call-start = ((), (), s32[]{:S(2)}) async-start(), calls=%async_computation | async-start | bytes 4718592 | tf_op jit(solution)/shard_map/all_gather | solution.py:261
  26.9 23.0 %collective-permute-start.3 = (bf16[2,448,256]{1,2,0:T(8,128)(2,1)}, bf16[2,448,256]{1,2,0:T(8,128)(2,1)S(1)}, u32[]{:S(2)}, u32[]{:S(2)}) collective-permute-start(bf16[2,448,256]{1,2,0:T(8,128)(2,1)} %get-tuple-element.125), channel_id=1, source_target_pairs={{0,3},{1,0},{2,1},{3,2},{4,7},{5,4},{6,5},{7,6},{8,11},{9,8},{10,9... | collective-permute-start | bytes 1376264 | tf_op jit(solution)/shard_map/ppermute | solution.py:271
  27.0 47.1 %collective-permute-start.2 = (bf16[2,448,256]{1,2,0:T(8,128)(2,1)S(1)}, bf16[2,448,256]{1,2,0:T(8,128)(2,1)S(1)}, u32[]{:S(2)}, u32[]{:S(2)}) collective-permute-start(bf16[2,448,256]{1,2,0:T(8,128)(2,1)S(1)} %get-tuple-element.126), channel_id=1, source_target_pairs={{0,2},{1,3},{2,0},{3,1},{4,6},{5,7},{6,4},{7,5},{8,10},{9,11},{10,... | collective-permute-start | bytes 1376264 | tf_op jit(solution)/shard_map/ppermute | solution.py:271
  39.2 34.8 %collective-permute-start.1 = (bf16[2,448,256]{1,2,0:T(8,128)(2,1)S(1)}, bf16[2,448,256]{1,2,0:T(8,128)(2,1)S(1)}, u32[]{:S(2)}, u32[]{:S(2)}) collective-permute-start(bf16[2,448,256]{1,2,0:T(8,128)(2,1)S(1)} %get-tuple-element.127), channel_id=1, source_target_pairs={{0,1},{1,2},{2,3},{3,0},{4,5},{5,6},{6,7},{7,4},{8,9},{9,10},{10,1... | collective-permute-start | bytes 1376264 | tf_op jit(solution)/shard_map/ppermute | solution.py:271
  106.1 21.6 %collective-permute-start.5 = (bf16[448,1024]{1,0:T(8,128)(2,1)S(1)}, bf16[448,1024]{1,0:T(8,128)(2,1)S(1)}, u32[]{:S(2)}, u32[]{:S(2)}) collective-permute-start(bf16[448,1024]{1,0:T(8,128)(2,1)S(1)} %get-tuple-element.123), channel_id=1, source_target_pairs={{3,2},{7,6},{11,10},{15,14},{19,18},{23,22},{27,26},{31,30}} | collective-permute-start | bytes 2752520 | tf_op jit(solution)/shard_map/ppermute | solution.py:314
  131.1 22.9 %collective-permute-start.7 = (bf16[448,1024]{1,0:T(8,128)(2,1)}, bf16[448,1024]{1,0:T(8,128)(2,1)S(1)}, u32[]{:S(2)}, u32[]{:S(2)}) collective-permute-start(bf16[448,1024]{1,0:T(8,128)(2,1)} %get-tuple-element.121), channel_id=1, source_target_pairs={{2,1},{3,2},{6,5},{7,6},{10,9},{11,10},{14,13},{15,14},{18,17},{19... | collective-permute-start | bytes 2752520 | tf_op jit(solution)/shard_map/ppermute | solution.py:314
  138.8 30.4 %collective-permute-start.10 = (bf16[2,448,256]{1,2,0:T(8,128)(2,1)S(1)}, bf16[2,448,256]{1,2,0:T(8,128)(2,1)}, u32[]{:S(2)}, u32[]{:S(2)}) collective-permute-start(bf16[2,448,256]{1,2,0:T(8,128)(2,1)S(1)} %get-tuple-element.117), channel_id=1, source_target_pairs={{0,3},{1,0},{2,1},{3,2},{4,7},{5,4},{6,5},{7,6},{8,11},{9,8},{10,9... | collective-permute-start | bytes 1376264 | tf_op jit(solution)/shard_map/ppermute | solution.py:271
  140.4 51.9 %collective-permute-start.9 = (bf16[2,448,256]{1,2,0:T(8,128)(2,1)S(1)}, bf16[2,448,256]{1,2,0:T(8,128)(2,1)}, u32[]{:S(2)}, u32[]{:S(2)}) collective-permute-start(bf16[2,448,256]{1,2,0:T(8,128)(2,1)S(1)} %get-tuple-element.118), channel_id=1, source_target_pairs={{0,2},{1,3},{2,0},{3,1},{4,6},{5,7},{6,4},{7,5},{8,10},{9,11},{10,... | collective-permute-start | bytes 1376264 | tf_op jit(solution)/shard_map/ppermute | solution.py:271
  142.3 50.0 %collective-permute-start.8 = (bf16[2,448,256]{1,2,0:T(8,128)(2,1)S(1)}, bf16[2,448,256]{1,2,0:T(8,128)(2,1)}, u32[]{:S(2)}, u32[]{:S(2)}) collective-permute-start(bf16[2,448,256]{1,2,0:T(8,128)(2,1)S(1)} %get-tuple-element.119), channel_id=1, source_target_pairs={{0,1},{1,2},{2,3},{3,0},{4,5},{5,6},{6,7},{7,4},{8,9},{9,10},{10,1... | collective-permute-start | bytes 1376264 | tf_op jit(solution)/shard_map/ppermute | solution.py:271
  194.2 31.1 %collective-permute-start.12 = (bf16[448,1024]{1,0:T(8,128)(2,1)}, bf16[448,1024]{1,0:T(8,128)(2,1)}, u32[]{:S(2)}, u32[]{:S(2)}) collective-permute-start(bf16[448,1024]{1,0:T(8,128)(2,1)} %get-tuple-element.115), channel_id=1, source_target_pairs={{1,0},{2,1},{3,2},{5,4},{6,5},{7,6},{9,8},{10,9},{11,10},{13,12},{... | collective-permute-start | bytes 2752520 | tf_op jit(solution)/shard_map/ppermute | solution.py:314
  208.6 21.5 %collective-permute-start.11 = (bf16[448,1024]{1,0:T(8,128)(2,1)}, bf16[448,1024]{1,0:T(8,128)(2,1)}, u32[]{:S(2)}, u32[]{:S(2)}) collective-permute-start(bf16[448,1024]{1,0:T(8,128)(2,1)} %get-tuple-element.116), channel_id=1, source_target_pairs={{0,1},{1,2},{2,3},{4,5},{5,6},{6,7},{8,9},{9,10},{10,11},{12,13},{... | collective-permute-start | bytes 2752520 | tf_op jit(solution)/shard_map/ppermute | solution.py:313
  232.8 44.4 %collective-permute-start.15 = (bf16[2,448,1024]{2,1,0:T(8,128)(2,1)S(1)}, bf16[2,448,1024]{2,1,0:T(8,128)(2,1)}, u32[]{:S(2)}, u32[]{:S(2)}) collective-permute-start(bf16[2,448,1024]{2,1,0:T(8,128)(2,1)S(1)} %pad_maximum_fusion.3.refs_0_.refs_11_.refs_13_.refs_16_.refs_20_), channel_id=1, source_target_pairs={{0,8},{4,12},{8,16},{12,20},{16,24},{20,28},{24,0},{28,4},{1,9},{5... | collective-permute-start | bytes 5505032 | tf_op jit(solution)/shard_map/ppermute | solution.py:351
  238.4 38.8 %collective-permute-start.14 = (bf16[2,448,1024]{2,1,0:T(8,128)(2,1)S(1)}, bf16[2,448,1024]{2,1,0:T(8,128)(2,1)}, u32[]{:S(2)}, u32[]{:S(2)}) collective-permute-start(bf16[2,448,1024]{2,1,0:T(8,128)(2,1)S(1)} %pad_maximum_fusion.3.refs_0_.refs_11_.refs_13_.refs_16_.refs_20_), channel_id=1, source_target_pairs={{0,1},{1,2},{2,3},{4,5},{5,6},{6,7},{8,9},{9,10},{10,11},{12,13},{... | collective-permute-start | bytes 5505032 | tf_op jit(solution)/shard_map/ppermute | solution.py:332
  239.7 37.6 %collective-permute-start.13 = (bf16[2,448,1024]{2,1,0:T(8,128)(2,1)S(1)}, bf16[2,448,1024]{2,1,0:T(8,128)(2,1)}, u32[]{:S(2)}, u32[]{:S(2)}) collective-permute-start(bf16[2,448,1024]{2,1,0:T(8,128)(2,1)S(1)} %pad_maximum_fusion.3.refs_0_.refs_11_.refs_13_.refs_16_.refs_20_), channel_id=1, source_target_pairs={{1,0},{2,1},{3,2},{5,4},{6,5},{7,6},{9,8},{10,9},{11,10},{13,12},{... | collective-permute-start | bytes 5505032 | tf_op jit(solution)/shard_map/ppermute | solution.py:333
  292.2 43.7 %collective-permute-start.17 = (bf16[2,448,1024]{2,1,0:T(8,128)(2,1)}, bf16[2,448,1024]{2,1,0:T(8,128)(2,1)S(1)}, u32[]{:S(2)}, u32[]{:S(2)}) collective-permute-start(bf16[2,448,1024]{2,1,0:T(8,128)(2,1)} %collective-permute-done.14.refs_2_.refs_3_), channel_id=1, source_target_pairs={{1,2},{2,3},{5,6},{6,7},{9,10},{10,11},{13,14},{14,15},{17,18},{18... | collective-permute-start | bytes 5505032 | tf_op jit(solution)/shard_map/ppermute | solution.py:332
  293.5 44.1 %collective-permute-start.21 = (bf16[2,448,1024]{2,1,0:T(8,128)(2,1)S(1)}, bf16[2,448,1024]{2,1,0:T(8,128)(2,1)S(1)}, u32[]{:S(2)}, u32[]{:S(2)}) collective-permute-start(bf16[2,448,1024]{2,1,0:T(8,128)(2,1)S(1)} %pad_maximum_fusion.3.refs_0_.refs_11_.refs_13_.refs_16_.refs_20_), channel_id=1, source_target_pairs={{0,16},{4,20},{8,24},{12,28},{16,0},{20,4},{24,8},{28,12},{1,17},{... | collective-permute-start | bytes 5505032 | tf_op jit(solution)/shard_map/ppermute | solution.py:351
  338.9 27.9 %collective-permute-start.26 = (bf16[2,448,1024]{2,1,0:T(8,128)(2,1)S(1)}, bf16[2,448,1024]{2,1,0:T(8,128)(2,1)S(1)}, u32[]{:S(2)}, u32[]{:S(2)}) collective-permute-start(bf16[2,448,1024]{2,1,0:T(8,128)(2,1)S(1)} %broadcast_select_fusion.2), channel_id=1, source_target_pairs={{0,4},{4,0},{8,12},{12,8},{16,20},{20,16},{24,28},{28,24},{1,5},{5... | collective-permute-start | bytes 5505032 | tf_op jit(solution)/shard_map/ppermute | solution.py:347
  340.7 26.1 %collective-permute-start.22 = (bf16[2,448,1024]{2,1,0:T(8,128)(2,1)S(1)}, bf16[2,448,1024]{2,1,0:T(8,128)(2,1)S(1)}, u32[]{:S(2)}, u32[]{:S(2)}) collective-permute-start(bf16[2,448,1024]{2,1,0:T(8,128)(2,1)S(1)} %collective-permute-done.16.refs_4_.refs_6_), channel_id=1, source_target_pairs={{1,0},{5,4},{9,8},{13,12},{17,16},{21,20},{25,24},{29,28}} | collective-permute-start | bytes 5505032 | tf_op jit(solution)/shard_map/ppermute | solution.py:333
  341.4 43.5 %collective-permute-start.23 = (bf16[2,448,1024]{2,1,0:T(8,128)(2,1)S(1)}, bf16[2,448,1024]{2,1,0:T(8,128)(2,1)S(1)}, u32[]{:S(2)}, u32[]{:S(2)}) collective-permute-start(bf16[2,448,1024]{2,1,0:T(8,128)(2,1)S(1)} %collective-permute-done.17.refs_5_.refs_7_), channel_id=1, source_target_pairs={{2,3},{6,7},{10,11},{14,15},{18,19},{22,23},{26,27},{30,31}} | collective-permute-start | bytes 5505032 | tf_op jit(solution)/shard_map/ppermute | solution.py:332
  343.3 23.5 %collective-permute-start.25 = (bf16[448,1024]{1,0:T(8,128)(2,1)S(1)}, bf16[448,1024]{1,0:T(8,128)(2,1)S(1)}, u32[]{:S(2)}, u32[]{:S(2)}) collective-permute-start(bf16[448,1024]{1,0:T(8,128)(2,1)S(1)} %get-tuple-element.111), channel_id=1, source_target_pairs={{2,1},{3,2},{6,5},{7,6},{10,9},{11,10},{14,13},{15,14},{18,17},{19... | collective-permute-start | bytes 2752520 | tf_op jit(solution)/shard_map/ppermute | solution.py:314
  386.9 23.2 %collective-permute-start.27 = (bf16[448,1024]{1,0:T(8,128)(2,1)}, bf16[448,1024]{1,0:T(8,128)(2,1)}, u32[]{:S(2)}, u32[]{:S(2)}) collective-permute-start(bf16[448,1024]{1,0:T(8,128)(2,1)} %get-tuple-element.109), channel_id=1, source_target_pairs={{0,1},{1,2},{2,3},{4,5},{5,6},{6,7},{8,9},{9,10},{10,11},{12,13},{... | collective-permute-start | bytes 2752520 | tf_op jit(solution)/shard_map/ppermute | solution.py:313
  388.2 22.8 %collective-permute-start.28 = (bf16[448,1024]{1,0:T(8,128)(2,1)}, bf16[448,1024]{1,0:T(8,128)(2,1)}, u32[]{:S(2)}, u32[]{:S(2)}) collective-permute-start(bf16[448,1024]{1,0:T(8,128)(2,1)} %get-tuple-element.110), channel_id=1, source_target_pairs={{1,0},{2,1},{3,2},{5,4},{6,5},{7,6},{9,8},{10,9},{11,10},{13,12},{... | collective-permute-start | bytes 2752520 | tf_op jit(solution)/shard_map/ppermute | solution.py:314
  414.4 40.9 %collective-permute-start.31 = (bf16[2,448,1024]{2,1,0:T(8,128)(2,1)S(1)}, bf16[2,448,1024]{2,1,0:T(8,128)(2,1)S(1)}, u32[]{:S(2)}, u32[]{:S(2)}) collective-permute-start(bf16[2,448,1024]{2,1,0:T(8,128)(2,1)S(1)} %pad_maximum_fusion.4.refs_10_.refs_12_.refs_14_.refs_17_.refs_21_), channel_id=1, source_target_pairs={{0,8},{4,12},{8,16},{12,20},{16,24},{20,28},{24,0},{28,4},{1,9},{5... | collective-permute-start | bytes 5505032 | tf_op jit(solution)/shard_map/ppermute | solution.py:351
  414.5 42.1 %collective-permute-start.30 = (bf16[2,448,1024]{2,1,0:T(8,128)(2,1)S(1)}, bf16[2,448,1024]{2,1,0:T(8,128)(2,1)S(1)}, u32[]{:S(2)}, u32[]{:S(2)}) collective-permute-start(bf16[2,448,1024]{2,1,0:T(8,128)(2,1)S(1)} %pad_maximum_fusion.4.refs_10_.refs_12_.refs_14_.refs_17_.refs_21_), channel_id=1, source_target_pairs={{0,1},{1,2},{2,3},{4,5},{5,6},{6,7},{8,9},{9,10},{10,11},{12,13},{... | collective-permute-start | bytes 5505032 | tf_op jit(solution)/shard_map/ppermute | solution.py:332
  416.0 41.7 %collective-permute-start.29 = (bf16[2,448,1024]{2,1,0:T(8,128)(2,1)S(1)}, bf16[2,448,1024]{2,1,0:T(8,128)(2,1)S(1)}, u32[]{:S(2)}, u32[]{:S(2)}) collective-permute-start(bf16[2,448,1024]{2,1,0:T(8,128)(2,1)S(1)} %pad_maximum_fusion.4.refs_10_.refs_12_.refs_14_.refs_17_.refs_21_), channel_id=1, source_target_pairs={{1,0},{2,1},{3,2},{5,4},{6,5},{7,6},{9,8},{10,9},{11,10},{13,12},{... | collective-permute-start | bytes 5505032 | tf_op jit(solution)/shard_map/ppermute | solution.py:333
  457.7 40.3 %collective-permute-start.35 = (bf16[2,448,1024]{2,1,0:T(8,128)(2,1)}, bf16[2,448,1024]{2,1,0:T(8,128)(2,1)}, u32[]{:S(2)}, u32[]{:S(2)}) collective-permute-start(bf16[2,448,1024]{2,1,0:T(8,128)(2,1)} %copy-done.1), channel_id=1, source_target_pairs={{0,16},{4,20},{8,24},{12,28},{16,0},{20,4},{24,8},{28,12},{1,17},{... | collective-permute-start | bytes 5505032 | tf_op jit(solution)/shard_map/ppermute | solution.py:351
  462.0 28.0 %collective-permute-start.34 = (bf16[2,448,1024]{2,1,0:T(8,128)(2,1)}, bf16[2,448,1024]{2,1,0:T(8,128)(2,1)}, u32[]{:S(2)}, u32[]{:S(2)}) collective-permute-start(bf16[2,448,1024]{2,1,0:T(8,128)(2,1)} %broadcast_select_fusion.1), channel_id=1, source_target_pairs={{0,4},{4,0},{8,12},{12,8},{16,20},{20,16},{24,28},{28,24},{1,5},{5... | collective-permute-start | bytes 5505032 | tf_op jit(solution)/shard_map/ppermute | solution.py:347
  467.1 30.9 %collective-permute-start.32 = (bf16[2,448,1024]{2,1,0:T(8,128)(2,1)S(1)}, bf16[2,448,1024]{2,1,0:T(8,128)(2,1)S(1)}, u32[]{:S(2)}, u32[]{:S(2)}) collective-permute-start(bf16[2,448,1024]{2,1,0:T(8,128)(2,1)S(1)} %collective-permute-done.29.refs_11_), channel_id=1, source_target_pairs={{1,0},{2,1},{5,4},{6,5},{9,8},{10,9},{13,12},{14,13},{17,16},{18,1... | collective-permute-start | bytes 5505032 | tf_op jit(solution)/shard_map/ppermute | solution.py:333
  468.0 47.0 %collective-permute-start.33 = (bf16[2,448,1024]{2,1,0:T(8,128)(2,1)S(1)}, bf16[2,448,1024]{2,1,0:T(8,128)(2,1)S(1)}, u32[]{:S(2)}, u32[]{:S(2)}) collective-permute-start(bf16[2,448,1024]{2,1,0:T(8,128)(2,1)S(1)} %collective-permute-done.30.refs_12_.refs_13_), channel_id=1, source_target_pairs={{1,2},{2,3},{5,6},{6,7},{9,10},{10,11},{13,14},{14,15},{17,18},{18... | collective-permute-start | bytes 5505032 | tf_op jit(solution)/shard_map/ppermute | solution.py:332
  518.6 45.1 %collective-permute-start.38 = (bf16[2,448,1024]{2,1,0:T(8,128)(2,1)}, bf16[2,448,1024]{2,1,0:T(8,128)(2,1)S(1)}, u32[]{:S(2)}, u32[]{:S(2)}) collective-permute-start(bf16[2,448,1024]{2,1,0:T(8,128)(2,1)} %broadcast_select_fusion), channel_id=1, source_target_pairs={{0,4},{4,0},{8,12},{12,8},{16,20},{20,16},{24,28},{28,24},{1,5},{5... | collective-permute-start | bytes 5505032 | tf_op jit(solution)/shard_map/ppermute | solution.py:347
  518.6 45.1 %collective-permute-start.36 = (bf16[2,448,1024]{2,1,0:T(8,128)(2,1)S(1)}, bf16[2,448,1024]{2,1,0:T(8,128)(2,1)S(1)}, u32[]{:S(2)}, u32[]{:S(2)}) collective-permute-start(bf16[2,448,1024]{2,1,0:T(8,128)(2,1)S(1)} %collective-permute-done.32.refs_14_.refs_16_), channel_id=1, source_target_pairs={{1,0},{5,4},{9,8},{13,12},{17,16},{21,20},{25,24},{29,28}} | collective-permute-start | bytes 5505032 | tf_op jit(solution)/shard_map/ppermute | solution.py:333
  519.4 44.3 %collective-permute-start.37 = (bf16[2,448,1024]{2,1,0:T(8,128)(2,1)S(1)}, bf16[2,448,1024]{2,1,0:T(8,128)(2,1)S(1)}, u32[]{:S(2)}, u32[]{:S(2)}) collective-permute-start(bf16[2,448,1024]{2,1,0:T(8,128)(2,1)S(1)} %collective-permute-done.33.refs_15_.refs_17_), channel_id=1, source_target_pairs={{2,3},{6,7},{10,11},{14,15},{18,19},{22,23},{26,27},{30,31}} | collective-permute-start | bytes 5505032 | tf_op jit(solution)/shard_map/ppermute | solution.py:332
  (35 other events, 600.3 us)
Sparse Core Ops, SparseCore 0:
  23.4 71.3 all-gather.1

commit v5 on v4

--- a/solution.py
+++ b/solution.py
@@ -7,7 +7,8 @@
 from jax.experimental.pallas import tpu as pltpu
 from jax.sharding import PartitionSpec as P
 
-CHUNKS = 2
+CHUNKS = 1
+LAST_PARTS = 2
 LANES = 128
 CONTRACT_LAST = (((1,), (1,)), ((), ()))
 
@@ -56,7 +57,7 @@
 
 
 def factor_kernel(shape, candidates, plan, base, scale, table_ref, *refs):
-    partners, chunk_total, chunk_rows = shape
+    partners, chunk_total, chunk_rows, row_count = shape
     total = len(plan)
     row_refs = refs[: sum(candidates)]
     columns = refs[len(row_refs) : len(row_refs) + partners * chunk_total]
@@ -129,7 +130,7 @@
                 product = product * scale
                 for extra in range(count):
                     start = (first + extra) * 2 + f
-                    wide[pl.ds(start, chunk_rows, stride=stride), :] = product[
+                    wide[pl.ds(start, row_count, stride=stride), :] = product[
                         :, extra * LANES : (extra + 1) * LANES
                     ]
 
@@ -162,11 +163,13 @@
     used, keys = sorted(pieces), sorted(columns)
     plan = [(used.index(piece), k) for piece, k in plan]
     pieces = [pieces[piece] for piece in used]
-    _, chunk_rows, tokens = pieces[0][0].shape
+    _, row_count, tokens = pieces[0][0].shape
     dtype = pieces[0][0].dtype
     chunk_total = len(columns[keys[0]])
+    chunk_rows = columns[keys[0]][0].shape[1]
     slice_width = chunk_total * chunk_rows
-    height = chunk_rows * 2 * (slice_width // LANES)
+    lane_tiles = slice_width // LANES
+    height = row_count * 2 * lane_tiles
     operands = [array for arrays in pieces for array in arrays]
     operands += [part for k in keys for part in columns[k]]
     aliases = {}
@@ -182,7 +185,7 @@
     return pl.pallas_call(
         functools.partial(
             factor_kernel,
-            (len(keys), chunk_total, chunk_rows),
+            (len(keys), chunk_total, chunk_rows, row_count),
             tuple(len(arrays) for arrays in pieces),
             tuple((piece, keys.index(k)) for piece, k in plan),
             base,
@@ -195,21 +198,23 @@
             out_specs=pl.BlockSpec((1, height, LANES), placed),
             scratch_shapes=[
                 pltpu.VMEM((len(keys), 2, slice_width, tokens), dtype),
-                pltpu.VMEM((2, 2, chunk_rows, tokens), dtype),
+                pltpu.VMEM((2, 2, row_count, tokens), dtype),
                 pltpu.VMEM((height, LANES), jnp.float32),
                 pltpu.VMEM((height, LANES), jnp.float32),
                 pltpu.SemaphoreType.DMA((len(keys), chunk_total)),
                 pltpu.SemaphoreType.DMA((2,)),
             ],
         ),
-        out_shape=jax.ShapeDtypeStruct((band, slices * chunk_total * height, LANES), dtype),
+        out_shape=jax.ShapeDtypeStruct(
+            (band, slices * slice_width * 2 * lane_tiles, LANES), dtype
+        ),
         input_output_aliases=aliases,
         compiler_params=pltpu.CompilerParams(
-            dimension_semantics=("arbitrary",), vmem_limit_bytes=48 * 2**20
+            dimension_semantics=("arbitrary",), vmem_limit_bytes=56 * 2**20
         ),
         cost_estimate=pl.CostEstimate(
-            flops=4 * total * chunk_rows * tokens * slice_width,
-            bytes_accessed=4 * total * chunk_rows * (tokens + slice_width)
+            flops=4 * total * row_count * tokens * slice_width,
+            bytes_accessed=4 * total * row_count * (tokens + slice_width)
             + 4 * len(keys) * slice_width * tokens,
             transcendentals=0,
         ),
@@ -244,7 +249,7 @@
     chunk_rows = slice_width // CHUNKS
     use_kernels = (
         slice_width % LANES == 0
-        and chunk_rows % 16 == 0
+        and chunk_rows % (16 * LAST_PARTS) == 0
         and local_features % LANES == 0
         and local_tokens % LANES == 0
     )
@@ -282,7 +287,7 @@
         )
 
     first_saved = saved_pieces(0, saved)
-    features, saved, *first_saved = tie(features, saved, *first_saved)
+    features, first_saved[1], first_saved[-1] = tie(features, first_saved[1], first_saved[-1])
     features = features.reshape(groups, per_group, local_tokens, local_features)
 
     def partial_products(chunk, offsets, features):
@@ -362,6 +367,8 @@
         ready[k] = place // share + 1
     for k in range(1, half_band, 2):
         ready[k] = max(ready[k - 1], ready[k + 1]) + 1
+        if ready[k] == groups - 1:
+            ready[k] -= 0.5
     calls = {}
     for k in sorted(ready, key=ready.get):
         for chunk in range(CHUNKS):
@@ -369,21 +376,41 @@
                 came = 0
                 if chunk == CHUNKS - 1 and place:
                     came = max(order[d][place - 1][0] for d in range(groups))
-                calls.setdefault(max(ready[k], came), []).append(((chunk, place), k))
-
-    def row_arrays(chunk, place):
+                if came == groups - 1:
+                    for part in range(LAST_PARTS):
+                        time = came + part / LAST_PARTS
+                        calls.setdefault(time, []).append(((chunk, place, part), k))
+                else:
+                    calls.setdefault(max(ready[k], came), []).append(((chunk, place, None), k))
+
+    part_rows = chunk_rows // LAST_PARTS
+
+    def row_arrays(chunk, place, part):
         own, held = rows[chunk]
         if place == 0:
             return [own]
         kinds = sorted({order[d][place - 1] for d in range(groups)})
-        return [held[hops][int(left)] for hops, left in kinds]
-
-    def row_entry(d, chunk, place):
-        if place == 0:
-            return d * CHUNKS + chunk, 0
-        kinds = sorted({order[e][place - 1] for e in range(groups)})
-        hops, left = order[d][place - 1]
-        return (d - hops if left else d + hops) * CHUNKS + chunk, kinds.index((hops, left))
+        arrays = [held[hops][int(left)] for hops, left in kinds]
+        if part is None:
+            return arrays
+        return [
+            parts[part] if hops == groups - 1 else piece_of(parts, part)
+            for (hops, _), parts in zip(kinds, arrays)
+        ]
+
+    def piece_of(array, part):
+        return array[:, part * part_rows : (part + 1) * part_rows]
+
+    def row_entry(d, chunk, place, part):
+        hops, left, choice = 0, False, 0
+        if place:
+            kinds = sorted({order[e][place - 1] for e in range(groups)})
+            hops, left = order[d][place - 1]
+            choice = kinds.index((hops, left))
+        position = (d - hops if left else d + hops) * CHUNKS + chunk
+        if part is not None:
+            position = position * LAST_PARTS + part
+        return position, choice
 
     first_offsets = tuple(sorted({1, groups - 1}))
     other_offsets = tuple(o for o in range(groups) if o not in first_offsets)
@@ -436,7 +463,10 @@
     received = None
     for step in range(1, groups):
         received = tie(*reduce_step(partial, step, received))
-        if step == groups - 2:
+        if step == 1:
+            moved = tie(*received, *first_saved)
+            received, first_saved = moved[:2], list(moved[2:])
+        if step == groups - 2 and later_saved:
             moved = tie(*received, *[piece for pieces in later_saved for piece in pieces])
             received, moved = moved[:2], moved[2:]
             later_saved = [
@@ -458,13 +488,25 @@
         for step in range(1, groups):
             if later and step > 1:
                 received = reduce_step(partial, step - 1, received or None)
-            left, right = gather_step(step, left, right)
-            held[step] = (right, left)
             made = partner_step(step, found)
+            if step < groups - 1 or later or not use_kernels:
+                left, right = gather_step(step, left, right)
+                held[step] = (right, left)
+            else:
+                lefts, rights, sent_on = [], [], ()
+                for part in range(LAST_PARTS):
+                    ends = (piece_of(left, part), piece_of(right, part))
+                    if sent_on:
+                        ends = tie(*ends, *sent_on)[:2]
+                    sent_on = gather_step(step, *ends)
+                    lefts.append(sent_on[0])
+                    rights.append(sent_on[1])
+                held[step] = (rights, lefts)
             column.update(made)
             found.update(made)
             if use_kernels and not later:
                 result = multiply(step - 1, result)
+                result = multiply(step - 0.5, result)
             if step < groups - 1 or later:
                 keys = list(found)
                 new_parts = [parts] if later and step == 1 else []
@@ -482,7 +524,8 @@
             received = reduce_step(partial, groups - 1, received)
 
     if use_kernels:
-        result = multiply(groups - 1, result)
+        for part in range(LAST_PARTS):
+            result = multiply(groups - 1 + part / LAST_PARTS, result)
         result = result.reshape(band, -1, 2, LANES).transpose(2, 0, 1, 3)
     else:
 

time: 618 us -> 610 us (0.987)
  starting transfers between devices: 108 us -> 53.9 us
  waiting for transfers between devices: 281 us -> 308 us
  Pallas kernels: 143 us -> 161 us
    ppermute x6 -> x4, waiting for transfers between devices: 72.9 us -> 129 us  [gather_step(): lax.ppermute(left, 'dp', [(d, d + 1) for d in range(step - 1, groups - 1)])]
    ppermute x4 -> x2, waiting for transfers between devices: 47.6 us -> 4.7 us  [partner_step(): lax.ppermute(found[0], 'tensor', [(t, (t + k) % blocks) for t in range(bl...]
    pallas_call x4 -> x6, Pallas kernels: 112 us -> 133 us  [factor_rows(): pl.pallas_call(functools.partial(factor_kernel, (len(keys), chunk_total,...]
    ppermute x6 -> x3, starting transfers between devices: 34.4 us -> 14 us  [reduce_step(): lax.ppermute(left.astype(jnp.bfloat16), 'dp', [(d, d - 1) for d in range(...]
    ppermute x6 -> x3, waiting for transfers between devices: 43.3 us -> 62.8 us  [reduce_step(): lax.ppermute(left.astype(jnp.bfloat16), 'dp', [(d, d - 1) for d in range(...]
    ppermute x6 -> x3, waiting for transfers between devices: 70.3 us -> 58 us  [saved_pieces(): pieces.append(lax.ppermute(part(own_group + shift), 'dp', ring))]
    ppermute x4 -> x2, starting transfers between devices: 12.2 us -> 1.1 us  [partner_step(): lax.ppermute(found[0], 'tensor', [(t, (t + k) % blocks) for t in range(bl...]
    slice x0 -> x4, local copies, waits for them, and re-layouts: none -> 8.74 us  [piece_of(): return array[:, part * part_rows:(part + 1) * part_rows]]
  transfers between devices with their start and end apart: 40 -> 23, of which waited for: 24 -> 14; matrix products, arithmetic and copies ran while one was open for 5% -> 5% of each run, Pallas kernels for 17% -> 21%
where the time goes in v5:
time: 610 us; the launch traced here: 599 us
  waiting for transfers between devices  308 us (50%)
  Pallas kernels  161 us (26%)
  starting transfers between devices  53.9 us (9%)
  other arithmetic  32.4 us (5%)
  local copies, waits for them, and re-layouts  28.9 us (5%)
  between operations  14.1 us (2%)
    pallas_call x6, Pallas kernels, factor_rows(): pl.pallas_call(functools.partial(factor_kernel, (len(keys), chunk_total,...  133 us
    ppermute x4, waiting for transfers between devices, gather_step(): lax.ppermute(left, 'dp', [(d, d + 1) for d in range(step - 1, groups - 1)])  129 us
    ppermute x3, waiting for transfers between devices, reduce_step(): lax.ppermute(left.astype(jnp.bfloat16), 'dp', [(d, d - 1) for d in range(...  62.8 us
    ppermute x3, waiting for transfers between devices, saved_pieces(): pieces.append(lax.ppermute(part(own_group + shift), 'dp', ring))  58 us
    pallas_call x2, Pallas kernels, hidden_parts(): pl.pallas_call(functools.partial(hidden_kernel, base + count), grid_spec=...  28.1 us
    all_gather x1, waiting for transfers between devices, per_device(): features = lax.all_gather(sent, 'tensor', axis=0, tiled=True)  22.7 us
    ppermute x3, waiting for transfers between devices, reduce_step(): lax.ppermute(right.astype(jnp.bfloat16), 'dp', [(d, d + 1) for d in range...  21.7 us
    ppermute x3, starting transfers between devices, reduce_step(): lax.ppermute(left.astype(jnp.bfloat16), 'dp', [(d, d - 1) for d in range(...  14 us
  transfers between devices with their start and end apart: 23, of which 14 were waited for; matrix products, arithmetic and copies ran while one was open for 5% of the time, Pallas kernels for 21%

profile of v5, /device:TPU:29, one launch (start us, length us, event | category | flops | bytes accessed | tf_op | source)
XLA Modules:
  0.0 598.8 jit_solution(8441140061103681159)
XLA Ops:
  9.5 4.2 pad_maximum_fusion
  13.7 8.8 %collective-permute-done = bf16[256,1024]{1,0:T(8,128)(2,1)S(1)} collective-permute-done((bf16[256,1024]{1,0:T(8,128)(2,1)}, bf16[256,1024]{1,0:T(8,128)(2,1)S(1)}, u32[]{:S(2)}, u32[]{:S(2)}) %collective-permute-start) | collective-permute-done | bytes 524320 | tf_op jit(solution)/shard_map/ppermute | solution.py:263
  23.4 3.6 constant_dynamic-slice_fusion.4
  27.0 12.0 %collective-permute-start.1 = (bf16[2,896,256]{1,2,0:T(8,128)(2,1)}, bf16[2,896,256]{1,2,0:T(8,128)(2,1)S(1)}, u32[]{:S(2)}, u32[]{:S(2)}) collective-permute-start(bf16[2,896,256]{1,2,0:T(8,128)(2,1)} %get-tuple-element.96), channel_id=1, source_target_pairs={{0,1},{1,2},{2,3},{3,0},{4,5},{5,6},{6,7},{7,4},{8,9},{9,10},{10,1... | collective-permute-start | bytes 2752520 | tf_op jit(solution)/shard_map/ppermute | solution.py:276
  40.2 17.3 %collective-permute-done.1 = bf16[2,896,256]{1,2,0:T(8,128)(2,1)S(1)} collective-permute-done((bf16[2,896,256]{1,2,0:T(8,128)(2,1)}, bf16[2,896,256]{1,2,0:T(8,128)(2,1)S(1)}, u32[]{:S(2)}, u32[]{:S(2)}) %collective-permute-start.1) | collective-permute-done | bytes 917536 | tf_op jit(solution)/shard_map/ppermute | solution.py:276
  57.5 21.0 %collective-permute-done.2 = bf16[2,896,256]{1,2,0:T(8,128)(2,1)S(1)} collective-permute-done((bf16[2,896,256]{1,2,0:T(8,128)(2,1)}, bf16[2,896,256]{1,2,0:T(8,128)(2,1)S(1)}, u32[]{:S(2)}, u32[]{:S(2)}) %collective-permute-start.2) | collective-permute-done | bytes 917536 | tf_op jit(solution)/shard_map/ppermute | solution.py:276
  78.5 22.7 %all-gather.2.cloned.1.call-done = bf16[2048,1024]{1,0:T(8,128)(2,1)} async-done(((bf16[256,1024]{1,0:T(8,128)(2,1)}), bf16[2048,1024]{1,0:T(8,128)(2,1)}) %all-gather.2.cloned.1.call-update) | async-done | bytes 4194320 | tf_op jit(solution)/shard_map/all_gather | solution.py:266
  101.3 13.8 %shard_map.56 = f32[2,896,1024]{2,1,0:T(8,128)} custom-call(s32[123]{0:T(128)} %fusion.10.table_ref, bf16[3584,2048]{1,0:T(8,128)(2,1)} %weight_ref.3, bf16[4,2,256,1024]{3,2,1,0:T(8,128)(2,1)} %bitcast.89), custom_call_target="tpu_custom_call" | custom-call | flops 7516192768 | bytes 18874368 | tf_op jit(solution)/shard_map/pallas_call | solution.py:36
  115.1 5.6 fusion.6
  122.5 3.5 collective-permute-start.4
  126.0 14.3 %shard_map.55 = f32[2,896,1024]{2,1,0:T(8,128)} custom-call(s32[123]{0:T(128)} %fusion.10.table_ref, bf16[3584,2048]{1,0:T(8,128)(2,1)} %weight_ref.3, bf16[4,2,256,1024]{3,2,1,0:T(8,128)(2,1)} %bitcast.90), custom_call_target="tpu_custom_call" | custom-call | flops 7516192768 | bytes 18874368 | tf_op jit(solution)/shard_map/pallas_call | solution.py:36
  140.3 23.8 %collective-permute-done.4 = bf16[896,1024]{1,0:T(8,128)(2,1)} collective-permute-done((bf16[896,1024]{1,0:T(8,128)(2,1)}, bf16[896,1024]{1,0:T(8,128)(2,1)}, u32[]{:S(2)}, u32[]{:S(2)}) %collective-permute-start.4) | collective-permute-done | bytes 1835040 | tf_op jit(solution)/shard_map/ppermute | solution.py:319
  164.1 19.7 %collective-permute-done.5 = bf16[2,896,256]{1,2,0:T(8,128)(2,1)} collective-permute-done((bf16[2,896,256]{1,2,0:T(8,128)(2,1)}, bf16[2,896,256]{1,2,0:T(8,128)(2,1)}, u32[]{:S(2)}, u32[]{:S(2)}) %collective-permute-start.5) | collective-permute-done | bytes 917536 | tf_op jit(solution)/shard_map/ppermute | solution.py:276
  183.8 4.3 add_convert_fusion.2
  191.7 38.1 %collective-permute-done.7 = bf16[896,1024]{1,0:T(8,128)(2,1)S(1)} collective-permute-done((bf16[896,1024]{1,0:T(8,128)(2,1)S(1)}, bf16[896,1024]{1,0:T(8,128)(2,1)S(1)}, u32[]{:S(2)}, u32[]{:S(2)}) %collective-permute-start.7) | collective-permute-done | bytes 1835040 | tf_op jit(solution)/shard_map/ppermute | solution.py:319
  229.8 3.5 add_convert_fusion
  234.6 7.8 %collective-permute-start.9 = (bf16[896,1024]{1,0:T(8,128)(2,1)}, bf16[896,1024]{1,0:T(8,128)(2,1)}, u32[]{:S(2)}, u32[]{:S(2)}) collective-permute-start(bf16[896,1024]{1,0:T(8,128)(2,1)} %get-tuple-element.75), channel_id=1, source_target_pairs={{1,0},{2,1},{3,2},{5,4},{6,5},{7,6},{9,8},{10,9},{11,10},{13,12},{... | collective-permute-start | bytes 5505032 | tf_op jit(solution)/shard_map/ppermute | solution.py:319
  255.9 21.6 %collective-permute-done.8 = bf16[896,1024]{1,0:T(8,128)(2,1)} collective-permute-done((bf16[896,1024]{1,0:T(8,128)(2,1)}, bf16[896,1024]{1,0:T(8,128)(2,1)}, u32[]{:S(2)}, u32[]{:S(2)}) %collective-permute-start.8) | collective-permute-done | bytes 1835040 | tf_op jit(solution)/shard_map/ppermute | solution.py:318
  278.5 3.7 fusion.9
  285.6 6.6 %collective-permute-start.11 = (bf16[2,896,1024]{2,1,0:T(8,128)(2,1)}, bf16[2,896,1024]{2,1,0:T(8,128)(2,1)}, u32[]{:S(2)}, u32[]{:S(2)}) collective-permute-start(bf16[2,896,1024]{2,1,0:T(8,128)(2,1)} %pad_maximum_fusion.2.refs_0_.refs_1_.refs_3_.refs_6_.refs_4_), channel_id=1, source_target_pairs={{1,0},{2,1},{3,2},{5,4},{6,5},{7,6},{9,8},{10,9},{11,10},{13,12},{... | collective-permute-start | bytes 11010056 | tf_op jit(solution)/shard_map/ppermute | solution.py:338
  292.7 10.2 %shard_map.57.refs_5_ = bf16[5,50176,128]{2,1,0:T(8,128)(2,1)} custom-call(s32[123]{0:T(128)} %fusion.10.table_ref, bf16[2,896,1024]{2,1,0:T(8,128)(2,1)} %pad_maximum_fusion.2.refs_0_.refs_1_.refs_3_.refs_6_.refs_4_, bf16[2,896,1024]{2,1,0:T(8,128)(2,1)} %pad_maximum_fusion.2.refs_0_.refs_1_.refs_3_.refs_6_.refs_4_), custom_call_target="tpu_custom_call" | custom-call | flops 3288334336 | bytes 10551296 | tf_op jit(solution)/shard_map/pallas_call | solution.py:185
  303.0 62.5 %collective-permute-done.10.refs_2_.refs_3_ = bf16[2,896,1024]{2,1,0:T(8,128)(2,1)} collective-permute-done((bf16[2,896,1024]{2,1,0:T(8,128)(2,1)}, bf16[2,896,1024]{2,1,0:T(8,128)(2,1)}, u32[]{:S(2)}, u32[]{:S(2)}) %collective-permute-start.10) | collective-permute-done | bytes 3670048 | tf_op jit(solution)/shard_map/ppermute | solution.py:337
  366.3 4.7 collective-permute-done.12.refs_4_.refs_8_.refs_6_
  371.0 4.2 broadcast_select_fusion.1
  375.3 4.1 collective-permute-start.15
  382.4 19.6 %shard_map.58.refs_10_ = bf16[5,50176,128]{2,1,0:T(8,128)(2,1)} custom-call(s32[123]{0:T(128)} %fusion.10.table_ref, bf16[2,896,1024]{2,1,0:T(8,128)(2,1)} %pad_maximum_fusion.2.refs_0_.refs_1_.refs_3_.refs_6_.refs_4_, bf16[2,896,1024]{2,1,0:T(8,128)(2,1)} %collective-permute-done.11.refs_1_, ...), custom_call_target="tpu_custom_call", output_to_operand_aliasing={{}: (6, {})} | custom-call | flops 9865003008 | bytes 27983872 | tf_op jit(solution)/shard_map/pallas_call | solution.py:185
  402.1 65.1 %collective-permute-done.14.refs_5_ = bf16[2,896,1024]{2,1,0:T(8,128)(2,1)S(1)} collective-permute-done((bf16[2,896,1024]{2,1,0:T(8,128)(2,1)}, bf16[2,896,1024]{2,1,0:T(8,128)(2,1)S(1)}, u32[]{:S(2)}, u32[]{:S(2)}) %collective-permute-start.14) | collective-permute-done | bytes 3670048 | tf_op jit(solution)/shard_map/ppermute | solution.py:337
  467.2 5.6 broadcast_select_fusion
  482.6 44.2 %shard_map.59.refs_7_ = bf16[5,50176,128]{2,1,0:T(8,128)(2,1)} custom-call(s32[123]{0:T(128)} %fusion.10.table_ref, bf16[2,896,1024]{2,1,0:T(8,128)(2,1)} %pad_maximum_fusion.2.refs_0_.refs_1_.refs_3_.refs_6_.refs_4_, bf16[2,896,1024]{2,1,0:T(8,128)(2,1)} %collective-permute-done.11.refs_1_, ...), custom_call_target="tpu_custom_call", output_to_operand_aliasing={{}: (11, {})} | custom-call | flops 26306674688 | bytes 69730304 | tf_op jit(solution)/shard_map/pallas_call | solution.py:185
  531.3 19.6 %shard_map.60.refs_9_ = bf16[5,50176,128]{2,1,0:T(8,128)(2,1)} custom-call(s32[123]{0:T(128)} %fusion.10.table_ref, bf16[2,896,1024]{2,1,0:T(8,128)(2,1)} %pad_maximum_fusion.2.refs_0_.refs_1_.refs_3_.refs_6_.refs_4_, bf16[2,896,1024]{2,1,0:T(8,128)(2,1)} %collective-permute-done.11.refs_1_, ...), custom_call_target="tpu_custom_call", output_to_operand_aliasing={{}: (8, {})} | custom-call | flops 9865003008 | bytes 24313856 | tf_op jit(solution)/shard_map/pallas_call | solution.py:185
  550.9 19.7 %shard_map.61.refs_9_ = bf16[5,50176,128]{2,1,0:T(8,128)(2,1)} custom-call(s32[123]{0:T(128)} %fusion.10.table_ref, bf16[2,448,1024]{2,1,0:T(8,128)(2,1)} %get-tuple-element.83.refs_0_, bf16[2,448,1024]{2,1,0:T(8,128)(2,1)} %get-tuple-element.81.refs_1_, bf16[2,448,1024]{2,1,0:T(8,128)(2,1)} %copy-done.4, ...), custom_call_target="tpu_custom_call", output_to_operand_aliasing={{}: (10, {})} | custom-call | flops 8220835840 | bytes 35553280 | tf_op jit(solution)/shard_map/pallas_call | solution.py:185
  571.8 19.9 %shard_map.62 = bf16[5,50176,128]{2,1,0:T(8,128)(2,1)} custom-call(s32[123]{0:T(128)} %fusion.10.table_ref, bf16[2,448,1024]{2,1,0:T(8,128)(2,1)} %get-tuple-element.84.refs_0_, bf16[2,448,1024]{2,1,0:T(8,128)(2,1)} %get-tuple-element.82.refs_1_, bf16[2,448,1024]{2,1,0:T(8,128)(2,1)} %copy-done.3, ...), custom_call_target="tpu_custom_call", output_to_operand_aliasing={{}: (10, {})} | custom-call | flops 8220835840 | bytes 35553280 | tf_op jit(solution)/shard_map/pallas_call | solution.py:185
  (70 shorter events, 49.4 us)
Async XLA Ops:
  6.5 94.7 %all-gather.2.cloned.1.call-start = ((), (), s32[]{:S(2)}) async-start(), calls=%async_computation | async-start | bytes 4718592 | tf_op jit(solution)/shard_map/all_gather | solution.py:266
  6.5 15.9 %collective-permute-start = (bf16[256,1024]{1,0:T(8,128)(2,1)}, bf16[256,1024]{1,0:T(8,128)(2,1)S(1)}, u32[]{:S(2)}, u32[]{:S(2)}) collective-permute-start(bf16[256,1024]{1,0:T(8,128)(2,1)} %param.5), channel_id=1, source_target_pairs={{0,0},{1,8},{2,16},{3,24},{4,4},{5,12},{6,20},{7,28},{8,9},{9,17},... | collective-permute-start | bytes 1572872 | tf_op jit(solution)/shard_map/ppermute | solution.py:263
  27.0 30.5 %collective-permute-start.1 = (bf16[2,896,256]{1,2,0:T(8,128)(2,1)}, bf16[2,896,256]{1,2,0:T(8,128)(2,1)S(1)}, u32[]{:S(2)}, u32[]{:S(2)}) collective-permute-start(bf16[2,896,256]{1,2,0:T(8,128)(2,1)} %get-tuple-element.96), channel_id=1, source_target_pairs={{0,1},{1,2},{2,3},{3,0},{4,5},{5,6},{6,7},{7,4},{8,9},{9,10},{10,1... | collective-permute-start | bytes 2752520 | tf_op jit(solution)/shard_map/ppermute | solution.py:276
  39.0 39.5 %collective-permute-start.2 = (bf16[2,896,256]{1,2,0:T(8,128)(2,1)}, bf16[2,896,256]{1,2,0:T(8,128)(2,1)S(1)}, u32[]{:S(2)}, u32[]{:S(2)}) collective-permute-start(bf16[2,896,256]{1,2,0:T(8,128)(2,1)} %get-tuple-element.95), channel_id=1, source_target_pairs={{0,3},{1,0},{2,1},{3,2},{4,7},{5,4},{6,5},{7,6},{8,11},{9,8},{10,9... | collective-permute-start | bytes 2752520 | tf_op jit(solution)/shard_map/ppermute | solution.py:276
  57.5 57.6 %copy-start.5 = (bf16[2,896,256]{1,2,0:T(8,128)(2,1)}, bf16[2,896,256]{1,2,0:T(8,128)(2,1)S(1)}, u32[]{:S(2)}) copy-start(bf16[2,896,256]{1,2,0:T(8,128)(2,1)S(1)} %collective-permute-done.1) | copy-start | bytes 2752516
  78.5 36.6 %copy-start.6 = (bf16[2,896,256]{1,2,0:T(8,128)(2,1)}, bf16[2,896,256]{1,2,0:T(8,128)(2,1)S(1)}, u32[]{:S(2)}) copy-start(bf16[2,896,256]{1,2,0:T(8,128)(2,1)S(1)} %collective-permute-done.2) | copy-start | bytes 2752516
  120.6 19.7 %collective-permute-start.3 = (bf16[896,1024]{1,0:T(8,128)(2,1)}, bf16[896,1024]{1,0:T(8,128)(2,1)}, u32[]{:S(2)}, u32[]{:S(2)}) collective-permute-start(bf16[896,1024]{1,0:T(8,128)(2,1)} %get-tuple-element.80), channel_id=1, source_target_pairs={{0,1},{4,5},{8,9},{12,13},{16,17},{20,21},{24,25},{28,29}} | collective-permute-start | bytes 5505032 | tf_op jit(solution)/shard_map/ppermute | solution.py:318
  122.5 41.6 %collective-permute-start.4 = (bf16[896,1024]{1,0:T(8,128)(2,1)}, bf16[896,1024]{1,0:T(8,128)(2,1)}, u32[]{:S(2)}, u32[]{:S(2)}) collective-permute-start(bf16[896,1024]{1,0:T(8,128)(2,1)} %get-tuple-element.79), channel_id=1, source_target_pairs={{3,2},{7,6},{11,10},{15,14},{19,18},{23,22},{27,26},{31,30}} | collective-permute-start | bytes 5505032 | tf_op jit(solution)/shard_map/ppermute | solution.py:319
  126.0 103.8 %slice-start = ((s8[7340032]{0:T(1024)(128)(4,1)}), s8[4194304]{0:T(1024)(128)(4,1)S(1)}, s32[]{:S(2)}) async-start(s8[7340032]{0:T(1024)(128)(4,1)} %bitcast.76), calls=%async_computation.1 | async-start | bytes 8388608
  126.0 103.8 %slice-start.1 = ((s8[7340032]{0:T(1024)(128)(4,1)}), s8[3145728]{0:T(1024)(128)(4,1)S(1)}, s32[]{:S(2)}) async-start(s8[7340032]{0:T(1024)(128)(4,1)} %bitcast.76), calls=%async_computation.2 | async-start | bytes 6291456
  126.0 57.8 %collective-permute-start.5 = (bf16[2,896,256]{1,2,0:T(8,128)(2,1)}, bf16[2,896,256]{1,2,0:T(8,128)(2,1)}, u32[]{:S(2)}, u32[]{:S(2)}) collective-permute-start(bf16[2,896,256]{1,2,0:T(8,128)(2,1)} %get-tuple-element.93), channel_id=1, source_target_pairs={{0,2},{1,3},{2,0},{3,1},{4,6},{5,7},{6,4},{7,5},{8,10},{9,11},{10,... | collective-permute-start | bytes 2752520 | tf_op jit(solution)/shard_map/ppermute | solution.py:276
  188.1 3.6 collective-permute-start.6
  188.9 40.9 %collective-permute-start.7 = (bf16[896,1024]{1,0:T(8,128)(2,1)S(1)}, bf16[896,1024]{1,0:T(8,128)(2,1)S(1)}, u32[]{:S(2)}, u32[]{:S(2)}) collective-permute-start(bf16[896,1024]{1,0:T(8,128)(2,1)S(1)} %get-tuple-element.77), channel_id=1, source_target_pairs={{2,1},{3,2},{6,5},{7,6},{10,9},{11,10},{14,13},{15,14},{18,17},{19... | collective-permute-start | bytes 5505032 | tf_op jit(solution)/shard_map/ppermute | solution.py:319
  233.3 44.3 %collective-permute-start.8 = (bf16[896,1024]{1,0:T(8,128)(2,1)}, bf16[896,1024]{1,0:T(8,128)(2,1)}, u32[]{:S(2)}, u32[]{:S(2)}) collective-permute-start(bf16[896,1024]{1,0:T(8,128)(2,1)} %get-tuple-element.76), channel_id=1, source_target_pairs={{0,1},{1,2},{2,3},{4,5},{5,6},{6,7},{8,9},{9,10},{10,11},{12,13},{... | collective-permute-start | bytes 5505032 | tf_op jit(solution)/shard_map/ppermute | solution.py:318
  234.6 43.9 %collective-permute-start.9 = (bf16[896,1024]{1,0:T(8,128)(2,1)}, bf16[896,1024]{1,0:T(8,128)(2,1)}, u32[]{:S(2)}, u32[]{:S(2)}) collective-permute-start(bf16[896,1024]{1,0:T(8,128)(2,1)} %get-tuple-element.75), channel_id=1, source_target_pairs={{1,0},{2,1},{3,2},{5,4},{6,5},{7,6},{9,8},{10,9},{11,10},{13,12},{... | collective-permute-start | bytes 5505032 | tf_op jit(solution)/shard_map/ppermute | solution.py:319
  248.6 29.8 %slice-start.2 = ((s8[7340032]{0:T(1024)(128)(4,1)}), s8[3145728]{0:T(1024)(128)(4,1)S(1)}, s32[]{:S(2)}) async-start(s8[7340032]{0:T(1024)(128)(4,1)} %bitcast.78), calls=%async_computation.3 | async-start | bytes 6291456
  253.2 25.2 %slice-start.3 = ((s8[7340032]{0:T(1024)(128)(4,1)}), s8[4194304]{0:T(1024)(128)(4,1)S(1)}, s32[]{:S(2)}) async-start(s8[7340032]{0:T(1024)(128)(4,1)} %bitcast.78), calls=%async_computation.4 | async-start | bytes 8388608
  284.3 81.1 %collective-permute-start.10 = (bf16[2,896,1024]{2,1,0:T(8,128)(2,1)}, bf16[2,896,1024]{2,1,0:T(8,128)(2,1)}, u32[]{:S(2)}, u32[]{:S(2)}) collective-permute-start(bf16[2,896,1024]{2,1,0:T(8,128)(2,1)} %pad_maximum_fusion.2.refs_0_.refs_1_.refs_3_.refs_6_.refs_4_), channel_id=1, source_target_pairs={{0,1},{1,2},{2,3},{4,5},{5,6},{6,7},{8,9},{9,10},{10,11},{12,13},{... | collective-permute-start | bytes 11010056 | tf_op jit(solution)/shard_map/ppermute | solution.py:337
  285.6 80.7 %collective-permute-start.11 = (bf16[2,896,1024]{2,1,0:T(8,128)(2,1)}, bf16[2,896,1024]{2,1,0:T(8,128)(2,1)}, u32[]{:S(2)}, u32[]{:S(2)}) collective-permute-start(bf16[2,896,1024]{2,1,0:T(8,128)(2,1)} %pad_maximum_fusion.2.refs_0_.refs_1_.refs_3_.refs_6_.refs_4_), channel_id=1, source_target_pairs={{1,0},{2,1},{3,2},{5,4},{6,5},{7,6},{9,8},{10,9},{11,10},{13,12},{... | collective-permute-start | bytes 11010056 | tf_op jit(solution)/shard_map/ppermute | solution.py:338
  292.2 78.8 %collective-permute-start.12 = (bf16[2,896,1024]{2,1,0:T(8,128)(2,1)}, bf16[2,896,1024]{2,1,0:T(8,128)(2,1)}, u32[]{:S(2)}, u32[]{:S(2)}) collective-permute-start(bf16[2,896,1024]{2,1,0:T(8,128)(2,1)} %pad_maximum_fusion.2.refs_0_.refs_1_.refs_3_.refs_6_.refs_4_), channel_id=1, source_target_pairs={{0,8},{4,12},{8,16},{12,20},{16,24},{20,28},{24,0},{28,4},{1,9},{5... | collective-permute-start | bytes 11010056 | tf_op jit(solution)/shard_map/ppermute | solution.py:356
  375.3 26.8 %collective-permute-start.15 = (bf16[2,896,1024]{2,1,0:T(8,128)(2,1)}, bf16[2,896,1024]{2,1,0:T(8,128)(2,1)}, u32[]{:S(2)}, u32[]{:S(2)}) collective-permute-start(bf16[2,896,1024]{2,1,0:T(8,128)(2,1)} %broadcast_select_fusion.1), channel_id=1, source_target_pairs={{0,4},{4,0},{8,12},{12,8},{16,20},{20,16},{24,28},{28,24},{1,5},{5... | collective-permute-start | bytes 11010056 | tf_op jit(solution)/shard_map/ppermute | solution.py:352
  379.4 22.6 %collective-permute-start.13 = (bf16[2,896,1024]{2,1,0:T(8,128)(2,1)}, bf16[2,896,1024]{2,1,0:T(8,128)(2,1)S(1)}, u32[]{:S(2)}, u32[]{:S(2)}) collective-permute-start(bf16[2,896,1024]{2,1,0:T(8,128)(2,1)} %collective-permute-done.11.refs_1_), channel_id=1, source_target_pairs={{1,0},{2,1},{5,4},{6,5},{9,8},{10,9},{13,12},{14,13},{17,16},{18,1... | collective-permute-start | bytes 11010056 | tf_op jit(solution)/shard_map/ppermute | solution.py:338
  380.3 86.9 %collective-permute-start.14 = (bf16[2,896,1024]{2,1,0:T(8,128)(2,1)}, bf16[2,896,1024]{2,1,0:T(8,128)(2,1)S(1)}, u32[]{:S(2)}, u32[]{:S(2)}) collective-permute-start(bf16[2,896,1024]{2,1,0:T(8,128)(2,1)} %collective-permute-done.10.refs_2_.refs_3_), channel_id=1, source_target_pairs={{1,2},{2,3},{5,6},{6,7},{9,10},{10,11},{13,14},{14,15},{17,18},{18... | collective-permute-start | bytes 11010056 | tf_op jit(solution)/shard_map/ppermute | solution.py:337
  381.8 85.4 %collective-permute-start.16 = (bf16[2,896,1024]{2,1,0:T(8,128)(2,1)}, bf16[2,896,1024]{2,1,0:T(8,128)(2,1)}, u32[]{:S(2)}, u32[]{:S(2)}) collective-permute-start(bf16[2,896,1024]{2,1,0:T(8,128)(2,1)} %pad_maximum_fusion.2.refs_0_.refs_1_.refs_3_.refs_6_.refs_4_), channel_id=1, source_target_pairs={{0,16},{4,20},{8,24},{12,28},{16,0},{20,4},{24,8},{28,12},{1,17},{... | collective-permute-start | bytes 11010056 | tf_op jit(solution)/shard_map/ppermute | solution.py:356
  402.1 74.9 %copy-start = (bf16[2,896,1024]{2,1,0:T(8,128)(2,1)}, bf16[2,896,1024]{2,1,0:T(8,128)(2,1)S(1)}, u32[]{:S(2)}) copy-start(bf16[2,896,1024]{2,1,0:T(8,128)(2,1)S(1)} %collective-permute-done.13.refs_4_) | copy-start | bytes 11010052
  467.2 13.2 %copy-start.2 = (bf16[2,896,1024]{2,1,0:T(8,128)(2,1)}, bf16[2,896,1024]{2,1,0:T(8,128)(2,1)S(1)}, u32[]{:S(2)}) copy-start(bf16[2,896,1024]{2,1,0:T(8,128)(2,1)S(1)} %collective-permute-done.14.refs_5_) | copy-start | bytes 11010052
  472.8 58.5 %collective-permute-start.21 = (bf16[2,896,1024]{2,1,0:T(8,128)(2,1)}, bf16[2,896,1024]{2,1,0:T(8,128)(2,1)}, u32[]{:S(2)}, u32[]{:S(2)}) collective-permute-start(bf16[2,896,1024]{2,1,0:T(8,128)(2,1)} %broadcast_select_fusion), channel_id=1, source_target_pairs={{0,4},{4,0},{8,12},{12,8},{16,20},{20,16},{24,28},{28,24},{1,5},{5... | collective-permute-start | bytes 11010056 | tf_op jit(solution)/shard_map/ppermute | solution.py:352
  475.7 51.1 %collective-permute-start.17 = (bf16[2,448,1024]{2,1,0:T(8,128)(2,1)}, bf16[2,448,1024]{2,1,0:T(8,128)(2,1)}, u32[]{:S(2)}, u32[]{:S(2)}) collective-permute-start(bf16[2,448,1024]{2,1,0:T(8,128)(2,1)} %get-tuple-element.87), channel_id=1, source_target_pairs={{2,3},{6,7},{10,11},{14,15},{18,19},{22,23},{26,27},{30,31}} | collective-permute-start | bytes 5505032 | tf_op jit(solution)/shard_map/ppermute | solution.py:337
  479.2 47.6 %collective-permute-start.18 = (bf16[2,448,1024]{2,1,0:T(8,128)(2,1)}, bf16[2,448,1024]{2,1,0:T(8,128)(2,1)S(1)}, u32[]{:S(2)}, u32[]{:S(2)}) collective-permute-start(bf16[2,448,1024]{2,1,0:T(8,128)(2,1)} %get-tuple-element.85), channel_id=1, source_target_pairs={{1,0},{5,4},{9,8},{13,12},{17,16},{21,20},{25,24},{29,28}} | collective-permute-start | bytes 5505032 | tf_op jit(solution)/shard_map/ppermute | solution.py:338
  482.6 46.5 %copy-start.1 = (bf16[2,896,1024]{2,1,0:T(8,128)(2,1)S(1)}, bf16[2,896,1024]{2,1,0:T(8,128)(2,1)}, u32[]{:S(2)}) copy-start(bf16[2,896,1024]{2,1,0:T(8,128)(2,1)} %copy-done) | copy-start | bytes 11010052
  526.8 43.8 %collective-permute-start.19 = (bf16[2,448,1024]{2,1,0:T(8,128)(2,1)}, bf16[2,448,1024]{2,1,0:T(8,128)(2,1)S(1)}, u32[]{:S(2)}, u32[]{:S(2)}) collective-permute-start(bf16[2,448,1024]{2,1,0:T(8,128)(2,1)} %get-tuple-element.68), channel_id=1, source_target_pairs={{1,0},{5,4},{9,8},{13,12},{17,16},{21,20},{25,24},{29,28}} | collective-permute-start | bytes 5505032 | tf_op jit(solution)/shard_map/ppermute | solution.py:338
  527.6 44.1 %collective-permute-start.20 = (bf16[2,448,1024]{2,1,0:T(8,128)(2,1)}, bf16[2,448,1024]{2,1,0:T(8,128)(2,1)}, u32[]{:S(2)}, u32[]{:S(2)}) collective-permute-start(bf16[2,448,1024]{2,1,0:T(8,128)(2,1)} %get-tuple-element.69), channel_id=1, source_target_pairs={{2,3},{6,7},{10,11},{14,15},{18,19},{22,23},{26,27},{30,31}} | collective-permute-start | bytes 5505032 | tf_op jit(solution)/shard_map/ppermute | solution.py:337
  (3 other events, 6.5 us)
Sparse Core Ops, SparseCore 0:
  23.4 77.7 all-gather.1

commit v6 on v5

--- a/solution.py
+++ b/solution.py
@@ -265,9 +265,9 @@
     sent, saved = tie(sent, saved)
     features = lax.all_gather(sent, "tensor", axis=0, tiled=True)
 
-    def saved_pieces(chunk, saved):
+    def saved_pieces(chunk, saved, nothing):
         def part(index):
-            first = (index % groups) * slice_width + chunk * chunk_rows
+            first = (index % groups) * slice_width + chunk * chunk_rows + nothing
             return lax.dynamic_slice_in_dim(saved, first, chunk_rows, 1)
 
         pieces = [part(own_group)]
@@ -286,17 +286,24 @@
             axis=2,
         )
 
-    first_saved = saved_pieces(0, saved)
-    features, first_saved[1], first_saved[-1] = tie(features, first_saved[1], first_saved[-1])
+    arrived = sent[:16, :LANES]
+    signs = [
+        lax.ppermute(arrived, "dp", [(d, (d + shift) % groups) for d in range(groups)])
+        for shift in range(1, groups)
+    ]
+    nothing = sum(jnp.minimum(jnp.abs(sign[0, 0].astype(jnp.float32)), 0.0) for sign in signs)
+    first_saved = saved_pieces(0, saved, nothing.astype(jnp.int32))
     features = features.reshape(groups, per_group, local_tokens, local_features)
 
     def partial_products(chunk, offsets, features):
+        count = len(offsets[0])
         if use_kernels:
             base = bases["hidden", chunk, offsets]
-            return hidden_parts(down_weight, features, chunk_rows, table, base, len(offsets))
+            return hidden_parts(down_weight, features, chunk_rows, table, base, count)
         ordered = jnp.roll(features, -own_group, axis=0)
+        own_offsets = jnp.asarray(np.array(offsets, np.int32))[own_group]
         made = []
-        for offset in offsets:
+        for offset in [own_offsets[place] for place in range(count)]:
             first = (own_group + offset) % groups * slice_width + chunk * chunk_rows
             part = lax.dynamic_slice_in_dim(down_weight, first, chunk_rows, 0)
             made.append(
@@ -310,6 +317,10 @@
         return jnp.stack(made)
 
     def reduce_step(partial, step, received):
+        if step == 1 and groups > 3:
+            ends = [(0, 1), (groups - 1, groups - 2)]
+            moved = lax.ppermute(partial("first").astype(jnp.bfloat16), "dp", ends)
+            return moved, moved
         right, left = partial(groups - step), partial(step)
         if received is not None:
             right = right + received[0].astype(jnp.float32)
@@ -412,16 +423,21 @@
             position = position * LAST_PARTS + part
         return position, choice
 
-    first_offsets = tuple(sorted({1, groups - 1}))
-    other_offsets = tuple(o for o in range(groups) if o not in first_offsets)
-    all_offsets = tuple(range(groups))
+    middle = (0, *range(2, groups - 1))
+    first_offsets = tuple((groups - 1,) if d == 0 else (1,) for d in range(groups))
+    other_offsets = tuple(
+        (*middle, 1) if d == 0 else (*middle, groups - 1) for d in range(groups)
+    )
+    all_offsets = tuple(
+        (*first_offsets[d], *other_offsets[d]) for d in range(groups)
+    )
     hidden_calls = [(0, first_offsets), (0, other_offsets)]
     hidden_calls += [(chunk, all_offsets) for chunk in range(1, CHUNKS)]
     bases, lines = {}, [[] for _ in range(groups)]
     for chunk, offsets in hidden_calls:
         bases["hidden", chunk, offsets] = len(lines[0])
         for d in range(groups):
-            lines[d] += [(d + offset) % groups * CHUNKS + chunk for offset in offsets]
+            lines[d] += [(d + offset) % groups * CHUNKS + chunk for offset in offsets[d]]
             lines[d] += [(d + g) % groups for g in range(groups)]
     for time, plan in calls.items():
         bases["factor", time] = len(lines[0])
@@ -451,15 +467,23 @@
             pieces, parts, plan, table, base, result, band, groups, inverse_count
         )
 
-    def lookup(*made):
-        return lambda offset: next(
-            array[offsets.index(offset)] for offsets, array in made if offset in offsets
-        )
+    def lookup(first, others):
+        def partial(offset):
+            if offset == "first":
+                return first
+            if offset in middle:
+                return others[middle.index(offset)]
+            return jnp.where((own_group == 0) == (offset == 1), others[len(middle)], first)
+
+        return partial
 
     first_parts = partial_products(0, first_offsets, features)
+    first_parts, first_saved[1], first_saved[-1] = tie(
+        first_parts, first_saved[1], first_saved[-1]
+    )
     other_parts = partial_products(0, other_offsets, features)
-    partial = lookup((first_offsets, first_parts), (other_offsets, other_parts))
-    later_saved = [saved_pieces(chunk, saved) for chunk in range(1, CHUNKS)]
+    partial = lookup(first_parts[0], other_parts)
+    later_saved = [saved_pieces(chunk, saved, 0) for chunk in range(1, CHUNKS)]
     received = None
     for step in range(1, groups):
         received = tie(*reduce_step(partial, step, received))
@@ -516,7 +540,7 @@
                 received, moved = moved[: len(received)], moved[len(received) :]
                 found = dict(zip(keys, moved))
                 if new_parts:
-                    partial = lookup((all_offsets, moved[-1]))
+                    partial = lookup(moved[-1][0], moved[-1][1:])
                 if result is not None:
                     result, left, right = tie(result, left, right)
         column.update(partner_step(groups, found))

time: 610 us -> 593 us (0.972)
  waiting for transfers between devices: 308 us -> 285 us
  other arithmetic: 32.4 us -> 39.3 us
    ppermute x3, waiting for transfers between devices: 58 us -> 19.8 us  [saved_pieces(): pieces.append(lax.ppermute(part(own_group + shift), 'dp', ring))]
    ppermute x3 -> x2, waiting for transfers between devices: 62.8 us -> 37.6 us  [reduce_step(): lax.ppermute(left.astype(jnp.bfloat16), 'dp', [(d, d - 1) for d in range(...]
    ppermute x0 -> x4, waiting for transfers between devices: none -> 22.6 us  [the longest x1 21.1 us: reduce_step(): moved = lax.ppermute(partial('first').astype(jnp.bfloat16), 'dp', ends)]
    ppermute x0 -> x4, starting transfers between devices: none -> 15.1 us  [the longest x3 12.8 us: per_device(): lax.ppermute(arrived, 'dp', [(d, (d + shift) % groups) for d in range(gro...]
    all_gather x1, waiting for transfers between devices: 22.7 us -> 33.2 us  [per_device(): features = lax.all_gather(sent, 'tensor', axis=0, tiled=True)]
    ppermute x3, starting transfers between devices: 12 us -> 1.98 us  [saved_pieces(): pieces.append(lax.ppermute(part(own_group + shift), 'dp', ring))]
    ppermute x3 -> x2, waiting for transfers between devices: 21.7 us -> 25 us  [reduce_step(): lax.ppermute(right.astype(jnp.bfloat16), 'dp', [(d, d + 1) for d in range...]
    ppermute x3 -> x2, starting transfers between devices: 14 us -> 10.9 us  [reduce_step(): lax.ppermute(left.astype(jnp.bfloat16), 'dp', [(d, d - 1) for d in range(...]
  transfers between devices with their start and end apart: 23 -> 25, of which waited for: 14 -> 13; matrix products, arithmetic and copies ran while one was open for 5% -> 6% of each run, Pallas kernels for 21% -> 24%
where the time goes in v6:
time: 593 us; the launch traced here: 583 us
  waiting for transfers between devices  285 us (48%)
  Pallas kernels  161 us (27%)
  starting transfers between devices  56.9 us (10%)
  other arithmetic  39.3 us (7%)
  local copies, waits for them, and re-layouts  25.5 us (4%)
  between operations  15.7 us (3%)
    pallas_call x6, Pallas kernels, factor_rows(): pl.pallas_call(functools.partial(factor_kernel, (len(keys), chunk_total,...  133 us
    ppermute x4, waiting for transfers between devices, gather_step(): lax.ppermute(left, 'dp', [(d, d + 1) for d in range(step - 1, groups - 1)])  126 us
    ppermute x2, waiting for transfers between devices, reduce_step(): lax.ppermute(left.astype(jnp.bfloat16), 'dp', [(d, d - 1) for d in range(...  37.6 us
    all_gather x1, waiting for transfers between devices, per_device(): features = lax.all_gather(sent, 'tensor', axis=0, tiled=True)  33.2 us
    pallas_call x2, Pallas kernels, hidden_parts(): pl.pallas_call(functools.partial(hidden_kernel, base + count), grid_spec=...  27.6 us
    ppermute x2, waiting for transfers between devices, reduce_step(): lax.ppermute(right.astype(jnp.bfloat16), 'dp', [(d, d + 1) for d in range...  25 us
    ppermute x1, waiting for transfers between devices, reduce_step(): moved = lax.ppermute(partial('first').astype(jnp.bfloat16), 'dp', ends)  21.1 us
    ppermute x3, waiting for transfers between devices, saved_pieces(): pieces.append(lax.ppermute(part(own_group + shift), 'dp', ring))  19.8 us
  transfers between devices with their start and end apart: 25, of which 13 were waited for; matrix products, arithmetic and copies ran while one was open for 6% of the time, Pallas kernels for 24%

profile of v6, /device:TPU:29, one launch (start us, length us, event | category | flops | bytes accessed | tf_op | source)
XLA Modules:
  0.0 583.1 jit_solution(7067034663723993016)
XLA Ops:
  6.5 2.9 collective-permute-start
  9.5 4.2 pad_maximum_fusion
  13.7 8.8 %collective-permute-done = bf16[256,1024]{1,0:T(8,128)(2,1)S(1)} collective-permute-done((bf16[256,1024]{1,0:T(8,128)(2,1)}, bf16[256,1024]{1,0:T(8,128)(2,1)S(1)}, u32[]{:S(2)}, u32[]{:S(2)}) %collective-permute-start) | collective-permute-done | bytes 524320 | tf_op jit(solution)/shard_map/ppermute | solution.py:263
  24.0 12.0 %collective-permute-start.1 = (bf16[16,128]{1,0:T(8,128)(2,1)S(1)}, bf16[16,128]{1,0:T(8,128)(2,1)S(1)}, u32[]{:S(2)}, u32[]{:S(2)}) collective-permute-start(bf16[16,128]{1,0:T(8,128)(2,1)S(1)} %slice.55), channel_id=1, source_target_pairs={{0,1},{1,2},{2,3},{3,0},{4,5},{5,6},{6,7},{7,4},{8,9},{9,10},{10,1... | collective-permute-start | bytes 12296 | tf_op jit(solution)/shard_map/ppermute | solution.py:291
  41.5 5.8 constant_dynamic-slice_fusion.4
  50.4 33.2 %all-gather.2.cloned.1.call-done = bf16[2048,1024]{1,0:T(8,128)(2,1)} async-done(((bf16[256,1024]{1,0:T(8,128)(2,1)}), bf16[2048,1024]{1,0:T(8,128)(2,1)}) %all-gather.2.cloned.1.call-update) | async-done | bytes 4194320 | tf_op jit(solution)/shard_map/all_gather | solution.py:266
  83.6 9.8 %shard_map.56 = f32[1,896,1024]{2,1,0:T(8,128)} custom-call(s32[123]{0:T(128)} %fusion.10.table_ref, bf16[3584,2048]{1,0:T(8,128)(2,1)} %weight_ref.3, bf16[4,2,256,1024]{3,2,1,0:T(8,128)(2,1)} %bitcast.75), custom_call_target="tpu_custom_call" | custom-call | flops 3758096384 | bytes 11534336 | tf_op jit(solution)/shard_map/pallas_call | solution.py:36
  93.4 3.0 convert_bitcast_fusion
  98.7 17.8 %shard_map.55 = f32[3,896,1024]{2,1,0:T(8,128)} custom-call(s32[123]{0:T(128)} %fusion.10.table_ref, bf16[3584,2048]{1,0:T(8,128)(2,1)} %weight_ref.3, bf16[4,2,256,1024]{3,2,1,0:T(8,128)(2,1)} %bitcast.76), custom_call_target="tpu_custom_call" | custom-call | flops 11274289152 | bytes 26214400 | tf_op jit(solution)/shard_map/pallas_call | solution.py:36
  116.6 21.1 %collective-permute-done.6 = bf16[896,1024]{1,0:T(8,128)(2,1)S(1)} collective-permute-done((bf16[896,1024]{1,0:T(8,128)(2,1)S(1)}, bf16[896,1024]{1,0:T(8,128)(2,1)S(1)}, u32[]{:S(2)}, u32[]{:S(2)}) %collective-permute-start.6) | collective-permute-done | bytes 1835040 | tf_op jit(solution)/shard_map/ppermute | solution.py:322
  137.7 19.8 %collective-permute-done.7 = bf16[2,896,256]{1,2,0:T(8,128)(2,1)S(1)} collective-permute-done((bf16[2,896,256]{1,2,0:T(8,128)(2,1)}, bf16[2,896,256]{1,2,0:T(8,128)(2,1)S(1)}, u32[]{:S(2)}, u32[]{:S(2)}) %collective-permute-start.7) | collective-permute-done | bytes 917536 | tf_op jit(solution)/shard_map/ppermute | solution.py:276
  157.4 4.5 add_convert_fusion
  163.8 4.8 collective-permute-start.9
  168.7 36.7 %collective-permute-done.9 = bf16[896,1024]{1,0:T(8,128)(2,1)} collective-permute-done((bf16[896,1024]{1,0:T(8,128)(2,1)S(1)}, bf16[896,1024]{1,0:T(8,128)(2,1)}, u32[]{:S(2)}, u32[]{:S(2)}) %collective-permute-start.9) | collective-permute-done | bytes 1835040 | tf_op jit(solution)/shard_map/ppermute | solution.py:330
  205.4 7.5 %fusion.6 = (bf16[896,1024]{1,0:T(8,128)(2,1)}, bf16[896,1024]{1,0:T(8,128)(2,1)}) fusion(bf16[896,1024]{1,0:T(8,128)(2,1)} %collective-permute-done.9, f32[1,896,1024]{2,1,0:T(8,128)} %shard_map.56, f32[3,896,1024]{2,1,0:T(8,128)} %shard_map.55, pred[]{:T(512)S(6)} %eq.23, bf16[896,1024]{1,0:T(8,128)(2,1)} %collective-permute-done.8, pred[]{:T(512)S(6)} %eq.22), kind=kLoop, calls=%fused_computation.15 | loop fusion | flops 7340032 | bytes 14680066 | tf_op jit(solution)/shard_map/convert_element_type | solution.py:331
  214.2 6.1 %collective-permute-start.11 = (bf16[896,1024]{1,0:T(8,128)(2,1)}, bf16[896,1024]{1,0:T(8,128)(2,1)}, u32[]{:S(2)}, u32[]{:S(2)}) collective-permute-start(bf16[896,1024]{1,0:T(8,128)(2,1)} %get-tuple-element.75), channel_id=1, source_target_pairs={{1,0},{2,1},{3,2},{5,4},{6,5},{7,6},{9,8},{10,9},{11,10},{13,12},{... | collective-permute-start | bytes 5505032 | tf_op jit(solution)/shard_map/ppermute | solution.py:330
  230.8 25.0 %collective-permute-done.10 = bf16[896,1024]{1,0:T(8,128)(2,1)} collective-permute-done((bf16[896,1024]{1,0:T(8,128)(2,1)}, bf16[896,1024]{1,0:T(8,128)(2,1)}, u32[]{:S(2)}, u32[]{:S(2)}) %collective-permute-start.10) | collective-permute-done | bytes 1835040 | tf_op jit(solution)/shard_map/ppermute | solution.py:329
  256.7 4.3 fusion.9
  264.4 6.6 %collective-permute-start.13 = (bf16[2,896,1024]{2,1,0:T(8,128)(2,1)}, bf16[2,896,1024]{2,1,0:T(8,128)(2,1)}, u32[]{:S(2)}, u32[]{:S(2)}) collective-permute-start(bf16[2,896,1024]{2,1,0:T(8,128)(2,1)} %pad_maximum_fusion.2.refs_0_.refs_1_.refs_3_.refs_6_.refs_4_), channel_id=1, source_target_pairs={{1,0},{2,1},{3,2},{5,4},{6,5},{7,6},{9,8},{10,9},{11,10},{13,12},{... | collective-permute-start | bytes 11010056 | tf_op jit(solution)/shard_map/ppermute | solution.py:349
  271.0 2.6 collective-permute-start.14
  273.6 10.2 %shard_map.57.refs_5_ = bf16[5,50176,128]{2,1,0:T(8,128)(2,1)} custom-call(s32[123]{0:T(128)} %fusion.10.table_ref, bf16[2,896,1024]{2,1,0:T(8,128)(2,1)} %pad_maximum_fusion.2.refs_0_.refs_1_.refs_3_.refs_6_.refs_4_, bf16[2,896,1024]{2,1,0:T(8,128)(2,1)} %pad_maximum_fusion.2.refs_0_.refs_1_.refs_3_.refs_6_.refs_4_), custom_call_target="tpu_custom_call" | custom-call | flops 3288334336 | bytes 10551296 | tf_op jit(solution)/shard_map/pallas_call | solution.py:185
  283.8 60.4 %collective-permute-done.12.refs_2_.refs_3_ = bf16[2,896,1024]{2,1,0:T(8,128)(2,1)} collective-permute-done((bf16[2,896,1024]{2,1,0:T(8,128)(2,1)}, bf16[2,896,1024]{2,1,0:T(8,128)(2,1)}, u32[]{:S(2)}, u32[]{:S(2)}) %collective-permute-start.12) | collective-permute-done | bytes 3670048 | tf_op jit(solution)/shard_map/ppermute | solution.py:348
  345.2 10.8 %collective-permute-done.14.refs_4_.refs_8_.refs_6_ = bf16[2,896,1024]{2,1,0:T(8,128)(2,1)} collective-permute-done((bf16[2,896,1024]{2,1,0:T(8,128)(2,1)}, bf16[2,896,1024]{2,1,0:T(8,128)(2,1)}, u32[]{:S(2)}, u32[]{:S(2)}) %collective-permute-start.14) | collective-permute-done | bytes 3670048 | tf_op jit(solution)/shard_map/ppermute | solution.py:367
  355.9 4.2 broadcast_select_fusion.1
  360.2 4.3 collective-permute-start.17
  366.9 19.6 %shard_map.58.refs_10_ = bf16[5,50176,128]{2,1,0:T(8,128)(2,1)} custom-call(s32[123]{0:T(128)} %fusion.10.table_ref, bf16[2,896,1024]{2,1,0:T(8,128)(2,1)} %pad_maximum_fusion.2.refs_0_.refs_1_.refs_3_.refs_6_.refs_4_, bf16[2,896,1024]{2,1,0:T(8,128)(2,1)} %collective-permute-done.13.refs_1_, ...), custom_call_target="tpu_custom_call", output_to_operand_aliasing={{}: (6, {})} | custom-call | flops 9865003008 | bytes 27983872 | tf_op jit(solution)/shard_map/pallas_call | solution.py:185
  386.6 64.9 %collective-permute-done.16.refs_5_ = bf16[2,896,1024]{2,1,0:T(8,128)(2,1)S(1)} collective-permute-done((bf16[2,896,1024]{2,1,0:T(8,128)(2,1)}, bf16[2,896,1024]{2,1,0:T(8,128)(2,1)S(1)}, u32[]{:S(2)}, u32[]{:S(2)}) %collective-permute-start.16) | collective-permute-done | bytes 3670048 | tf_op jit(solution)/shard_map/ppermute | solution.py:348
  451.5 5.6 broadcast_select_fusion
  466.9 44.2 %shard_map.59.refs_7_ = bf16[5,50176,128]{2,1,0:T(8,128)(2,1)} custom-call(s32[123]{0:T(128)} %fusion.10.table_ref, bf16[2,896,1024]{2,1,0:T(8,128)(2,1)} %pad_maximum_fusion.2.refs_0_.refs_1_.refs_3_.refs_6_.refs_4_, bf16[2,896,1024]{2,1,0:T(8,128)(2,1)} %collective-permute-done.13.refs_1_, ...), custom_call_target="tpu_custom_call", output_to_operand_aliasing={{}: (11, {})} | custom-call | flops 26306674688 | bytes 69730304 | tf_op jit(solution)/shard_map/pallas_call | solution.py:185
  515.7 19.6 %shard_map.60.refs_9_ = bf16[5,50176,128]{2,1,0:T(8,128)(2,1)} custom-call(s32[123]{0:T(128)} %fusion.10.table_ref, bf16[2,896,1024]{2,1,0:T(8,128)(2,1)} %pad_maximum_fusion.2.refs_0_.refs_1_.refs_3_.refs_6_.refs_4_, bf16[2,896,1024]{2,1,0:T(8,128)(2,1)} %collective-permute-done.13.refs_1_, ...), custom_call_target="tpu_custom_call", output_to_operand_aliasing={{}: (8, {})} | custom-call | flops 9865003008 | bytes 24313856 | tf_op jit(solution)/shard_map/pallas_call | solution.py:185
  535.3 19.7 %shard_map.61.refs_9_ = bf16[5,50176,128]{2,1,0:T(8,128)(2,1)} custom-call(s32[123]{0:T(128)} %fusion.10.table_ref, bf16[2,448,1024]{2,1,0:T(8,128)(2,1)} %get-tuple-element.81.refs_0_, bf16[2,448,1024]{2,1,0:T(8,128)(2,1)} %get-tuple-element.79.refs_1_, bf16[2,448,1024]{2,1,0:T(8,128)(2,1)} %copy-done.5, ...), custom_call_target="tpu_custom_call", output_to_operand_aliasing={{}: (10, {})} | custom-call | flops 8220835840 | bytes 35553280 | tf_op jit(solution)/shard_map/pallas_call | solution.py:185
  556.2 19.9 %shard_map.62 = bf16[5,50176,128]{2,1,0:T(8,128)(2,1)} custom-call(s32[123]{0:T(128)} %fusion.10.table_ref, bf16[2,448,1024]{2,1,0:T(8,128)(2,1)} %get-tuple-element.82.refs_0_, bf16[2,448,1024]{2,1,0:T(8,128)(2,1)} %get-tuple-element.80.refs_1_, bf16[2,448,1024]{2,1,0:T(8,128)(2,1)} %copy-done.4, ...), custom_call_target="tpu_custom_call", output_to_operand_aliasing={{}: (10, {})} | custom-call | flops 8220835840 | bytes 35553280 | tf_op jit(solution)/shard_map/pallas_call | solution.py:185
  (76 shorter events, 47.5 us)
Async XLA Ops:
  6.5 77.1 %all-gather.2.cloned.1.call-start = ((), (), s32[]{:S(2)}) async-start(), calls=%async_computation | async-start | bytes 4718592 | tf_op jit(solution)/shard_map/all_gather | solution.py:266
  6.5 15.9 %collective-permute-start = (bf16[256,1024]{1,0:T(8,128)(2,1)}, bf16[256,1024]{1,0:T(8,128)(2,1)S(1)}, u32[]{:S(2)}, u32[]{:S(2)}) collective-permute-start(bf16[256,1024]{1,0:T(8,128)(2,1)} %param.5), channel_id=1, source_target_pairs={{0,0},{1,8},{2,16},{3,24},{4,4},{5,12},{6,20},{7,28},{8,9},{9,17},... | collective-permute-start | bytes 1572872 | tf_op jit(solution)/shard_map/ppermute | solution.py:263
  24.0 12.8 %collective-permute-start.1 = (bf16[16,128]{1,0:T(8,128)(2,1)S(1)}, bf16[16,128]{1,0:T(8,128)(2,1)S(1)}, u32[]{:S(2)}, u32[]{:S(2)}) collective-permute-start(bf16[16,128]{1,0:T(8,128)(2,1)S(1)} %slice.55), channel_id=1, source_target_pairs={{0,1},{1,2},{2,3},{3,0},{4,5},{5,6},{6,7},{7,4},{8,9},{9,10},{10,1... | collective-permute-start | bytes 12296 | tf_op jit(solution)/shard_map/ppermute | solution.py:291
  36.0 3.4 collective-permute-start.2
  36.0 4.4 collective-permute-start.3
  47.3 46.1 %collective-permute-start.4 = (bf16[2,896,256]{1,2,0:T(8,128)(2,1)}, bf16[2,896,256]{1,2,0:T(8,128)(2,1)S(1)}, u32[]{:S(2)}, u32[]{:S(2)}) collective-permute-start(bf16[2,896,256]{1,2,0:T(8,128)(2,1)} %get-tuple-element.94), channel_id=1, source_target_pairs={{0,1},{1,2},{2,3},{3,0},{4,5},{5,6},{6,7},{7,4},{8,9},{9,10},{10,1... | collective-permute-start | bytes 2752520 | tf_op jit(solution)/shard_map/ppermute | solution.py:276
  49.2 44.2 %collective-permute-start.5 = (bf16[2,896,256]{1,2,0:T(8,128)(2,1)}, bf16[2,896,256]{1,2,0:T(8,128)(2,1)S(1)}, u32[]{:S(2)}, u32[]{:S(2)}) collective-permute-start(bf16[2,896,256]{1,2,0:T(8,128)(2,1)} %get-tuple-element.93), channel_id=1, source_target_pairs={{0,3},{1,0},{2,1},{3,2},{4,7},{5,4},{6,5},{7,6},{8,11},{9,8},{10,9... | collective-permute-start | bytes 2752520 | tf_op jit(solution)/shard_map/ppermute | solution.py:276
  93.4 23.2 %copy-start.6 = (bf16[2,896,256]{1,2,0:T(8,128)(2,1)}, bf16[2,896,256]{1,2,0:T(8,128)(2,1)S(1)}, u32[]{:S(2)}) copy-start(bf16[2,896,256]{1,2,0:T(8,128)(2,1)S(1)} %collective-permute-done.4) | copy-start | bytes 2752516
  93.4 23.2 %copy-start.8 = (bf16[2,896,256]{1,2,0:T(8,128)(2,1)}, bf16[2,896,256]{1,2,0:T(8,128)(2,1)S(1)}, u32[]{:S(2)}) copy-start(bf16[2,896,256]{1,2,0:T(8,128)(2,1)S(1)} %collective-permute-done.5) | copy-start | bytes 2752516
  96.4 41.3 %collective-permute-start.6 = (bf16[896,1024]{1,0:T(8,128)(2,1)S(1)}, bf16[896,1024]{1,0:T(8,128)(2,1)S(1)}, u32[]{:S(2)}, u32[]{:S(2)}) collective-permute-start(bf16[896,1024]{1,0:T(8,128)(2,1)S(1)} %convert_bitcast_fusion), channel_id=1, source_target_pairs={{0,1},{3,2},{4,5},{7,6},{8,9},{11,10},{12,13},{15,14},{16,17},{19,... | collective-permute-start | bytes 5505032 | tf_op jit(solution)/shard_map/ppermute | solution.py:322
  98.7 58.8 %collective-permute-start.7 = (bf16[2,896,256]{1,2,0:T(8,128)(2,1)}, bf16[2,896,256]{1,2,0:T(8,128)(2,1)S(1)}, u32[]{:S(2)}, u32[]{:S(2)}) collective-permute-start(bf16[2,896,256]{1,2,0:T(8,128)(2,1)} %get-tuple-element.91), channel_id=1, source_target_pairs={{0,2},{1,3},{2,0},{3,1},{4,6},{5,7},{6,4},{7,5},{8,10},{9,11},{10,... | collective-permute-start | bytes 2752520 | tf_op jit(solution)/shard_map/ppermute | solution.py:276
  161.9 6.7 %collective-permute-start.8 = (bf16[896,1024]{1,0:T(8,128)(2,1)}, bf16[896,1024]{1,0:T(8,128)(2,1)}, u32[]{:S(2)}, u32[]{:S(2)}) collective-permute-start(bf16[896,1024]{1,0:T(8,128)(2,1)} %get-tuple-element.78), channel_id=1, source_target_pairs={{0,1},{1,2},{4,5},{5,6},{8,9},{9,10},{12,13},{13,14},{16,17},{17,1... | collective-permute-start | bytes 5505032 | tf_op jit(solution)/shard_map/ppermute | solution.py:329
  163.8 41.6 %collective-permute-start.9 = (bf16[896,1024]{1,0:T(8,128)(2,1)S(1)}, bf16[896,1024]{1,0:T(8,128)(2,1)}, u32[]{:S(2)}, u32[]{:S(2)}) collective-permute-start(bf16[896,1024]{1,0:T(8,128)(2,1)S(1)} %get-tuple-element.77), channel_id=1, source_target_pairs={{2,1},{3,2},{6,5},{7,6},{10,9},{11,10},{14,13},{15,14},{18,17},{19... | collective-permute-start | bytes 5505032 | tf_op jit(solution)/shard_map/ppermute | solution.py:330
  205.4 14.9 %copy-start.7 = (bf16[2,896,256]{1,2,0:T(8,128)(2,1)S(1)}, bf16[2,896,256]{1,2,0:T(8,128)(2,1)}, u32[]{:S(2)}) copy-start(bf16[2,896,256]{1,2,0:T(8,128)(2,1)} %copy-done.6) | copy-start | bytes 2752516
  205.4 14.9 %copy-start.9 = (bf16[2,896,256]{1,2,0:T(8,128)(2,1)S(1)}, bf16[2,896,256]{1,2,0:T(8,128)(2,1)}, u32[]{:S(2)}) copy-start(bf16[2,896,256]{1,2,0:T(8,128)(2,1)} %copy-done.8) | copy-start | bytes 2752516
  212.9 42.8 %collective-permute-start.10 = (bf16[896,1024]{1,0:T(8,128)(2,1)}, bf16[896,1024]{1,0:T(8,128)(2,1)}, u32[]{:S(2)}, u32[]{:S(2)}) collective-permute-start(bf16[896,1024]{1,0:T(8,128)(2,1)} %get-tuple-element.76), channel_id=1, source_target_pairs={{0,1},{1,2},{2,3},{4,5},{5,6},{6,7},{8,9},{9,10},{10,11},{12,13},{... | collective-permute-start | bytes 5505032 | tf_op jit(solution)/shard_map/ppermute | solution.py:329
  214.2 42.4 %collective-permute-start.11 = (bf16[896,1024]{1,0:T(8,128)(2,1)}, bf16[896,1024]{1,0:T(8,128)(2,1)}, u32[]{:S(2)}, u32[]{:S(2)}) collective-permute-start(bf16[896,1024]{1,0:T(8,128)(2,1)} %get-tuple-element.75), channel_id=1, source_target_pairs={{1,0},{2,1},{3,2},{5,4},{6,5},{7,6},{9,8},{10,9},{11,10},{13,12},{... | collective-permute-start | bytes 5505032 | tf_op jit(solution)/shard_map/ppermute | solution.py:330
  263.1 81.1 %collective-permute-start.12 = (bf16[2,896,1024]{2,1,0:T(8,128)(2,1)}, bf16[2,896,1024]{2,1,0:T(8,128)(2,1)}, u32[]{:S(2)}, u32[]{:S(2)}) collective-permute-start(bf16[2,896,1024]{2,1,0:T(8,128)(2,1)} %pad_maximum_fusion.2.refs_0_.refs_1_.refs_3_.refs_6_.refs_4_), channel_id=1, source_target_pairs={{0,1},{1,2},{2,3},{4,5},{5,6},{6,7},{8,9},{9,10},{10,11},{12,13},{... | collective-permute-start | bytes 11010056 | tf_op jit(solution)/shard_map/ppermute | solution.py:348
  264.4 80.7 %collective-permute-start.13 = (bf16[2,896,1024]{2,1,0:T(8,128)(2,1)}, bf16[2,896,1024]{2,1,0:T(8,128)(2,1)}, u32[]{:S(2)}, u32[]{:S(2)}) collective-permute-start(bf16[2,896,1024]{2,1,0:T(8,128)(2,1)} %pad_maximum_fusion.2.refs_0_.refs_1_.refs_3_.refs_6_.refs_4_), channel_id=1, source_target_pairs={{1,0},{2,1},{3,2},{5,4},{6,5},{7,6},{9,8},{10,9},{11,10},{13,12},{... | collective-permute-start | bytes 11010056 | tf_op jit(solution)/shard_map/ppermute | solution.py:349
  271.0 84.9 %collective-permute-start.14 = (bf16[2,896,1024]{2,1,0:T(8,128)(2,1)}, bf16[2,896,1024]{2,1,0:T(8,128)(2,1)}, u32[]{:S(2)}, u32[]{:S(2)}) collective-permute-start(bf16[2,896,1024]{2,1,0:T(8,128)(2,1)} %pad_maximum_fusion.2.refs_0_.refs_1_.refs_3_.refs_6_.refs_4_), channel_id=1, source_target_pairs={{0,8},{4,12},{8,16},{12,20},{16,24},{20,28},{24,0},{28,4},{1,9},{5... | collective-permute-start | bytes 11010056 | tf_op jit(solution)/shard_map/ppermute | solution.py:367
  360.2 26.4 %collective-permute-start.17 = (bf16[2,896,1024]{2,1,0:T(8,128)(2,1)}, bf16[2,896,1024]{2,1,0:T(8,128)(2,1)}, u32[]{:S(2)}, u32[]{:S(2)}) collective-permute-start(bf16[2,896,1024]{2,1,0:T(8,128)(2,1)} %broadcast_select_fusion.1), channel_id=1, source_target_pairs={{0,4},{4,0},{8,12},{12,8},{16,20},{20,16},{24,28},{28,24},{1,5},{5... | collective-permute-start | bytes 11010056 | tf_op jit(solution)/shard_map/ppermute | solution.py:363
  364.4 22.1 %collective-permute-start.15 = (bf16[2,896,1024]{2,1,0:T(8,128)(2,1)}, bf16[2,896,1024]{2,1,0:T(8,128)(2,1)S(1)}, u32[]{:S(2)}, u32[]{:S(2)}) collective-permute-start(bf16[2,896,1024]{2,1,0:T(8,128)(2,1)} %collective-permute-done.13.refs_1_), channel_id=1, source_target_pairs={{1,0},{2,1},{5,4},{6,5},{9,8},{10,9},{13,12},{14,13},{17,16},{18,1... | collective-permute-start | bytes 11010056 | tf_op jit(solution)/shard_map/ppermute | solution.py:349
  365.3 86.2 %collective-permute-start.16 = (bf16[2,896,1024]{2,1,0:T(8,128)(2,1)}, bf16[2,896,1024]{2,1,0:T(8,128)(2,1)S(1)}, u32[]{:S(2)}, u32[]{:S(2)}) collective-permute-start(bf16[2,896,1024]{2,1,0:T(8,128)(2,1)} %collective-permute-done.12.refs_2_.refs_3_), channel_id=1, source_target_pairs={{1,2},{2,3},{5,6},{6,7},{9,10},{10,11},{13,14},{14,15},{17,18},{18... | collective-permute-start | bytes 11010056 | tf_op jit(solution)/shard_map/ppermute | solution.py:348
  366.8 84.7 %collective-permute-start.18 = (bf16[2,896,1024]{2,1,0:T(8,128)(2,1)}, bf16[2,896,1024]{2,1,0:T(8,128)(2,1)}, u32[]{:S(2)}, u32[]{:S(2)}) collective-permute-start(bf16[2,896,1024]{2,1,0:T(8,128)(2,1)} %pad_maximum_fusion.2.refs_0_.refs_1_.refs_3_.refs_6_.refs_4_), channel_id=1, source_target_pairs={{0,16},{4,20},{8,24},{12,28},{16,0},{20,4},{24,8},{28,12},{1,17},{... | collective-permute-start | bytes 11010056 | tf_op jit(solution)/shard_map/ppermute | solution.py:367
  386.6 74.8 %copy-start = (bf16[2,896,1024]{2,1,0:T(8,128)(2,1)}, bf16[2,896,1024]{2,1,0:T(8,128)(2,1)S(1)}, u32[]{:S(2)}) copy-start(bf16[2,896,1024]{2,1,0:T(8,128)(2,1)S(1)} %collective-permute-done.15.refs_4_) | copy-start | bytes 11010052
  451.5 13.2 %copy-start.2 = (bf16[2,896,1024]{2,1,0:T(8,128)(2,1)}, bf16[2,896,1024]{2,1,0:T(8,128)(2,1)S(1)}, u32[]{:S(2)}) copy-start(bf16[2,896,1024]{2,1,0:T(8,128)(2,1)S(1)} %collective-permute-done.16.refs_5_) | copy-start | bytes 11010052
  457.1 58.5 %collective-permute-start.23 = (bf16[2,896,1024]{2,1,0:T(8,128)(2,1)}, bf16[2,896,1024]{2,1,0:T(8,128)(2,1)}, u32[]{:S(2)}, u32[]{:S(2)}) collective-permute-start(bf16[2,896,1024]{2,1,0:T(8,128)(2,1)} %broadcast_select_fusion), channel_id=1, source_target_pairs={{0,4},{4,0},{8,12},{12,8},{16,20},{20,16},{24,28},{28,24},{1,5},{5... | collective-permute-start | bytes 11010056 | tf_op jit(solution)/shard_map/ppermute | solution.py:363
  460.1 51.1 %collective-permute-start.19 = (bf16[2,448,1024]{2,1,0:T(8,128)(2,1)}, bf16[2,448,1024]{2,1,0:T(8,128)(2,1)}, u32[]{:S(2)}, u32[]{:S(2)}) collective-permute-start(bf16[2,448,1024]{2,1,0:T(8,128)(2,1)} %get-tuple-element.85), channel_id=1, source_target_pairs={{2,3},{6,7},{10,11},{14,15},{18,19},{22,23},{26,27},{30,31}} | collective-permute-start | bytes 5505032 | tf_op jit(solution)/shard_map/ppermute | solution.py:348
  463.5 47.6 %collective-permute-start.20 = (bf16[2,448,1024]{2,1,0:T(8,128)(2,1)}, bf16[2,448,1024]{2,1,0:T(8,128)(2,1)S(1)}, u32[]{:S(2)}, u32[]{:S(2)}) collective-permute-start(bf16[2,448,1024]{2,1,0:T(8,128)(2,1)} %get-tuple-element.83), channel_id=1, source_target_pairs={{1,0},{5,4},{9,8},{13,12},{17,16},{21,20},{25,24},{29,28}} | collective-permute-start | bytes 5505032 | tf_op jit(solution)/shard_map/ppermute | solution.py:349
  466.9 46.5 %copy-start.1 = (bf16[2,896,1024]{2,1,0:T(8,128)(2,1)S(1)}, bf16[2,896,1024]{2,1,0:T(8,128)(2,1)}, u32[]{:S(2)}) copy-start(bf16[2,896,1024]{2,1,0:T(8,128)(2,1)} %copy-done) | copy-start | bytes 11010052
  511.2 43.8 %collective-permute-start.21 = (bf16[2,448,1024]{2,1,0:T(8,128)(2,1)}, bf16[2,448,1024]{2,1,0:T(8,128)(2,1)S(1)}, u32[]{:S(2)}, u32[]{:S(2)}) collective-permute-start(bf16[2,448,1024]{2,1,0:T(8,128)(2,1)} %get-tuple-element.68), channel_id=1, source_target_pairs={{1,0},{5,4},{9,8},{13,12},{17,16},{21,20},{25,24},{29,28}} | collective-permute-start | bytes 5505032 | tf_op jit(solution)/shard_map/ppermute | solution.py:349
  512.0 44.1 %collective-permute-start.22 = (bf16[2,448,1024]{2,1,0:T(8,128)(2,1)}, bf16[2,448,1024]{2,1,0:T(8,128)(2,1)}, u32[]{:S(2)}, u32[]{:S(2)}) collective-permute-start(bf16[2,448,1024]{2,1,0:T(8,128)(2,1)} %get-tuple-element.69), channel_id=1, source_target_pairs={{2,3},{6,7},{10,11},{14,15},{18,19},{22,23},{26,27},{30,31}} | collective-permute-start | bytes 5505032 | tf_op jit(solution)/shard_map/ppermute | solution.py:348
  (5 other events, 12.8 us)
Sparse Core Ops, SparseCore 0:
  23.4 60.1 all-gather.1

commit v7 on v6

--- a/solution.py
+++ b/solution.py
@@ -423,14 +423,9 @@
             position = position * LAST_PARTS + part
         return position, choice
 
-    middle = (0, *range(2, groups - 1))
     first_offsets = tuple((groups - 1,) if d == 0 else (1,) for d in range(groups))
-    other_offsets = tuple(
-        (*middle, 1) if d == 0 else (*middle, groups - 1) for d in range(groups)
-    )
-    all_offsets = tuple(
-        (*first_offsets[d], *other_offsets[d]) for d in range(groups)
-    )
+    other_offsets = (tuple(range(groups)),) * groups
+    all_offsets = tuple((*first, *others) for first, others in zip(first_offsets, other_offsets))
     hidden_calls = [(0, first_offsets), (0, other_offsets)]
     hidden_calls += [(chunk, all_offsets) for chunk in range(1, CHUNKS)]
     bases, lines = {}, [[] for _ in range(groups)]
@@ -471,9 +466,7 @@
         def partial(offset):
             if offset == "first":
                 return first
-            if offset in middle:
-                return others[middle.index(offset)]
-            return jnp.where((own_group == 0) == (offset == 1), others[len(middle)], first)
+            return others[offset]
 
         return partial
 
@@ -512,14 +505,19 @@
         for step in range(1, groups):
             if later and step > 1:
                 received = reduce_step(partial, step - 1, received or None)
+            halved = use_kernels and not later and step == groups - 1
+            if halved:
+                keys = list(found)
+                moved = tie(piece_of(left, 0), piece_of(right, 0), *found.values())
+                first_ends, found = moved[:2], dict(zip(keys, moved[2:]))
             made = partner_step(step, found)
-            if step < groups - 1 or later or not use_kernels:
+            if not halved:
                 left, right = gather_step(step, left, right)
                 held[step] = (right, left)
             else:
                 lefts, rights, sent_on = [], [], ()
                 for part in range(LAST_PARTS):
-                    ends = (piece_of(left, part), piece_of(right, part))
+                    ends = first_ends if part == 0 else (piece_of(left, part), piece_of(right, part))
                     if sent_on:
                         ends = tie(*ends, *sent_on)[:2]
                     sent_on = gather_step(step, *ends)

time: 593 us -> 587 us (0.990)
  other arithmetic: 39.3 us -> 32.9 us
  transfers between devices with their start and end apart: 25 -> 25, of which waited for: 13 -> 13; matrix products, arithmetic and copies ran while one was open for 6% -> 5% of each run, Pallas kernels for 24% -> 25%
where the time goes in v7:
time: 587 us; the launch traced here: 578 us
  waiting for transfers between devices  282 us (48%)
  Pallas kernels  165 us (28%)
  starting transfers between devices  56.8 us (10%)
  other arithmetic  32.9 us (6%)
  local copies, waits for them, and re-layouts  25.5 us (4%)
  between operations  16.1 us (3%)
    pallas_call x6, Pallas kernels, factor_rows(): pl.pallas_call(functools.partial(factor_kernel, (len(keys), chunk_total,...  133 us
    ppermute x4, waiting for transfers between devices, gather_step(): lax.ppermute(left, 'dp', [(d, d + 1) for d in range(step - 1, groups - 1)])  128 us
    ppermute x2, waiting for transfers between devices, reduce_step(): lax.ppermute(left.astype(jnp.bfloat16), 'dp', [(d, d - 1) for d in range(...  38.8 us
    all_gather x1, waiting for transfers between devices, per_device(): features = lax.all_gather(sent, 'tensor', axis=0, tiled=True)  32.4 us
    pallas_call x2, Pallas kernels, hidden_parts(): pl.pallas_call(functools.partial(hidden_kernel, base + count), grid_spec=...  31.6 us
    ppermute x2, waiting for transfers between devices, reduce_step(): lax.ppermute(right.astype(jnp.bfloat16), 'dp', [(d, d + 1) for d in range...  24.9 us
    ppermute x3, waiting for transfers between devices, saved_pieces(): pieces.append(lax.ppermute(part(own_group + shift), 'dp', ring))  19.8 us
    ppermute x1, waiting for transfers between devices, reduce_step(): moved = lax.ppermute(partial('first').astype(jnp.bfloat16), 'dp', ends)  17.1 us
  transfers between devices with their start and end apart: 25, of which 13 were waited for; matrix products, arithmetic and copies ran while one was open for 5% of the time, Pallas kernels for 25%

profile of v7, /device:TPU:29, one launch (start us, length us, event | category | flops | bytes accessed | tf_op | source)
XLA Modules:
  0.0 577.7 jit_solution(13475024281072191125)
XLA Ops:
  6.5 2.9 collective-permute-start
  9.5 4.2 pad_maximum_fusion
  13.7 8.8 %collective-permute-done = bf16[256,1024]{1,0:T(8,128)(2,1)S(1)} collective-permute-done((bf16[256,1024]{1,0:T(8,128)(2,1)}, bf16[256,1024]{1,0:T(8,128)(2,1)S(1)}, u32[]{:S(2)}, u32[]{:S(2)}) %collective-permute-start) | collective-permute-done | bytes 524320 | tf_op jit(solution)/shard_map/ppermute | solution.py:263
  24.0 12.0 %collective-permute-start.1 = (bf16[16,128]{1,0:T(8,128)(2,1)S(1)}, bf16[16,128]{1,0:T(8,128)(2,1)S(1)}, u32[]{:S(2)}, u32[]{:S(2)}) collective-permute-start(bf16[16,128]{1,0:T(8,128)(2,1)S(1)} %slice.58), channel_id=1, source_target_pairs={{0,1},{1,2},{2,3},{3,0},{4,5},{5,6},{6,7},{7,4},{8,9},{9,10},{10,1... | collective-permute-start | bytes 12296 | tf_op jit(solution)/shard_map/ppermute | solution.py:291
  42.0 5.8 constant_dynamic-slice_fusion.4
  51.2 32.4 %all-gather.2.cloned.1.call-done = bf16[2048,1024]{1,0:T(8,128)(2,1)} async-done(((bf16[256,1024]{1,0:T(8,128)(2,1)}), bf16[2048,1024]{1,0:T(8,128)(2,1)}) %all-gather.2.cloned.1.call-update) | async-done | bytes 4194320 | tf_op jit(solution)/shard_map/all_gather | solution.py:266
  83.6 9.8 %shard_map.56 = f32[1,896,1024]{2,1,0:T(8,128)} custom-call(s32[124]{0:T(128)} %fusion.12.table_ref, bf16[3584,2048]{1,0:T(8,128)(2,1)} %weight_ref.3, bf16[4,2,256,1024]{3,2,1,0:T(8,128)(2,1)} %bitcast.79), custom_call_target="tpu_custom_call" | custom-call | flops 3758096384 | bytes 11534336 | tf_op jit(solution)/shard_map/pallas_call | solution.py:36
  93.4 2.3 convert_bitcast_fusion
  98.1 21.8 %shard_map.55 = f32[4,896,1024]{2,1,0:T(8,128)} custom-call(s32[124]{0:T(128)} %fusion.12.table_ref, bf16[3584,2048]{1,0:T(8,128)(2,1)} %weight_ref.3, bf16[4,2,256,1024]{3,2,1,0:T(8,128)(2,1)} %bitcast.80), custom_call_target="tpu_custom_call" | custom-call | flops 15032385536 | bytes 33554432 | tf_op jit(solution)/shard_map/pallas_call | solution.py:36
  119.9 17.1 %collective-permute-done.6 = bf16[896,1024]{1,0:T(8,128)(2,1)S(1)} collective-permute-done((bf16[896,1024]{1,0:T(8,128)(2,1)S(1)}, bf16[896,1024]{1,0:T(8,128)(2,1)S(1)}, u32[]{:S(2)}, u32[]{:S(2)}) %collective-permute-start.6) | collective-permute-done | bytes 1835040 | tf_op jit(solution)/shard_map/ppermute | solution.py:322
  137.0 19.8 %collective-permute-done.7 = bf16[2,896,256]{1,2,0:T(8,128)(2,1)S(1)} collective-permute-done((bf16[2,896,256]{1,2,0:T(8,128)(2,1)}, bf16[2,896,256]{1,2,0:T(8,128)(2,1)S(1)}, u32[]{:S(2)}, u32[]{:S(2)}) %collective-permute-start.7) | collective-permute-done | bytes 917536 | tf_op jit(solution)/shard_map/ppermute | solution.py:276
  156.8 3.0 add_convert_fusion
  160.6 4.8 collective-permute-start.9
  165.4 37.9 %collective-permute-done.9 = bf16[896,1024]{1,0:T(8,128)(2,1)S(1)} collective-permute-done((bf16[896,1024]{1,0:T(8,128)(2,1)S(1)}, bf16[896,1024]{1,0:T(8,128)(2,1)S(1)}, u32[]{:S(2)}, u32[]{:S(2)}) %collective-permute-start.9) | collective-permute-done | bytes 1835040 | tf_op jit(solution)/shard_map/ppermute | solution.py:330
  203.3 6.5 %fusion.5 = (bf16[896,1024]{1,0:T(8,128)(2,1)}, bf16[896,1024]{1,0:T(8,128)(2,1)}) fusion(f32[4,896,1024]{2,1,0:T(8,128)} %shard_map.55, bf16[896,1024]{1,0:T(8,128)(2,1)S(1)} %collective-permute-done.9, bf16[896,1024]{1,0:T(8,128)(2,1)S(1)} %collective-permute-done.8), kind=kLoop, calls=%fused_computation.8 | loop fusion | flops 5505024 | bytes 14680064 | tf_op jit(solution)/shard_map/convert_element_type | solution.py:331
  211.1 6.0 %collective-permute-start.11 = (bf16[896,1024]{1,0:T(8,128)(2,1)}, bf16[896,1024]{1,0:T(8,128)(2,1)}, u32[]{:S(2)}, u32[]{:S(2)}) collective-permute-start(bf16[896,1024]{1,0:T(8,128)(2,1)} %get-tuple-element.83), channel_id=1, source_target_pairs={{1,0},{2,1},{3,2},{5,4},{6,5},{7,6},{9,8},{10,9},{11,10},{13,12},{... | collective-permute-start | bytes 5505032 | tf_op jit(solution)/shard_map/ppermute | solution.py:330
  227.6 24.9 %collective-permute-done.10 = bf16[896,1024]{1,0:T(8,128)(2,1)} collective-permute-done((bf16[896,1024]{1,0:T(8,128)(2,1)}, bf16[896,1024]{1,0:T(8,128)(2,1)}, u32[]{:S(2)}, u32[]{:S(2)}) %collective-permute-start.10) | collective-permute-done | bytes 1835040 | tf_op jit(solution)/shard_map/ppermute | solution.py:329
  253.4 4.3 fusion.11
  261.1 6.6 %collective-permute-start.13 = (bf16[2,896,1024]{2,1,0:T(8,128)(2,1)}, bf16[2,896,1024]{2,1,0:T(8,128)(2,1)}, u32[]{:S(2)}, u32[]{:S(2)}) collective-permute-start(bf16[2,896,1024]{2,1,0:T(8,128)(2,1)} %pad_maximum_fusion.2.refs_0_.refs_1_.refs_3_.refs_6_.refs_4_), channel_id=1, source_target_pairs={{1,0},{2,1},{3,2},{5,4},{6,5},{7,6},{9,8},{10,9},{11,10},{13,12},{... | collective-permute-start | bytes 11010056 | tf_op jit(solution)/shard_map/ppermute | solution.py:349
  268.5 10.2 %shard_map.57.refs_5_ = bf16[5,50176,128]{2,1,0:T(8,128)(2,1)} custom-call(s32[124]{0:T(128)} %fusion.12.table_ref, bf16[2,896,1024]{2,1,0:T(8,128)(2,1)} %pad_maximum_fusion.2.refs_0_.refs_1_.refs_3_.refs_6_.refs_4_, bf16[2,896,1024]{2,1,0:T(8,128)(2,1)} %pad_maximum_fusion.2.refs_0_.refs_1_.refs_3_.refs_6_.refs_4_), custom_call_target="tpu_custom_call" | custom-call | flops 3288334336 | bytes 10551296 | tf_op jit(solution)/shard_map/pallas_call | solution.py:185
  278.7 62.2 %collective-permute-done.12.refs_2_.refs_3_ = bf16[2,896,1024]{2,1,0:T(8,128)(2,1)} collective-permute-done((bf16[2,896,1024]{2,1,0:T(8,128)(2,1)}, bf16[2,896,1024]{2,1,0:T(8,128)(2,1)}, u32[]{:S(2)}, u32[]{:S(2)}) %collective-permute-start.12) | collective-permute-done | bytes 3670048 | tf_op jit(solution)/shard_map/ppermute | solution.py:348
  341.9 9.6 %collective-permute-done.14.refs_4_.refs_8_.refs_6_ = bf16[2,896,1024]{2,1,0:T(8,128)(2,1)} collective-permute-done((bf16[2,896,1024]{2,1,0:T(8,128)(2,1)}, bf16[2,896,1024]{2,1,0:T(8,128)(2,1)}, u32[]{:S(2)}, u32[]{:S(2)}) %collective-permute-start.14) | collective-permute-done | bytes 3670048 | tf_op jit(solution)/shard_map/ppermute | solution.py:367
  351.4 4.2 broadcast_select_fusion.1
  355.7 4.7 collective-permute-start.17
  362.8 19.6 %shard_map.58.refs_10_ = bf16[5,50176,128]{2,1,0:T(8,128)(2,1)} custom-call(s32[124]{0:T(128)} %fusion.12.table_ref, bf16[2,896,1024]{2,1,0:T(8,128)(2,1)} %pad_maximum_fusion.2.refs_0_.refs_1_.refs_3_.refs_6_.refs_4_, bf16[2,896,1024]{2,1,0:T(8,128)(2,1)} %collective-permute-done.13.refs_1_, ...), custom_call_target="tpu_custom_call", output_to_operand_aliasing={{}: (6, {})} | custom-call | flops 9865003008 | bytes 27983872 | tf_op jit(solution)/shard_map/pallas_call | solution.py:185
  382.5 64.9 %collective-permute-done.16.refs_5_ = bf16[2,896,1024]{2,1,0:T(8,128)(2,1)S(1)} collective-permute-done((bf16[2,896,1024]{2,1,0:T(8,128)(2,1)}, bf16[2,896,1024]{2,1,0:T(8,128)(2,1)S(1)}, u32[]{:S(2)}, u32[]{:S(2)}) %collective-permute-start.16) | collective-permute-done | bytes 3670048 | tf_op jit(solution)/shard_map/ppermute | solution.py:348
  447.5 4.0 fusion.15
  451.5 2.4 broadcast_select_fusion
  460.6 44.2 %shard_map.59.refs_7_ = bf16[5,50176,128]{2,1,0:T(8,128)(2,1)} custom-call(s32[124]{0:T(128)} %fusion.12.table_ref, bf16[2,896,1024]{2,1,0:T(8,128)(2,1)} %pad_maximum_fusion.2.refs_0_.refs_1_.refs_3_.refs_6_.refs_4_, bf16[2,896,1024]{2,1,0:T(8,128)(2,1)} %collective-permute-done.13.refs_1_, ...), custom_call_target="tpu_custom_call", output_to_operand_aliasing={{}: (11, {})} | custom-call | flops 26306674688 | bytes 69730304 | tf_op jit(solution)/shard_map/pallas_call | solution.py:185
  510.4 19.6 %shard_map.60.refs_9_ = bf16[5,50176,128]{2,1,0:T(8,128)(2,1)} custom-call(s32[124]{0:T(128)} %fusion.12.table_ref, bf16[2,896,1024]{2,1,0:T(8,128)(2,1)} %pad_maximum_fusion.2.refs_0_.refs_1_.refs_3_.refs_6_.refs_4_, bf16[2,896,1024]{2,1,0:T(8,128)(2,1)} %collective-permute-done.13.refs_1_, ...), custom_call_target="tpu_custom_call", output_to_operand_aliasing={{}: (8, {})} | custom-call | flops 9865003008 | bytes 24313856 | tf_op jit(solution)/shard_map/pallas_call | solution.py:185
  530.1 19.7 %shard_map.61.refs_9_ = bf16[5,50176,128]{2,1,0:T(8,128)(2,1)} custom-call(s32[124]{0:T(128)} %fusion.12.table_ref, bf16[2,448,1024]{2,1,0:T(8,128)(2,1)} %get-tuple-element.89.refs_0_, bf16[2,448,1024]{2,1,0:T(8,128)(2,1)} %get-tuple-element.87.refs_1_, bf16[2,448,1024]{2,1,0:T(8,128)(2,1)} %collective-permute-done.20.refs_2_, ...), custom_call_target="tpu_custom_call", output_to_operand_aliasing={{}: (10, {})} | custom-call | flops 8220835840 | bytes 35553280 | tf_op jit(solution)/shard_map/pallas_call | solution.py:185
  550.8 19.9 %shard_map.62 = bf16[5,50176,128]{2,1,0:T(8,128)(2,1)} custom-call(s32[124]{0:T(128)} %fusion.12.table_ref, bf16[2,448,1024]{2,1,0:T(8,128)(2,1)} %get-tuple-element.90.refs_0_, bf16[2,448,1024]{2,1,0:T(8,128)(2,1)} %get-tuple-element.88.refs_1_, bf16[2,448,1024]{2,1,0:T(8,128)(2,1)} %collective-permute-done.21.refs_2_, ...), custom_call_target="tpu_custom_call", output_to_operand_aliasing={{}: (10, {})} | custom-call | flops 8220835840 | bytes 35553280 | tf_op jit(solution)/shard_map/pallas_call | solution.py:185
  (63 shorter events, 45.5 us)
Async XLA Ops:
  6.5 77.1 %all-gather.2.cloned.1.call-start = ((), (), s32[]{:S(2)}) async-start(), calls=%async_computation | async-start | bytes 4718592 | tf_op jit(solution)/shard_map/all_gather | solution.py:266
  6.5 15.9 %collective-permute-start = (bf16[256,1024]{1,0:T(8,128)(2,1)}, bf16[256,1024]{1,0:T(8,128)(2,1)S(1)}, u32[]{:S(2)}, u32[]{:S(2)}) collective-permute-start(bf16[256,1024]{1,0:T(8,128)(2,1)} %param.5), channel_id=1, source_target_pairs={{0,0},{1,8},{2,16},{3,24},{4,4},{5,12},{6,20},{7,28},{8,9},{9,17},... | collective-permute-start | bytes 1572872 | tf_op jit(solution)/shard_map/ppermute | solution.py:263
  22.5 0.8 copy-start.5
  24.0 12.8 %collective-permute-start.1 = (bf16[16,128]{1,0:T(8,128)(2,1)S(1)}, bf16[16,128]{1,0:T(8,128)(2,1)S(1)}, u32[]{:S(2)}, u32[]{:S(2)}) collective-permute-start(bf16[16,128]{1,0:T(8,128)(2,1)S(1)} %slice.58), channel_id=1, source_target_pairs={{0,1},{1,2},{2,3},{3,0},{4,5},{5,6},{6,7},{7,4},{8,9},{9,10},{10,1... | collective-permute-start | bytes 12296 | tf_op jit(solution)/shard_map/ppermute | solution.py:291
  36.0 3.4 collective-permute-start.2
  36.0 4.7 collective-permute-start.3
  47.8 45.6 %collective-permute-start.4 = (bf16[2,896,256]{1,2,0:T(8,128)(2,1)}, bf16[2,896,256]{1,2,0:T(8,128)(2,1)S(1)}, u32[]{:S(2)}, u32[]{:S(2)}) collective-permute-start(bf16[2,896,256]{1,2,0:T(8,128)(2,1)} %get-tuple-element.102), channel_id=1, source_target_pairs={{0,1},{1,2},{2,3},{3,0},{4,5},{5,6},{6,7},{7,4},{8,9},{9,10},{10,1... | collective-permute-start | bytes 2752520 | tf_op jit(solution)/shard_map/ppermute | solution.py:276
  49.9 43.4 %collective-permute-start.5 = (bf16[2,896,256]{1,2,0:T(8,128)(2,1)}, bf16[2,896,256]{1,2,0:T(8,128)(2,1)S(1)}, u32[]{:S(2)}, u32[]{:S(2)}) collective-permute-start(bf16[2,896,256]{1,2,0:T(8,128)(2,1)} %get-tuple-element.101), channel_id=1, source_target_pairs={{0,3},{1,0},{2,1},{3,2},{4,7},{5,4},{6,5},{7,6},{8,11},{9,8},{10,9... | collective-permute-start | bytes 2752520 | tf_op jit(solution)/shard_map/ppermute | solution.py:276
  95.7 41.3 %collective-permute-start.6 = (bf16[896,1024]{1,0:T(8,128)(2,1)S(1)}, bf16[896,1024]{1,0:T(8,128)(2,1)S(1)}, u32[]{:S(2)}, u32[]{:S(2)}) collective-permute-start(bf16[896,1024]{1,0:T(8,128)(2,1)S(1)} %convert_bitcast_fusion), channel_id=1, source_target_pairs={{0,1},{3,2},{4,5},{7,6},{8,9},{11,10},{12,13},{15,14},{16,17},{19,... | collective-permute-start | bytes 5505032 | tf_op jit(solution)/shard_map/ppermute | solution.py:322
  98.0 58.8 %collective-permute-start.7 = (bf16[2,896,256]{1,2,0:T(8,128)(2,1)}, bf16[2,896,256]{1,2,0:T(8,128)(2,1)S(1)}, u32[]{:S(2)}, u32[]{:S(2)}) collective-permute-start(bf16[2,896,256]{1,2,0:T(8,128)(2,1)} %get-tuple-element.99), channel_id=1, source_target_pairs={{0,2},{1,3},{2,0},{3,1},{4,6},{5,7},{6,4},{7,5},{8,10},{9,11},{10,... | collective-permute-start | bytes 2752520 | tf_op jit(solution)/shard_map/ppermute | solution.py:276
  156.8 3.1 copy-start.4
  159.8 5.6 collective-permute-start.8
  160.6 42.7 %collective-permute-start.9 = (bf16[896,1024]{1,0:T(8,128)(2,1)S(1)}, bf16[896,1024]{1,0:T(8,128)(2,1)S(1)}, u32[]{:S(2)}, u32[]{:S(2)}) collective-permute-start(bf16[896,1024]{1,0:T(8,128)(2,1)S(1)} %get-tuple-element.85), channel_id=1, source_target_pairs={{2,1},{3,2},{6,5},{7,6},{10,9},{11,10},{14,13},{15,14},{18,17},{19... | collective-permute-start | bytes 5505032 | tf_op jit(solution)/shard_map/ppermute | solution.py:330
  209.8 42.7 %collective-permute-start.10 = (bf16[896,1024]{1,0:T(8,128)(2,1)}, bf16[896,1024]{1,0:T(8,128)(2,1)}, u32[]{:S(2)}, u32[]{:S(2)}) collective-permute-start(bf16[896,1024]{1,0:T(8,128)(2,1)} %get-tuple-element.84), channel_id=1, source_target_pairs={{0,1},{1,2},{2,3},{4,5},{5,6},{6,7},{8,9},{9,10},{10,11},{12,13},{... | collective-permute-start | bytes 5505032 | tf_op jit(solution)/shard_map/ppermute | solution.py:329
  211.1 42.3 %collective-permute-start.11 = (bf16[896,1024]{1,0:T(8,128)(2,1)}, bf16[896,1024]{1,0:T(8,128)(2,1)}, u32[]{:S(2)}, u32[]{:S(2)}) collective-permute-start(bf16[896,1024]{1,0:T(8,128)(2,1)} %get-tuple-element.83), channel_id=1, source_target_pairs={{1,0},{2,1},{3,2},{5,4},{6,5},{7,6},{9,8},{10,9},{11,10},{13,12},{... | collective-permute-start | bytes 5505032 | tf_op jit(solution)/shard_map/ppermute | solution.py:330
  223.6 1.8 copy-start.3
  259.9 81.1 %collective-permute-start.12 = (bf16[2,896,1024]{2,1,0:T(8,128)(2,1)}, bf16[2,896,1024]{2,1,0:T(8,128)(2,1)}, u32[]{:S(2)}, u32[]{:S(2)}) collective-permute-start(bf16[2,896,1024]{2,1,0:T(8,128)(2,1)} %pad_maximum_fusion.2.refs_0_.refs_1_.refs_3_.refs_6_.refs_4_), channel_id=1, source_target_pairs={{0,1},{1,2},{2,3},{4,5},{5,6},{6,7},{8,9},{9,10},{10,11},{12,13},{... | collective-permute-start | bytes 11010056 | tf_op jit(solution)/shard_map/ppermute | solution.py:348
  261.1 80.7 %collective-permute-start.13 = (bf16[2,896,1024]{2,1,0:T(8,128)(2,1)}, bf16[2,896,1024]{2,1,0:T(8,128)(2,1)}, u32[]{:S(2)}, u32[]{:S(2)}) collective-permute-start(bf16[2,896,1024]{2,1,0:T(8,128)(2,1)} %pad_maximum_fusion.2.refs_0_.refs_1_.refs_3_.refs_6_.refs_4_), channel_id=1, source_target_pairs={{1,0},{2,1},{3,2},{5,4},{6,5},{7,6},{9,8},{10,9},{11,10},{13,12},{... | collective-permute-start | bytes 11010056 | tf_op jit(solution)/shard_map/ppermute | solution.py:349
  267.7 83.7 %collective-permute-start.14 = (bf16[2,896,1024]{2,1,0:T(8,128)(2,1)}, bf16[2,896,1024]{2,1,0:T(8,128)(2,1)}, u32[]{:S(2)}, u32[]{:S(2)}) collective-permute-start(bf16[2,896,1024]{2,1,0:T(8,128)(2,1)} %pad_maximum_fusion.2.refs_0_.refs_1_.refs_3_.refs_6_.refs_4_), channel_id=1, source_target_pairs={{0,8},{4,12},{8,16},{12,20},{16,24},{20,28},{24,0},{28,4},{1,9},{5... | collective-permute-start | bytes 11010056 | tf_op jit(solution)/shard_map/ppermute | solution.py:367
  355.7 26.8 %collective-permute-start.17 = (bf16[2,896,1024]{2,1,0:T(8,128)(2,1)}, bf16[2,896,1024]{2,1,0:T(8,128)(2,1)}, u32[]{:S(2)}, u32[]{:S(2)}) collective-permute-start(bf16[2,896,1024]{2,1,0:T(8,128)(2,1)} %broadcast_select_fusion.1), channel_id=1, source_target_pairs={{0,4},{4,0},{8,12},{12,8},{16,20},{20,16},{24,28},{28,24},{1,5},{5... | collective-permute-start | bytes 11010056 | tf_op jit(solution)/shard_map/ppermute | solution.py:363
  360.4 22.1 %collective-permute-start.15 = (bf16[2,896,1024]{2,1,0:T(8,128)(2,1)}, bf16[2,896,1024]{2,1,0:T(8,128)(2,1)S(1)}, u32[]{:S(2)}, u32[]{:S(2)}) collective-permute-start(bf16[2,896,1024]{2,1,0:T(8,128)(2,1)} %collective-permute-done.13.refs_1_), channel_id=1, source_target_pairs={{1,0},{2,1},{5,4},{6,5},{9,8},{10,9},{13,12},{14,13},{17,16},{18,1... | collective-permute-start | bytes 11010056 | tf_op jit(solution)/shard_map/ppermute | solution.py:349
  361.3 86.2 %collective-permute-start.16 = (bf16[2,896,1024]{2,1,0:T(8,128)(2,1)}, bf16[2,896,1024]{2,1,0:T(8,128)(2,1)S(1)}, u32[]{:S(2)}, u32[]{:S(2)}) collective-permute-start(bf16[2,896,1024]{2,1,0:T(8,128)(2,1)} %collective-permute-done.12.refs_2_.refs_3_), channel_id=1, source_target_pairs={{1,2},{2,3},{5,6},{6,7},{9,10},{10,11},{13,14},{14,15},{17,18},{18... | collective-permute-start | bytes 11010056 | tf_op jit(solution)/shard_map/ppermute | solution.py:348
  362.8 84.7 %collective-permute-start.18 = (bf16[2,896,1024]{2,1,0:T(8,128)(2,1)}, bf16[2,896,1024]{2,1,0:T(8,128)(2,1)}, u32[]{:S(2)}, u32[]{:S(2)}) collective-permute-start(bf16[2,896,1024]{2,1,0:T(8,128)(2,1)} %pad_maximum_fusion.2.refs_0_.refs_1_.refs_3_.refs_6_.refs_4_), channel_id=1, source_target_pairs={{0,16},{4,20},{8,24},{12,28},{16,0},{20,4},{24,8},{28,12},{1,17},{... | collective-permute-start | bytes 11010056 | tf_op jit(solution)/shard_map/ppermute | solution.py:367
  382.5 69.0 %copy-start = (bf16[2,896,1024]{2,1,0:T(8,128)(2,1)}, bf16[2,896,1024]{2,1,0:T(8,128)(2,1)S(1)}, u32[]{:S(2)}) copy-start(bf16[2,896,1024]{2,1,0:T(8,128)(2,1)S(1)} %collective-permute-done.15.refs_4_) | copy-start | bytes 11010052
  447.4 10.9 %copy-start.2 = (bf16[2,896,1024]{2,1,0:T(8,128)(2,1)}, bf16[2,896,1024]{2,1,0:T(8,128)(2,1)S(1)}, u32[]{:S(2)}) copy-start(bf16[2,896,1024]{2,1,0:T(8,128)(2,1)S(1)} %collective-permute-done.16.refs_5_) | copy-start | bytes 11010052
  453.9 56.5 %collective-permute-start.23 = (bf16[2,896,1024]{2,1,0:T(8,128)(2,1)S(1)}, bf16[2,896,1024]{2,1,0:T(8,128)(2,1)}, u32[]{:S(2)}, u32[]{:S(2)}) collective-permute-start(bf16[2,896,1024]{2,1,0:T(8,128)(2,1)S(1)} %broadcast_select_fusion), channel_id=1, source_target_pairs={{0,4},{4,0},{8,12},{12,8},{16,20},{20,16},{24,28},{28,24},{1,5},{5... | collective-permute-start | bytes 11010056 | tf_op jit(solution)/shard_map/ppermute | solution.py:363
  454.8 50.0 %collective-permute-start.19 = (bf16[2,448,1024]{2,1,0:T(8,128)(2,1)}, bf16[2,448,1024]{2,1,0:T(8,128)(2,1)}, u32[]{:S(2)}, u32[]{:S(2)}) collective-permute-start(bf16[2,448,1024]{2,1,0:T(8,128)(2,1)} %get-tuple-element.74), channel_id=1, source_target_pairs={{2,3},{6,7},{10,11},{14,15},{18,19},{22,23},{26,27},{30,31}} | collective-permute-start | bytes 5505032 | tf_op jit(solution)/shard_map/ppermute | solution.py:348
  456.1 48.8 %collective-permute-start.20 = (bf16[2,448,1024]{2,1,0:T(8,128)(2,1)}, bf16[2,448,1024]{2,1,0:T(8,128)(2,1)}, u32[]{:S(2)}, u32[]{:S(2)}) collective-permute-start(bf16[2,448,1024]{2,1,0:T(8,128)(2,1)} %get-tuple-element.75), channel_id=1, source_target_pairs={{1,0},{5,4},{9,8},{13,12},{17,16},{21,20},{25,24},{29,28}} | collective-permute-start | bytes 5505032 | tf_op jit(solution)/shard_map/ppermute | solution.py:349
  460.6 47.6 %copy-start.1 = (bf16[2,896,1024]{2,1,0:T(8,128)(2,1)S(1)}, bf16[2,896,1024]{2,1,0:T(8,128)(2,1)}, u32[]{:S(2)}) copy-start(bf16[2,896,1024]{2,1,0:T(8,128)(2,1)} %copy-done) | copy-start | bytes 11010052
  504.8 44.9 %collective-permute-start.21 = (bf16[2,448,1024]{2,1,0:T(8,128)(2,1)}, bf16[2,448,1024]{2,1,0:T(8,128)(2,1)}, u32[]{:S(2)}, u32[]{:S(2)}) collective-permute-start(bf16[2,448,1024]{2,1,0:T(8,128)(2,1)} %get-tuple-element.76), channel_id=1, source_target_pairs={{1,0},{5,4},{9,8},{13,12},{17,16},{21,20},{25,24},{29,28}} | collective-permute-start | bytes 5505032 | tf_op jit(solution)/shard_map/ppermute | solution.py:349
  506.7 44.0 %collective-permute-start.22 = (bf16[2,448,1024]{2,1,0:T(8,128)(2,1)}, bf16[2,448,1024]{2,1,0:T(8,128)(2,1)}, u32[]{:S(2)}, u32[]{:S(2)}) collective-permute-start(bf16[2,448,1024]{2,1,0:T(8,128)(2,1)} %get-tuple-element.77), channel_id=1, source_target_pairs={{2,3},{6,7},{10,11},{14,15},{18,19},{22,23},{26,27},{30,31}} | collective-permute-start | bytes 5505032 | tf_op jit(solution)/shard_map/ppermute | solution.py:348
Sparse Core Ops, SparseCore 0:
  23.4 60.1 all-gather.1
